TPU v7x, 768 devices: a whole 4x8x12 slice. The times are simulated.
768 devices in a mesh: rows: 24 (over z, core), rep: 32 (over y, x).
Axes of the slice: x: 4, y: 8, z: 12, core: 2. Of those that a mesh axis runs over, the one named last changes fastest.
Arguments:
- out_grad: bfloat16 [98304, 256], P(('rows', 'rep')), may hold values from -6 to 6
- pre_relu: bfloat16 [98304, 256], P(('rows', 'rep')), may hold values from -6 to 6
- features: bfloat16 [98304, 256], P('rows'), may hold values from -0.059814453 to 0.059814453
- weight: bfloat16 [256, 256], replicated, may hold values from -0.375 to 0.375
- send_rows: int32 [768, 24, 32], P(('rows', 'rep')), may hold values from 0 to 127
- send_count: int32 [768, 24], P(('rows', 'rep')), may hold values from 1 to 32, as said below
- tile_index: int32 [768, 96], P(('rows', 'rep')), may hold values from 0 to 191, as said below
- tile_count: int32 [768], P(('rows', 'rep')), may hold values from 1 to 96, as said below
- tile_values: bfloat16 [768, 96, 128, 128], P(('rows', 'rep')), may hold values from -0.109375 to 0.109375
Outputs:
- feature_grad: bfloat16 [98304, 256], P(('rows', 'rep'))
- weight_grad: float32 [256, 256], replicated
Inputs may be any that keep to these rules, and one draw needn't show every extreme that they name: `send_count`: every device sends exactly 32 rows to at least one peer. `tile_index`: distinct on each device; a position k is row block k // 32 and column block k % 32. `tile_count`: some device has all 96 slots live.
All inputs are finite; a program needn't handle non-finite values.
Results may differ from a plain program's by a relative error of at most 0.0049.
Values may be sent and summed in bfloat16 or wider, within the bound.
No kernel may reach another device: no remote copies, remote signals or barrier semaphores. Data moves between devices by JAX's collectives and lax.ppermute only.
A program may use at most 64 MiB of HBM per device.

v0:
```python
import jax
import jax.numpy as jnp
from jax import lax
from jax.sharding import PartitionSpec as P


def per_device(
    out_grad, pre_relu, features, weight, send_rows, send_count, tile_index, tile_count, tile_values
):
    node_dev, width = out_grad.shape
    n_rows = lax.axis_size("rows")
    per_peer = send_rows.shape[2]
    tile_slots = tile_values.shape[1]
    tile_size = tile_values.shape[2]
    node_group = features.shape[0]
    col_blocks = node_group // tile_size
    total_rows = n_rows * per_peer
    row_blocks = (total_rows + tile_size - 1) // tile_size
    grad_pre = jnp.where(pre_relu > 0, out_grad, jnp.zeros_like(out_grad))
    slot_iota = jnp.arange(per_peer, dtype=jnp.int32)
    picked = grad_pre[send_rows[0]]
    live = (slot_iota[None, :] < send_count[0][:, None])[:, :, None]
    outgoing = jnp.where(live, picked, jnp.zeros_like(picked))
    received = lax.all_to_all(outgoing, "rows", split_axis=0, concat_axis=0, tiled=True)
    flat_rows = received.reshape(total_rows, width)
    flat_rows = jnp.concatenate(
        [flat_rows, jnp.zeros((row_blocks * tile_size - total_rows, width), jnp.bfloat16)], axis=0
    )
    kept = (jnp.arange(tile_slots, dtype=jnp.int32) < tile_count[0])[:, None, None]
    live_tiles = jnp.where(kept, tile_values[0], jnp.zeros_like(tile_values[0]))
    dense_tiles = jnp.zeros((row_blocks * col_blocks, tile_size, tile_size), jnp.bfloat16)
    dense_tiles = (
        dense_tiles.at[tile_index[0]]
        .set(live_tiles)
        .reshape(row_blocks, col_blocks, tile_size, tile_size)
    )
    partial_grad = jnp.einsum(
        "rckl,rkd->cld",
        dense_tiles,
        flat_rows.reshape(row_blocks, tile_size, width),
        preferred_element_type=jnp.float32,
    ).reshape(node_group, width)
    grads = lax.psum_scatter(partial_grad, "rep", scatter_dimension=0, tiled=True)
    own_rows = lax.dynamic_slice_in_dim(features, lax.axis_index("rep") * node_dev, node_dev, 0)
    local_weight = lax.dot_general(
        own_rows.astype(jnp.float32),
        grads,
        (((0,), (0,)), ((), ())),
        precision=lax.Precision.HIGHEST,
    )
    weight_grad = lax.psum(local_weight, ("rows", "rep"))
    feature_grad = lax.dot_general(
        grads.astype(jnp.bfloat16),
        weight,
        (((1,), (1,)), ((), ())),
        preferred_element_type=jnp.float32,
    ).astype(jnp.bfloat16)
    return (feature_grad, weight_grad)


def solution(mesh):
    return jax.shard_map(
        per_device,
        mesh=mesh,
        in_specs=(
            P(("rows", "rep"), None),
            P(("rows", "rep"), None),
            P("rows", None),
            P(),
            P(("rows", "rep"), None, None),
            P(("rows", "rep"), None),
            P(("rows", "rep"), None),
            P(("rows", "rep")),
            P(("rows", "rep"), None, None, None),
        ),
        out_specs=(P(("rows", "rep"), None), P()),
        check_vma=False,
    )
```

profile of v0, /device:TPU:1, one launch (start us, length us, event | category | flops | bytes accessed | tf_op | source)
XLA Modules:
  0.0 779.6 jit_solution(4032053583813280095)
XLA Ops:
  7.2 0.0 copy-start
  7.2 0.0 copy-start.2
  7.2 0.9 compare_select_fusion.1
  8.1 0.1 reshape.96
  8.1 0.7 iota_compare_fusion
  8.9 0.9 compare_select_fusion
  9.8 2.7 gather_fusion
  12.4 0.9 broadcast_select_fusion
  13.4 16.7 %all-to-all-start = ((bf16[24,32,256]{2,1,0:T(8,128)(2,1)}), bf16[24,32,256]{2,1,0:T(8,128)(2,1)S(1)}, u32[]{:S(2)}, u32[]{:S(2)}) async-start(bf16[24,32,256]{2,1,0:T(8,128)(2,1)} %broadcast_select_fusion), calls=%async_computation | async-start | bytes 786432 | tf_op jit(solution)/shard_map/all_to_all | solution.py:24
  30.1 0.0 reduce-scatter.2.cloned.1.call-start
  30.8 0.0 copy-done.2
  30.8 3.8 bitcast_select_fusion
  34.6 4.2 broadcast_in_dim.30
  38.8 14.6 %scatter_fusion = bf16[192,128,128]{2,1,0:T(8,128)(2,1)} fusion(bf16[192,128,128]{2,1,0:T(8,128)(2,1)} %broadcast_in_dim.30, s32[96]{0:T(128)S(1)} %fusion.3, bf16[96,128,128]{2,1,0:T(8,128)(2,1)} %bitcast_select_fusion), kind=kCustom, calls=%fused_computation.1 | custom fusion | bytes 9437568 | tf_op jit(solution)/shard_map/scatter | solution.py:34
  53.5 8.6 %copy.11 = bf16[32,128,128,6]{2,1,0,3:T(8,128)(2,1)} copy(bf16[32,128,128,6]{1,2,0,3:T(8,128)(2,1)} %bitcast.25) | data formatting | bytes 12582912 | tf_op jit(solution)/shard_map/rckl,rkd->cld/dot_general | solution.py:37
  62.1 0.0 all-to-all-done
  62.1 7.8 convolution_bitcast_fusion
  69.9 0.0 copy-start.1
  69.9 0.0 reduce-scatter.2.cloned.1.call-update
  69.9 0.0 all-reduce.2.cloned.1.call-start
  70.0 228.2 %reduce-scatter.2.cloned.1.call-done = f32[128,256]{1,0:T(8,128)} async-done(((f32[4096,256]{1,0:T(8,128)}), f32[128,256]{1,0:T(8,128)}) %reduce-scatter.2.cloned.1.call-update) | async-done | bytes 131088 | tf_op jit(solution)/shard_map/reduce_scatter | solution.py:43
  298.2 0.0 copy-done
  298.2 1.9 fusion
  300.1 0.0 all-reduce.2.cloned.1.call-update
  300.2 0.0 copy-done.1
  300.2 1.7 convolution_convert_fusion
  301.9 469.2 %all-reduce.2.cloned.1.call-done = f32[256,256]{1,0:T(8,128)} async-done(((f32[256,256]{1,0:T(8,128)}), f32[256,256]{1,0:T(8,128)}) %all-reduce.2.cloned.1.call-update) | async-done | bytes 262160 | tf_op jit(solution)/shard_map/psum | solution.py:51
  771.1 1.7 copy.15
  (3 shorter events, 0.0 us)
Async XLA Ops:
  7.2 291.0 %copy-start = (bf16[4096,256]{1,0:T(8,128)(2,1)S(1)}, bf16[4096,256]{1,0:T(8,128)(2,1)}, u32[]{:S(2)}) copy-start(bf16[4096,256]{1,0:T(8,128)(2,1)} %param.11) | copy-start | bytes 6291460
  7.2 23.6 %copy-start.2 = (s32[1,96]{1,0:T(1,128)S(1)}, s32[1,96]{1,0:T(1,128)}, u32[]{:S(2)}) copy-start(s32[1,96]{1,0:T(1,128)} %param.15) | copy-start | bytes 1156
  13.4 48.8 %all-to-all-start = ((bf16[24,32,256]{2,1,0:T(8,128)(2,1)}), bf16[24,32,256]{2,1,0:T(8,128)(2,1)S(1)}, u32[]{:S(2)}, u32[]{:S(2)}) async-start(bf16[24,32,256]{2,1,0:T(8,128)(2,1)} %broadcast_select_fusion), calls=%async_computation | async-start | bytes 786432 | tf_op jit(solution)/shard_map/all_to_all | solution.py:24
  30.1 268.2 %reduce-scatter.2.cloned.1.call-start = ((), (), s32[]{:S(2)}) async-start(), calls=%async_computation.2 | async-start | bytes 4325376 | tf_op jit(solution)/shard_map/reduce_scatter | solution.py:43
  69.9 230.2 %copy-start.1 = (bf16[256,256]{1,0:T(8,128)(2,1)S(1)}, bf16[256,256]{1,0:T(8,128)(2,1)}, u32[]{:S(2)}) copy-start(bf16[256,256]{1,0:T(8,128)(2,1)} %param.12) | copy-start | bytes 393220
  69.9 701.2 %all-reduce.2.cloned.1.call-start = ((), (), s32[]{:S(2)}) async-start(), calls=%async_computation.3 | async-start | bytes 524288 | tf_op jit(solution)/shard_map/psum | solution.py:51
Sparse Core Ops, SparseCore 0:
  70.1 228.0 reduce-scatter.1
  305.1 466.0 all-reduce.1
where the time goes:
time: 780 us
  waiting for transfers between devices  697 us (89%)
  local copies, waits for them, and re-layouts  31.9 us (4%)
  starting transfers between devices  16.8 us (2%)
  between operations  14.8 us (2%)
  matrix products  11.5 us (1%)
    psum x1, waiting for transfers between devices, per_device(): weight_grad = lax.psum(local_weight, ('rows', 'rep'))  469 us
    reduce_scatter x1, waiting for transfers between devices, per_device(): lax.psum_scatter(partial_grad, 'rep', scatter_dimension=0, tiled=True)  228 us
    all_to_all x1, starting transfers between devices, per_device(): lax.all_to_all(outgoing, 'rows', split_axis=0, concat_axis=0, tiled=True)  16.7 us
  transfers between devices with their start and end apart: 3, of which 2 were waited for; matrix products, arithmetic and copies ran while one was open for 4% of the time, Pallas kernels for 0%

commit v1 on v0

v1 whole, which is shorter than its diff:
```python
import jax
import jax.numpy as jnp
from jax import lax
from jax.experimental import pallas as pl
from jax.experimental.pallas import tpu as pltpu
from jax.sharding import PartitionSpec as P


def tile_products(index_ref, count_ref, tiles_ref, rows_ref, features_ref, out_ref, weight_ref, dense, rows_t):
    row_blocks = rows_ref.shape[0] // tiles_ref.shape[1]
    col_blocks = out_ref.shape[0]
    size = tiles_ref.shape[1]
    dense[...] = jnp.zeros_like(dense)

    def place(t, carry):
        k = index_ref[t]
        dense[lax.rem(k, col_blocks) * row_blocks + lax.div(k, col_blocks)] = tiles_ref[t]
        return carry

    lax.fori_loop(0, count_ref[0], place, 0)
    rows_t[...] = rows_ref[...].T
    weight_ref[...] = jnp.zeros_like(weight_ref)

    def columns(j, carry):
        left = dense[pl.ds(2 * j * row_blocks, row_blocks)].reshape(row_blocks * size, size)
        right = dense[pl.ds((2 * j + 1) * row_blocks, row_blocks)].reshape(row_blocks * size, size)
        pair = jnp.concatenate([left, right], axis=1)
        part = jnp.dot(rows_t[...], pair, preferred_element_type=jnp.float32).astype(jnp.bfloat16)
        out_ref[2 * j] = part[:, :size]
        out_ref[2 * j + 1] = part[:, size:]
        weight_ref[...] += jnp.dot(
            part,
            features_ref[pl.ds(pl.multiple_of(2 * j * size, 2 * size), 2 * size), :],
            preferred_element_type=jnp.float32,
        )
        return carry

    lax.fori_loop(0, col_blocks // 2, columns, 0)


def per_device(
    out_grad, pre_relu, features, weight, send_rows, send_count, tile_index, tile_count, tile_values
):
    node_dev, width = out_grad.shape
    n_rows = lax.axis_size("rows")
    n_rep = lax.axis_size("rep")
    per_peer = send_rows.shape[2]
    tile_size = tile_values.shape[2]
    node_group = features.shape[0]
    col_blocks = node_group // tile_size
    total_rows = n_rows * per_peer
    row_blocks = total_rows // tile_size

    grad_pre = jnp.where(pre_relu > 0, out_grad, jnp.zeros_like(out_grad))
    slot_iota = jnp.arange(per_peer, dtype=jnp.int32)
    wanted = jnp.where(slot_iota[None, :] < send_count[0][:, None], send_rows[0], -1)
    picks = (wanted[:, :, None] == jnp.arange(node_dev, dtype=jnp.int32)).astype(jnp.bfloat16)
    outgoing = lax.dot_general(
        picks, grad_pre, (((2,), (0,)), ((), ())), preferred_element_type=jnp.float32
    ).astype(jnp.bfloat16)
    received = lax.all_to_all(outgoing, "rows", split_axis=0, concat_axis=0, tiled=True)

    partial_t, weight_part = pl.pallas_call(
        tile_products,
        out_shape=(
            jax.ShapeDtypeStruct((col_blocks, width, tile_size), jnp.bfloat16),
            jax.ShapeDtypeStruct((width, width), jnp.float32),
        ),
        in_specs=[
            pl.BlockSpec(memory_space=pltpu.SMEM),
            pl.BlockSpec(memory_space=pltpu.SMEM),
            pl.BlockSpec(memory_space=pltpu.VMEM),
            pl.BlockSpec(memory_space=pltpu.VMEM),
            pl.BlockSpec(memory_space=pltpu.VMEM),
        ],
        out_specs=(pl.BlockSpec(memory_space=pltpu.VMEM), pl.BlockSpec(memory_space=pltpu.VMEM)),
        scratch_shapes=[
            pltpu.VMEM((row_blocks * col_blocks, tile_size, tile_size), jnp.bfloat16),
            pltpu.VMEM((width, total_rows), jnp.bfloat16),
        ],
        compiler_params=pltpu.CompilerParams(vmem_limit_bytes=32 * 1024 * 1024),
    )(tile_index[0], tile_count, tile_values[0], received.reshape(total_rows, width), features)

    weight_terms = lax.all_to_all(
        weight_part.reshape(n_rep, width // n_rep, width), "rep", split_axis=0, concat_axis=0, tiled=True
    )
    parts = lax.all_to_all(partial_t, "rep", split_axis=0, concat_axis=0, tiled=True)

    own = jnp.sum(weight_terms, axis=0)
    everyone = lax.all_to_all(
        jnp.broadcast_to(own[None], (n_rows,) + own.shape), "rows", split_axis=0, concat_axis=0, tiled=True
    )
    own = jnp.sum(everyone, axis=0)
    whole = lax.all_to_all(
        jnp.broadcast_to(own[None], (n_rep,) + own.shape), "rep", split_axis=0, concat_axis=0, tiled=True
    )
    weight_grad = whole.reshape(width, width).T

    grads_t = jnp.sum(parts.astype(jnp.float32), axis=0)
    feature_grad = lax.dot_general(
        grads_t.astype(jnp.bfloat16),
        weight,
        (((0,), (1,)), ((), ())),
        preferred_element_type=jnp.float32,
    ).astype(jnp.bfloat16)
    return (feature_grad, weight_grad)


def solution(mesh):
    return jax.shard_map(
        per_device,
        mesh=mesh,
        in_specs=(
            P(("rows", "rep"), None),
            P(("rows", "rep"), None),
            P("rows", None),
            P(),
            P(("rows", "rep"), None, None),
            P(("rows", "rep"), None),
            P(("rows", "rep"), None),
            P(("rows", "rep")),
            P(("rows", "rep"), None, None, None),
        ),
        out_specs=(P(("rows", "rep"), None), P()),
        check_vma=False,
    )
```

time: 780 us -> 166 us (0.21)
  the two profiles are of different devices: /device:TPU:1 before, /device:TPU:6 now
where the time goes in v1:
time: 166 us
  waiting for transfers between devices  68.8 us (41%)
  blocking collectives  55.7 us (34%)
  starting transfers between devices  21 us (13%)
  Pallas kernels  9.87 us (6%)
  local copies, waits for them, and re-layouts  5.02 us (3%)
  matrix products  2.76 us (2%)
    all_to_all x1, waiting for transfers between devices, per_device(): lax.all_to_all(partial_t, 'rep', split_axis=0, concat_axis=0, tiled=True)  48.7 us
    all_to_all x1, waiting for transfers between devices, per_device(): lax.all_to_all(outgoing, 'rows', split_axis=0, concat_axis=0, tiled=True)  20.1 us
    all_to_all x1, blocking collectives, per_device(): lax.all_to_all(weight_part.reshape(n_rep, width // n_rep, width), 'rep',...  20 us
    all_to_all x1, blocking collectives, per_device(): lax.all_to_all(jnp.broadcast_to(own[None], (n_rows,) + own.shape), 'rows'...  19.4 us
    all_to_all x1, blocking collectives, per_device(): lax.all_to_all(jnp.broadcast_to(own[None], (n_rep,) + own.shape), 'rep',...  16.3 us
    all_to_all x1, starting transfers between devices, per_device(): lax.all_to_all(outgoing, 'rows', split_axis=0, concat_axis=0, tiled=True)  15.4 us
    pallas_call x1, Pallas kernels, per_device(): pl.pallas_call(tile_products, out_shape=(jax.ShapeDtypeStruct((col_blocks...  9.87 us
    all_to_all x1, starting transfers between devices, per_device(): lax.all_to_all(partial_t, 'rep', split_axis=0, concat_axis=0, tiled=True)  5.6 us
  transfers between devices with their start and end apart: 2, of which 2 were waited for; matrix products, arithmetic and copies ran while one was open for 1% of the time, Pallas kernels for 0%

profile of v1, /device:TPU:6, one launch (start us, length us, event | category | flops | bytes accessed | tf_op | source)
XLA Modules:
  0.0 165.6 jit_solution(13782160021959282595)
XLA Ops:
  0.6 0.0 copy-start
  0.6 0.8 bitcast_select_fusion
  1.5 1.9 %convolution_convert_fusion = bf16[24,32,256]{2,1,0:T(8,128)(2,1)} fusion(s32[24,32]{1,0:T(8,128)S(1)} %bitcast_select_fusion, bf16[128,256]{1,0:T(8,128)(2,1)} %param.9, bf16[128,256]{1,0:T(8,128)(2,1)} %param.10), kind=kOutput, calls=%fused_computation | convolution fusion | flops 50692096 | bytes 527360 | tf_op jit(solution)/shard_map/dot_general | solution.py:58
  3.4 15.4 %all-to-all-start = ((bf16[24,32,256]{2,1,0:T(8,128)(2,1)}), bf16[24,32,256]{2,1,0:T(8,128)(2,1)S(1)}, u32[]{:S(2)}, u32[]{:S(2)}) async-start(bf16[24,32,256]{2,1,0:T(8,128)(2,1)} %convolution_convert_fusion), calls=%async_computation | async-start | bytes 786432 | tf_op jit(solution)/shard_map/all_to_all | solution.py:61
  19.4 20.1 %all-to-all-done = bf16[24,32,256]{2,1,0:T(8,128)(2,1)S(1)} async-done(((bf16[24,32,256]{2,1,0:T(8,128)(2,1)}), bf16[24,32,256]{2,1,0:T(8,128)(2,1)S(1)}, u32[]{:S(2)}, u32[]{:S(2)}) %all-to-all-start) | async-done | bytes 393248 | tf_op jit(solution)/shard_map/all_to_all | solution.py:61
  39.5 0.0 copy-start.1
  39.5 1.9 %copy-done.1 = bf16[1,96,128,128]{3,2,1,0:T(8,128)(2,1)S(1)} copy-done((bf16[1,96,128,128]{3,2,1,0:T(8,128)(2,1)S(1)}, bf16[1,96,128,128]{3,2,1,0:T(8,128)(2,1)}, u32[]{:S(2)}) %copy-start.1) | copy-done | bytes 3145752
  41.4 0.0 copy-start.2
  41.4 1.6 copy-done.2
  42.9 0.0 copy-start.3
  42.9 0.7 copy-done.3
  43.6 9.9 %shard_map.104 = (bf16[32,256,128]{2,1,0:T(8,128)(2,1)}, f32[256,256]{1,0:T(8,128)S(1)}) custom-call(s32[96]{0:T(128)S(1)} %bitcast.18, s32[1]{0:T(128)S(6)} %copy.13.count_ref, bf16[96,128,128]{2,1,0:T(8,128)(2,1)S(1)} %bitcast.15, bf16[768,256]{1,0:T(8,128)(2,1)S(1)} %bitcast.16, bf16[4096,256]{1,0:T(8,128)(2,1)S(1)} %copy-done.2), custom_call_target="tpu_custom_call" | custom-call | tf_op jit(solution)/shard_map/pallas_call | solution.py:63
  53.5 20.0 %all_to_all.25 = f32[32,8,256]{2,1,0:T(8,128)S(1)} all-to-all(f32[32,8,256]{2,1,0:T(8,128)S(1)} %bitcast.17), channel_id=1, replica_groups=mesh['rows'=24,'rep'=32] {'rep'}, dimensions={0} | all-to-all | bytes 524288 | tf_op jit(solution)/shard_map/all_to_all | solution.py:84
  73.5 19.4 %all_to_all.26 = f32[24,8,256]{2,1,0:T(8,128)S(1)} all-to-all(f32[24,8,256]{2,1,0:T(8,128)S(1)} %broadcast_in_dim.9), channel_id=1, replica_groups=mesh['rows'=24,'rep'=32] {'rows'}, dimensions={0} | all-to-all | bytes 393216 | tf_op jit(solution)/shard_map/all_to_all | solution.py:90
  93.0 16.3 %all_to_all.27 = f32[32,8,256]{2,1,0:T(8,128)S(1)} all-to-all(f32[32,8,256]{2,1,0:T(8,128)S(1)} %broadcast_in_dim.10), channel_id=1, replica_groups=mesh['rows'=24,'rep'=32] {'rep'}, dimensions={0} | all-to-all | bytes 524288 | tf_op jit(solution)/shard_map/all_to_all | solution.py:94
  109.3 5.6 %all-to-all-start.1 = ((bf16[32,256,128]{2,1,0:T(8,128)(2,1)}), bf16[32,256,128]{2,1,0:T(8,128)(2,1)S(1)}, u32[]{:S(2)}, u32[]{:S(2)}) async-start(bf16[32,256,128]{2,1,0:T(8,128)(2,1)} %get-tuple-element.4), calls=%async_computation.1 | async-start | bytes 4194304 | tf_op jit(solution)/shard_map/all_to_all | solution.py:87
  114.9 0.8 copy.12
  115.7 48.7 %all-to-all-done.1 = bf16[32,256,128]{2,1,0:T(8,128)(2,1)S(1)} async-done(((bf16[32,256,128]{2,1,0:T(8,128)(2,1)}), bf16[32,256,128]{2,1,0:T(8,128)(2,1)S(1)}, u32[]{:S(2)}, u32[]{:S(2)}) %all-to-all-start.1) | async-done | bytes 2097184 | tf_op jit(solution)/shard_map/all_to_all | solution.py:87
  164.4 0.3 reduce_sum.30
  164.7 0.0 copy-done
  164.7 0.8 convolution_convert_fusion.1
  (4 shorter events, 0.1 us)
Async XLA Ops:
  0.6 164.1 %copy-start = (bf16[256,256]{1,0:T(8,128)(2,1)S(1)}, bf16[256,256]{1,0:T(8,128)(2,1)}, u32[]{:S(2)}) copy-start(bf16[256,256]{1,0:T(8,128)(2,1)} %param.12) | copy-start | bytes 393220
  3.4 36.1 %all-to-all-start = ((bf16[24,32,256]{2,1,0:T(8,128)(2,1)}), bf16[24,32,256]{2,1,0:T(8,128)(2,1)S(1)}, u32[]{:S(2)}, u32[]{:S(2)}) async-start(bf16[24,32,256]{2,1,0:T(8,128)(2,1)} %convolution_convert_fusion), calls=%async_computation | async-start | bytes 786432 | tf_op jit(solution)/shard_map/all_to_all | solution.py:61
  39.5 1.9 %copy-start.1 = (bf16[1,96,128,128]{3,2,1,0:T(8,128)(2,1)S(1)}, bf16[1,96,128,128]{3,2,1,0:T(8,128)(2,1)}, u32[]{:S(2)}) copy-start(bf16[1,96,128,128]{3,2,1,0:T(8,128)(2,1)} %param.17) | copy-start | bytes 9437188
  41.4 1.6 copy-start.2
  42.9 0.7 copy-start.3
  109.3 55.2 %all-to-all-start.1 = ((bf16[32,256,128]{2,1,0:T(8,128)(2,1)}), bf16[32,256,128]{2,1,0:T(8,128)(2,1)S(1)}, u32[]{:S(2)}, u32[]{:S(2)}) async-start(bf16[32,256,128]{2,1,0:T(8,128)(2,1)} %get-tuple-element.4), calls=%async_computation.1 | async-start | bytes 4194304 | tf_op jit(solution)/shard_map/all_to_all | solution.py:87

commit v2 on v1

v2 whole, which is shorter than its diff:
```python
import functools

import jax
import jax.numpy as jnp
from jax import lax
from jax.experimental import pallas as pl
from jax.experimental.pallas import tpu as pltpu
from jax.sharding import PartitionSpec as P

STEPS = 8
VMEM_BYTES = 60000000
FINISH_VMEM_BYTES = 16000000
SMEM = pl.BlockSpec(memory_space=pltpu.SMEM)
VMEM = pl.BlockSpec(memory_space=pltpu.VMEM)


def place_tiles(row_blocks, index_ref, count_ref, tiles_ref, features_ref, dense_ref, mixed_ref, total):
    size = tiles_ref.shape[1]
    col_blocks = dense_ref.shape[0] // row_blocks
    dense_ref[...] = jnp.zeros_like(dense_ref)
    total[...] = jnp.zeros_like(total)

    def place(t, carry):
        k = index_ref[t]
        dense_ref[lax.rem(k, col_blocks) * row_blocks + lax.div(k, col_blocks)] = tiles_ref[t]
        return carry

    lax.fori_loop(0, count_ref[0], place, 0)

    def mix(j, carry):
        left = dense_ref[pl.ds(2 * j * row_blocks, row_blocks)].reshape(row_blocks * size, size)
        right = dense_ref[pl.ds((2 * j + 1) * row_blocks, row_blocks)].reshape(row_blocks * size, size)
        total[...] += jnp.dot(
            jnp.concatenate([left, right], axis=1),
            features_ref[pl.ds(pl.multiple_of(2 * j * size, 2 * size), 2 * size), :],
            preferred_element_type=jnp.float32,
        )
        return carry

    lax.fori_loop(0, col_blocks // 2, mix, 0)
    mixed_ref[...] = total[...].astype(mixed_ref.dtype)


def partial_products(low, row_blocks, rows_ref, dense_ref, out_ref, rows_t):
    depth = rows_t.shape[0]
    size = dense_ref.shape[1]

    @pl.when(pl.program_id(0) == 0)
    def _():
        rows_t[...] = rows_ref[:, low : low + depth].T

    for j in range(out_ref.shape[0] // 2):
        left = dense_ref[2 * j * row_blocks : (2 * j + 1) * row_blocks].reshape(row_blocks * size, size)
        right = dense_ref[(2 * j + 1) * row_blocks : (2 * j + 2) * row_blocks].reshape(row_blocks * size, size)
        part = jnp.dot(
            rows_t[...], jnp.concatenate([left, right], axis=1), preferred_element_type=jnp.float32
        ).astype(out_ref.dtype)
        out_ref[2 * j, :depth] = part[:, :size]
        out_ref[2 * j + 1, :depth] = part[:, size:]


def first_products(row_blocks, rows_ref, mixed_ref, dense_ref, out_ref, rows_t, weight_term):
    depth = rows_t.shape[0]
    size = dense_ref.shape[1]
    count = out_ref.shape[0]
    share = weight_term.shape[0] // (count * STEPS)

    @pl.when(pl.program_id(0) == 0)
    def _():
        weight_term[...] = lax.dot_general(
            mixed_ref[...], rows_ref[...], (((0,), (0,)), ((), ())), preferred_element_type=jnp.float32
        )

    partial_products(0, row_blocks, rows_ref, dense_ref, out_ref, rows_t)
    for j in range(count):
        first = pl.multiple_of((pl.program_id(0) * count + j) * share, share)
        own = weight_term[pl.ds(first, share), :]
        out_ref[j, depth:] = jnp.concatenate([own[:, :size], own[:, size:]], axis=0).astype(out_ref.dtype)


def finish(first_ref, second_ref, weight_ref, feature_grad_ref, weight_grad_ref):
    half, size = first_ref.shape
    share = (second_ref.shape[1] - half) // 2
    second = second_ref[0, :half].astype(jnp.float32)
    for p in range(1, second_ref.shape[0]):
        second += second_ref[p, :half].astype(jnp.float32)
    grads_t = jnp.concatenate([first_ref[...], second.astype(jnp.bfloat16)], axis=0)
    feature_grad_ref[...] = lax.dot_general(
        grads_t, weight_ref[...], (((0,), (1,)), ((), ())), preferred_element_type=jnp.float32
    ).astype(feature_grad_ref.dtype)
    for p in range(second_ref.shape[0]):
        own = second_ref[p, half:].astype(jnp.float32)
        weight_grad_ref[p * share : (p + 1) * share] = jnp.concatenate([own[:share], own[share:]], axis=1)


def per_device(
    out_grad, pre_relu, features, weight, send_rows, send_count, tile_index, tile_count, tile_values
):
    node_dev, width = out_grad.shape
    n_rows = lax.axis_size("rows")
    n_rep = lax.axis_size("rep")
    per_peer = send_rows.shape[2]
    size = tile_values.shape[2]
    col_blocks = features.shape[0] // size
    total_rows = n_rows * per_peer
    row_blocks = total_rows // size
    half = width // 2
    share = width // n_rep
    extra = share * width // size
    exchange = functools.partial(lax.all_to_all, split_axis=0, concat_axis=0, tiled=True)

    grad_pre = jnp.where(pre_relu > 0, out_grad, jnp.zeros_like(out_grad))
    slot_iota = jnp.arange(per_peer, dtype=jnp.int32)
    wanted = jnp.where(slot_iota[None, :] < send_count[0][:, None], send_rows[0], -1)
    picks = (wanted[:, :, None] == jnp.arange(node_dev, dtype=jnp.int32)).astype(jnp.bfloat16)
    outgoing = lax.dot_general(
        picks, grad_pre, (((2,), (0,)), ((), ())), preferred_element_type=jnp.float32
    ).astype(jnp.bfloat16)
    received = exchange(outgoing, "rows").reshape(total_rows, width)

    dense, mixed = pl.pallas_call(
        functools.partial(place_tiles, row_blocks),
        out_shape=(
            jax.ShapeDtypeStruct((col_blocks * row_blocks, size, size), jnp.bfloat16),
            jax.ShapeDtypeStruct((total_rows, width), jnp.bfloat16),
        ),
        in_specs=[SMEM, SMEM, VMEM, VMEM],
        out_specs=(VMEM, VMEM),
        scratch_shapes=[pltpu.VMEM((total_rows, width), jnp.float32)],
        compiler_params=pltpu.CompilerParams(vmem_limit_bytes=VMEM_BYTES),
        cost_estimate=pl.CostEstimate(flops=1600000000, bytes_accessed=24000000, transcendentals=0),
    )(tile_index[0], tile_count, tile_values[0], features)

    rows_spec = pl.BlockSpec((total_rows, width), lambda i: (0, 0))
    dense_spec = pl.BlockSpec((col_blocks // STEPS * row_blocks, size, size), lambda i: (i, 0, 0))
    out_spec = pl.BlockSpec((col_blocks // STEPS, half + extra, size), lambda i: (i, 0, 0))
    out_shape = jax.ShapeDtypeStruct((col_blocks, half + extra, size), jnp.bfloat16)
    rows_t = pltpu.VMEM((half, total_rows), jnp.bfloat16)
    params = pltpu.CompilerParams(vmem_limit_bytes=VMEM_BYTES)
    first = pl.pallas_call(
        functools.partial(first_products, row_blocks),
        grid=(STEPS,),
        out_shape=out_shape,
        in_specs=[rows_spec, rows_spec, dense_spec],
        out_specs=out_spec,
        scratch_shapes=[rows_t, pltpu.VMEM((width, width), jnp.float32)],
        compiler_params=params,
        cost_estimate=pl.CostEstimate(flops=900000000, bytes_accessed=8000000, transcendentals=0),
    )(received, mixed, dense)
    first = exchange(first, "rep")

    second = pl.pallas_call(
        functools.partial(partial_products, half, row_blocks),
        grid=(STEPS,),
        out_shape=out_shape,
        in_specs=[rows_spec, dense_spec],
        out_specs=out_spec,
        scratch_shapes=[rows_t],
        compiler_params=params,
        cost_estimate=pl.CostEstimate(flops=800000000, bytes_accessed=8000000, transcendentals=0),
    )(received, dense)

    own = jnp.sum(first[:, half:].astype(jnp.float32), axis=0)
    own = jnp.sum(exchange(jnp.broadcast_to(own[None], (n_rows, extra, size)), "rows"), axis=0)
    own = jnp.broadcast_to(own.astype(jnp.bfloat16)[None], (n_rep, extra, size))
    second = exchange(second.at[:, half:].set(own), "rep")
    first = jnp.sum(first[:, :half].astype(jnp.float32), axis=0).astype(jnp.bfloat16)
    return pl.pallas_call(
        finish,
        out_shape=(
            jax.ShapeDtypeStruct((node_dev, width), jnp.bfloat16),
            jax.ShapeDtypeStruct((width, width), jnp.float32),
        ),
        in_specs=[VMEM, VMEM, VMEM],
        out_specs=(VMEM, VMEM),
        compiler_params=pltpu.CompilerParams(vmem_limit_bytes=FINISH_VMEM_BYTES),
    )(first, second, weight)


def solution(mesh):
    return jax.shard_map(
        per_device,
        mesh=mesh,
        in_specs=(
            P(("rows", "rep"), None),
            P(("rows", "rep"), None),
            P("rows", None),
            P(),
            P(("rows", "rep"), None, None),
            P(("rows", "rep"), None),
            P(("rows", "rep"), None),
            P(("rows", "rep")),
            P(("rows", "rep"), None, None, None),
        ),
        out_specs=(P(("rows", "rep"), None), P()),
        check_vma=False,
    )
```

time: 166 us -> 148 us (0.89)
  the two profiles are of different devices: /device:TPU:6 before, /device:TPU:1 now
where the time goes in v2:
time: 148 us; the launch traced here: 145 us
  waiting for transfers between devices  41.6 us (28%)
  blocking collectives  38.4 us (26%)
  starting transfers between devices  31.4 us (21%)
  Pallas kernels  26.9 us (18%)
  local copies, waits for them, and re-layouts  2.11 us (1%)
  matrix products  1.95 us (1%)
    all_to_all x1, blocking collectives, per_device(): first = exchange(first, 'rep')  38.4 us
    all_to_all x1, waiting for transfers between devices, per_device(): second = exchange(second.at[:, half:].set(own), 'rep')  28.4 us
    all_to_all x1, starting transfers between devices, per_device(): received = exchange(outgoing, 'rows').reshape(total_rows, width)  16.7 us
    all_to_all x1, starting transfers between devices, per_device(): exchange(jnp.broadcast_to(own[None], (n_rows, extra, size)), 'rows')  10.6 us
    pallas_call x1, Pallas kernels, per_device(): pl.pallas_call(functools.partial(place_tiles, row_blocks), out_shape=(jax...  10.6 us
    pallas_call x1, Pallas kernels, per_device(): pl.pallas_call(functools.partial(first_products, row_blocks), grid=(STEPS...  7.8 us
    pallas_call x1, Pallas kernels, per_device(): pl.pallas_call(functools.partial(partial_products, half, row_blocks), gri...  7.48 us
    all_to_all x1, waiting for transfers between devices, per_device(): received = exchange(outgoing, 'rows').reshape(total_rows, width)  6.96 us
  transfers between devices with their start and end apart: 3, of which 3 were waited for; matrix products, arithmetic and copies ran while one was open for 0% of the time, Pallas kernels for 13%

profile of v2, /device:TPU:1, one launch (start us, length us, event | category | flops | bytes accessed | tf_op | source)
XLA Modules:
  0.0 144.6 jit_solution(11650126964464209189)
XLA Ops:
  0.6 0.8 bitcast_select_fusion
  1.4 2.0 %convolution_convert_fusion = bf16[24,32,256]{2,1,0:T(8,128)(2,1)} fusion(s32[24,32]{1,0:T(8,128)S(1)} %bitcast_select_fusion, bf16[128,256]{1,0:T(8,128)(2,1)} %param.11, bf16[128,256]{1,0:T(8,128)(2,1)} %param.12), kind=kOutput, calls=%fused_computation | convolution fusion | flops 50692096 | bytes 527360 | tf_op jit(solution)/shard_map/dot_general | solution.py:116
  3.4 16.7 %all-to-all-start = ((bf16[24,32,256]{2,1,0:T(8,128)(2,1)}), bf16[24,32,256]{2,1,0:T(8,128)(2,1)S(1)}, u32[]{:S(2)}, u32[]{:S(2)}) async-start(bf16[24,32,256]{2,1,0:T(8,128)(2,1)} %convolution_convert_fusion), calls=%async_computation | async-start | bytes 786432 | tf_op jit(solution)/shard_map/all_to_all | solution.py:119
  20.7 10.6 %shard_map.104 = (bf16[192,128,128]{2,1,0:T(8,128)(2,1)}, bf16[768,256]{1,0:T(8,128)(2,1)}) custom-call(s32[96]{0:T(128)} %bitcast.13, s32[1]{0:T(128)S(6)} %copy.12.count_ref, bf16[96,128,128]{2,1,0:T(8,128)(2,1)} %bitcast.12, bf16[4096,256]{1,0:T(8,128)(2,1)} %features_ref.1), custom_call_target="tpu_custom_call" | custom-call | flops 1600000000 | bytes 24000000 | tf_op jit(solution)/shard_map/pallas_call | solution.py:121
  31.3 7.0 %all-to-all-done = bf16[24,32,256]{2,1,0:T(8,128)(2,1)S(1)} async-done(((bf16[24,32,256]{2,1,0:T(8,128)(2,1)}), bf16[24,32,256]{2,1,0:T(8,128)(2,1)S(1)}, u32[]{:S(2)}, u32[]{:S(2)}) %all-to-all-start) | async-done | bytes 393248 | tf_op jit(solution)/shard_map/all_to_all | solution.py:119
  38.3 0.0 copy-start.1
  38.3 0.7 copy-done.1
  39.0 7.8 %shard_map.105 = bf16[32,144,128]{2,1,0:T(8,128)(2,1)} custom-call(bf16[768,256]{1,0:T(8,128)(2,1)} %bitcast.9, bf16[768,256]{1,0:T(8,128)(2,1)} %get-tuple-element.16.mixed_ref, bf16[192,128,128]{2,1,0:T(8,128)(2,1)} %get-tuple-element.17.dense_ref), custom_call_target="tpu_custom_call" | custom-call | flops 900000000 | bytes 8000000 | tf_op jit(solution)/shard_map/pallas_call | solution.py:140
  46.8 38.4 %all_to_all.20 = bf16[32,144,128]{2,1,0:T(8,128)(2,1)S(1)} all-to-all(bf16[32,144,128]{2,1,0:T(8,128)(2,1)} %shard_map.105), channel_id=1, replica_groups=mesh['rows'=24,'rep'=32] {'rep'}, dimensions={0} | all-to-all | bytes 2359296 | tf_op jit(solution)/shard_map/all_to_all | solution.py:150
  85.3 0.7 broadcast_in_dim.7
  85.9 10.6 %all-to-all-start.2 = ((f32[24,16,128]{2,1,0:T(8,128)}), f32[24,16,128]{2,1,0:T(8,128)S(1)}, u32[]{:S(2)}, u32[]{:S(2)}) async-start(f32[24,16,128]{2,1,0:T(8,128)} %broadcast_in_dim.7), calls=%async_computation.2 | async-start | bytes 393216 | tf_op jit(solution)/shard_map/all_to_all | solution.py:164
  96.6 7.5 %shard_map.106 = bf16[32,144,128]{2,1,0:T(8,128)(2,1)} custom-call(bf16[768,256]{1,0:T(8,128)(2,1)} %bitcast.10, bf16[192,128,128]{2,1,0:T(8,128)(2,1)} %get-tuple-element.17.dense_ref), custom_call_target="tpu_custom_call" | custom-call | flops 800000000 | bytes 8000000 | tf_op jit(solution)/shard_map/pallas_call | solution.py:152
  104.1 6.2 %all-to-all-done.2 = f32[24,16,128]{2,1,0:T(8,128)S(1)} async-done(((f32[24,16,128]{2,1,0:T(8,128)}), f32[24,16,128]{2,1,0:T(8,128)S(1)}, u32[]{:S(2)}, u32[]{:S(2)}) %all-to-all-start.2) | async-done | bytes 196640 | tf_op jit(solution)/shard_map/all_to_all | solution.py:164
  110.3 0.7 broadcast_dynamic-update-slice_fusion
  111.0 0.0 copy-start
  111.0 4.1 %all-to-all-start.3 = ((bf16[32,144,128]{2,1,0:T(8,128)(2,1)}), bf16[32,144,128]{2,1,0:T(8,128)(2,1)S(1)}, u32[]{:S(2)}, u32[]{:S(2)}) async-start(bf16[32,144,128]{2,1,0:T(8,128)(2,1)} %broadcast_dynamic-update-slice_fusion), calls=%async_computation.3 | async-start | bytes 2359296 | tf_op jit(solution)/shard_map/all_to_all | solution.py:166
  115.1 0.2 slice_reduce_fusion.first_ref
  115.2 28.4 %all-to-all-done.3.second_ref = bf16[32,144,128]{2,1,0:T(8,128)(2,1)S(1)} async-done(((bf16[32,144,128]{2,1,0:T(8,128)(2,1)}), bf16[32,144,128]{2,1,0:T(8,128)(2,1)S(1)}, u32[]{:S(2)}, u32[]{:S(2)}) %all-to-all-start.3) | async-done | bytes 1179680 | tf_op jit(solution)/shard_map/all_to_all | solution.py:166
  143.6 0.0 copy-done
  143.6 1.0 shard_map.107
  (2 shorter events, 0.1 us)
Async XLA Ops:
  3.4 34.9 %all-to-all-start = ((bf16[24,32,256]{2,1,0:T(8,128)(2,1)}), bf16[24,32,256]{2,1,0:T(8,128)(2,1)S(1)}, u32[]{:S(2)}, u32[]{:S(2)}) async-start(bf16[24,32,256]{2,1,0:T(8,128)(2,1)} %convolution_convert_fusion), calls=%async_computation | async-start | bytes 786432 | tf_op jit(solution)/shard_map/all_to_all | solution.py:119
  38.3 0.7 copy-start.1
  85.9 24.4 %all-to-all-start.2 = ((f32[24,16,128]{2,1,0:T(8,128)}), f32[24,16,128]{2,1,0:T(8,128)S(1)}, u32[]{:S(2)}, u32[]{:S(2)}) async-start(f32[24,16,128]{2,1,0:T(8,128)} %broadcast_in_dim.7), calls=%async_computation.2 | async-start | bytes 393216 | tf_op jit(solution)/shard_map/all_to_all | solution.py:164
  111.0 32.6 %copy-start = (bf16[256,256]{1,0:T(8,128)(2,1)S(1)}, bf16[256,256]{1,0:T(8,128)(2,1)}, u32[]{:S(2)}) copy-start(bf16[256,256]{1,0:T(8,128)(2,1)} %weight_ref.1) | copy-start | bytes 393220
  111.0 32.6 %all-to-all-start.3 = ((bf16[32,144,128]{2,1,0:T(8,128)(2,1)}), bf16[32,144,128]{2,1,0:T(8,128)(2,1)S(1)}, u32[]{:S(2)}, u32[]{:S(2)}) async-start(bf16[32,144,128]{2,1,0:T(8,128)(2,1)} %broadcast_dynamic-update-slice_fusion), calls=%async_computation.3 | async-start | bytes 2359296 | tf_op jit(solution)/shard_map/all_to_all | solution.py:166

commit v3 on v2

v3 whole, which is shorter than its diff:
```python
import functools

import jax
import jax.numpy as jnp
from jax import lax
from jax.experimental import pallas as pl
from jax.experimental.pallas import tpu as pltpu
from jax.sharding import PartitionSpec as P

STEPS = 8
VMEM_BYTES = 60000000
FINISH_VMEM_BYTES = 16000000
SMEM = pl.BlockSpec(memory_space=pltpu.SMEM)
VMEM = pl.BlockSpec(memory_space=pltpu.VMEM)


def place_tiles(index_ref, count_ref, tiles_ref, features_ref, turned_ref, mixed_ref, dense, total):
    col_blocks, row_blocks, size, _ = dense.shape
    dense[...] = jnp.zeros_like(dense)
    turned_ref[...] = jnp.zeros_like(turned_ref)
    total[...] = jnp.zeros_like(total)
    count = count_ref[0]

    def place(t, carry):
        k = index_ref[t]
        c, r = lax.rem(k, col_blocks), lax.div(k, col_blocks)
        tile = jnp.where(t < count, tiles_ref[t], jnp.zeros_like(tiles_ref[t]))
        dense[c, r] = tile
        first = pl.multiple_of(c * size, size)
        turned_ref[pl.ds(first, size), pl.ds(pl.multiple_of(r * size, size), size)] = tile.T
        return carry

    lax.fori_loop(0, tiles_ref.shape[0], place, 0, unroll=4)

    def mix(j, carry):
        left = dense[2 * j].reshape(row_blocks * size, size)
        right = dense[2 * j + 1].reshape(row_blocks * size, size)
        total[...] += jnp.dot(
            jnp.concatenate([left, right], axis=1),
            features_ref[pl.ds(pl.multiple_of(2 * j * size, 2 * size), 2 * size), :],
            preferred_element_type=jnp.float32,
        )
        return carry

    lax.fori_loop(0, col_blocks // 2, mix, 0)
    mixed_ref[...] = total[...].astype(mixed_ref.dtype).T


def lanes_to_rows(block, size):
    return jnp.concatenate([block[:, i : i + size] for i in range(0, block.shape[1], size)], axis=0)


def rows_to_lanes(block, count):
    rows = block.shape[0] // count
    return jnp.concatenate([block[i * rows : (i + 1) * rows] for i in range(count)], axis=1)


def products(bounds, rows_ref, mixed_ref, turned_ref, *refs):
    *outs, weight_term = refs
    count = outs[0].shape[0]
    size = outs[0].shape[2]
    share = weight_term.shape[0] // (count * STEPS)

    @pl.when(pl.program_id(0) == 0)
    def _():
        weight_term[...] = jnp.dot(mixed_ref[...], rows_ref[...], preferred_element_type=jnp.float32)

    part = jnp.dot(turned_ref[...], rows_ref[...], preferred_element_type=jnp.float32).astype(outs[0].dtype)
    for j in range(count):
        for out, (low, high) in zip(outs, bounds):
            block = lanes_to_rows(part[j * size + low : j * size + high], size)
            out[j, : block.shape[0]] = block
        first = pl.multiple_of((pl.program_id(0) * count + j) * share, share)
        own = lanes_to_rows(weight_term[pl.ds(first, share), :], size)
        outs[0][j, outs[0].shape[1] - own.shape[0] :] = own.astype(outs[0].dtype)


def finish(lanes, sums_ref, middle_ref, last_ref, weight_ref, feature_grad_ref, weight_grad_ref):
    share = weight_grad_ref.shape[0] // last_ref.shape[0]
    rows = last_ref.shape[1] - share * lanes
    last = last_ref[0, :rows].astype(jnp.float32)
    for p in range(1, last_ref.shape[0]):
        last += last_ref[p, :rows].astype(jnp.float32)
    grads = jnp.concatenate(
        [rows_to_lanes(block, lanes) for block in (sums_ref[...], middle_ref[...], last.astype(jnp.bfloat16))], axis=0
    )
    feature_grad_ref[...] = lax.dot_general(
        grads, weight_ref[...], (((1,), (1,)), ((), ())), preferred_element_type=jnp.float32
    ).astype(feature_grad_ref.dtype)
    for p in range(last_ref.shape[0]):
        own = last_ref[p, rows:].astype(jnp.float32)
        weight_grad_ref[p * share : (p + 1) * share] = rows_to_lanes(own, lanes)


def sum_over_rows(term):
    n = lax.axis_size("rows")

    def shifted(value, to):
        return lax.ppermute(value, "rows", [(i, to(i)) for i in range(n)])

    term = term + shifted(term, lambda i: i ^ 1)
    term = term + shifted(term, lambda i: i ^ 2)
    third = n // 3
    up, down = shifted(term, lambda i: (i + third) % n), shifted(term, lambda i: (i - third) % n)
    place = lax.axis_index("rows") // third
    a = jnp.where(place == 0, term, jnp.where(place == 1, up, down))
    b = jnp.where(place == 1, term, jnp.where(place == 2, up, down))
    c = jnp.where(place == 2, term, jnp.where(place == 0, up, down))
    term = (a + b) + c
    return term + shifted(term, lambda i: (i + n // 2) % n)


def per_device(
    out_grad, pre_relu, features, weight, send_rows, send_count, tile_index, tile_count, tile_values
):
    node_dev, width = out_grad.shape
    n_rows = lax.axis_size("rows")
    n_rep = lax.axis_size("rep")
    per_peer = send_rows.shape[2]
    size = tile_values.shape[2]
    col_blocks = features.shape[0] // size
    total_rows = n_rows * per_peer
    row_blocks = total_rows // size
    lanes = width // size
    share = width // n_rep
    extra = share * lanes
    cuts = (0, size // 4, 3 * size // 4, size)
    bounds = tuple(zip(cuts[:-1], cuts[1:]))
    exchange = functools.partial(lax.all_to_all, split_axis=0, concat_axis=0, tiled=True)

    grad_pre = jnp.where(pre_relu > 0, out_grad, jnp.zeros_like(out_grad))
    slot_iota = jnp.arange(per_peer, dtype=jnp.int32)
    wanted = jnp.where(slot_iota[None, :] < send_count[0][:, None], send_rows[0], -1)
    picks = (wanted[:, :, None] == jnp.arange(node_dev, dtype=jnp.int32)).astype(jnp.bfloat16)
    outgoing = lax.dot_general(
        picks, grad_pre, (((2,), (0,)), ((), ())), preferred_element_type=jnp.float32
    ).astype(jnp.bfloat16)
    received = exchange(outgoing, "rows").reshape(total_rows, width)

    turned, mixed = pl.pallas_call(
        place_tiles,
        out_shape=(
            jax.ShapeDtypeStruct((col_blocks * size, total_rows), jnp.bfloat16),
            jax.ShapeDtypeStruct((width, total_rows), jnp.bfloat16),
        ),
        in_specs=[SMEM, SMEM, VMEM, VMEM],
        out_specs=(VMEM, VMEM),
        scratch_shapes=[
            pltpu.VMEM((col_blocks, row_blocks, size, size), jnp.bfloat16),
            pltpu.VMEM((total_rows, width), jnp.float32),
        ],
        compiler_params=pltpu.CompilerParams(vmem_limit_bytes=VMEM_BYTES),
        cost_estimate=pl.CostEstimate(flops=1600000000, bytes_accessed=24000000, transcendentals=0),
    )(tile_index[0], tile_count, tile_values[0], features)

    depths = [(high - low) * lanes + more for (low, high), more in zip(bounds, (extra, 0, extra))]
    first, middle, last = pl.pallas_call(
        functools.partial(products, bounds),
        grid=(STEPS,),
        out_shape=tuple(jax.ShapeDtypeStruct((col_blocks, depth, size), jnp.bfloat16) for depth in depths),
        in_specs=[
            pl.BlockSpec((total_rows, width), lambda i: (0, 0)),
            pl.BlockSpec((width, total_rows), lambda i: (0, 0)),
            pl.BlockSpec((col_blocks * size // STEPS, total_rows), lambda i: (i, 0)),
        ],
        out_specs=tuple(pl.BlockSpec((col_blocks // STEPS, depth, size), lambda i: (i, 0, 0)) for depth in depths),
        scratch_shapes=[pltpu.VMEM((width, width), jnp.float32)],
        compiler_params=pltpu.CompilerParams(vmem_limit_bytes=VMEM_BYTES),
        cost_estimate=pl.CostEstimate(flops=1700000000, bytes_accessed=9000000, transcendentals=0),
    )(received, mixed, turned)

    first = exchange(first, "rep")
    middle = exchange(middle, "rep")
    own = sum_over_rows(jnp.sum(first[:, depths[0] - extra :].astype(jnp.float32), axis=0))
    own = jnp.broadcast_to(own.astype(jnp.bfloat16)[None], (n_rep, extra, size))
    last = exchange(last.at[:, depths[2] - extra :].set(own), "rep")
    sums = [
        jnp.sum(part.astype(jnp.float32), axis=0).astype(jnp.bfloat16)
        for part in (first[:, : depths[0] - extra], middle)
    ]
    return pl.pallas_call(
        functools.partial(finish, lanes),
        out_shape=(
            jax.ShapeDtypeStruct((node_dev, width), jnp.bfloat16),
            jax.ShapeDtypeStruct((width, width), jnp.float32),
        ),
        in_specs=[VMEM, VMEM, VMEM, VMEM],
        out_specs=(VMEM, VMEM),
        compiler_params=pltpu.CompilerParams(vmem_limit_bytes=FINISH_VMEM_BYTES),
    )(sums[0], sums[1], last, weight)


def solution(mesh):
    return jax.shard_map(
        per_device,
        mesh=mesh,
        in_specs=(
            P(("rows", "rep"), None),
            P(("rows", "rep"), None),
            P("rows", None),
            P(),
            P(("rows", "rep"), None, None),
            P(("rows", "rep"), None),
            P(("rows", "rep"), None),
            P(("rows", "rep")),
            P(("rows", "rep"), None, None, None),
        ),
        out_specs=(P(("rows", "rep"), None), P()),
        check_vma=False,
    )
```

time: 148 us -> 147 us (level)
  the two profiles are of different devices: /device:TPU:1 before, /device:TPU:8 now
where the time goes in v3:
time: 147 us; the launch traced here: 146 us
  starting transfers between devices  51.2 us (35%)
  waiting for transfers between devices  38.3 us (26%)
  blocking collectives  28.1 us (19%)
  Pallas kernels  22.2 us (15%)
  matrix products  1.94 us (1%)
    all_to_all x1, blocking collectives, per_device(): first = exchange(first, 'rep')  28.1 us
    ppermute x5, starting transfers between devices, shifted(): return lax.ppermute(value, 'rows', [(i, to(i)) for i in range(n)])  20.6 us
    all_to_all x1, waiting for transfers between devices, per_device(): last = exchange(last.at[:, depths[2] - extra:].set(own), 'rep')  16.6 us
    all_to_all x1, starting transfers between devices, per_device(): received = exchange(outgoing, 'rows').reshape(total_rows, width)  15.4 us
    ppermute x5, waiting for transfers between devices, shifted(): return lax.ppermute(value, 'rows', [(i, to(i)) for i in range(n)])  14.7 us
    pallas_call x1, Pallas kernels, per_device(): pl.pallas_call(place_tiles, out_shape=(jax.ShapeDtypeStruct((col_blocks *...  13.1 us
    all_to_all x1, starting transfers between devices, per_device(): last = exchange(last.at[:, depths[2] - extra:].set(own), 'rep')  9.78 us
    pallas_call x1, Pallas kernels, per_device(): pl.pallas_call(functools.partial(products, bounds), grid=(STEPS,), out_sh...  8.3 us
  transfers between devices with their start and end apart: 8, of which 6 were waited for; matrix products, arithmetic and copies ran while one was open for 1% of the time, Pallas kernels for 9%

profile of v3, /device:TPU:8, one launch (start us, length us, event | category | flops | bytes accessed | tf_op | source)
XLA Modules:
  0.0 145.7 jit_solution(10273793034128581414)
XLA Ops:
  0.6 0.8 bitcast_select_fusion
  1.4 1.9 %convolution_convert_fusion = bf16[24,32,256]{2,1,0:T(8,128)(2,1)} fusion(s32[24,32]{1,0:T(8,128)S(1)} %bitcast_select_fusion, bf16[128,256]{1,0:T(8,128)(2,1)} %param.11, bf16[128,256]{1,0:T(8,128)(2,1)} %param.12), kind=kOutput, calls=%fused_computation | convolution fusion | flops 50692096 | bytes 527360 | tf_op jit(solution)/shard_map/dot_general | solution.py:135
  3.4 15.4 %all-to-all-start = ((bf16[24,32,256]{2,1,0:T(8,128)(2,1)}), bf16[24,32,256]{2,1,0:T(8,128)(2,1)S(1)}, u32[]{:S(2)}, u32[]{:S(2)}) async-start(bf16[24,32,256]{2,1,0:T(8,128)(2,1)} %convolution_convert_fusion), calls=%async_computation | async-start | bytes 786432 | tf_op jit(solution)/shard_map/all_to_all | solution.py:138
  19.4 13.1 %shard_map.104 = (bf16[4096,768]{1,0:T(8,128)(2,1)}, bf16[256,768]{1,0:T(8,128)(2,1)}) custom-call(s32[96]{0:T(128)} %bitcast.12, s32[1]{0:T(128)S(6)} %copy.12.count_ref, bf16[96,128,128]{2,1,0:T(8,128)(2,1)} %bitcast.11, bf16[4096,256]{1,0:T(8,128)(2,1)} %features_ref.1), custom_call_target="tpu_custom_call" | custom-call | flops 1600000000 | bytes 24000000 | tf_op jit(solution)/shard_map/pallas_call | solution.py:140
  32.4 7.0 %all-to-all-done = bf16[24,32,256]{2,1,0:T(8,128)(2,1)S(1)} async-done(((bf16[24,32,256]{2,1,0:T(8,128)(2,1)}), bf16[24,32,256]{2,1,0:T(8,128)(2,1)S(1)}, u32[]{:S(2)}, u32[]{:S(2)}) %all-to-all-start) | async-done | bytes 393248 | tf_op jit(solution)/shard_map/all_to_all | solution.py:138
  39.4 0.0 copy-start.1
  39.4 0.8 copy-done.1
  40.2 8.3 %shard_map.105 = (bf16[32,80,128]{2,1,0:T(8,128)(2,1)}, bf16[32,128,128]{2,1,0:T(8,128)(2,1)}, bf16[32,80,128]{2,1,0:T(8,128)(2,1)}) custom-call(bf16[768,256]{1,0:T(8,128)(2,1)} %bitcast.9, bf16[256,768]{1,0:T(8,128)(2,1)} %get-tuple-element.19.mixed_ref, bf16[4096,768]{1,0:T(8,128)(2,1)} %get-tuple-element.20.turned_ref), custom_call_target="tpu_custom_call" | custom-call | flops 1700000000 | bytes 9000000 | tf_op jit(solution)/shard_map/pallas_call | solution.py:157
  48.5 0.0 copy-start
  48.5 28.1 %all_to_all.20 = bf16[32,80,128]{2,1,0:T(8,128)(2,1)S(1)} all-to-all(bf16[32,80,128]{2,1,0:T(8,128)(2,1)} %get-tuple-element.21), channel_id=1, replica_groups=mesh['rows'=24,'rep'=32] {'rep'}, dimensions={0} | all-to-all | bytes 1310720 | tf_op jit(solution)/shard_map/all_to_all | solution.py:172
  76.7 5.4 %all-to-all-start.2 = ((bf16[32,128,128]{2,1,0:T(8,128)(2,1)}), bf16[32,128,128]{2,1,0:T(8,128)(2,1)S(1)}, u32[]{:S(2)}, u32[]{:S(2)}) async-start(bf16[32,128,128]{2,1,0:T(8,128)(2,1)} %get-tuple-element.22), calls=%async_computation.2 | async-start | bytes 2097152 | tf_op jit(solution)/shard_map/all_to_all | solution.py:173
  82.1 1.9 %collective-permute-start = (f32[16,128]{1,0:T(8,128)S(1)}, f32[16,128]{1,0:T(8,128)S(1)}, u32[]{:S(2)}, u32[]{:S(2)}) collective-permute-start(f32[16,128]{1,0:T(8,128)S(1)} %convert_reduce_fusion), channel_id=1, source_target_pairs={{0,32},{32,0},{64,96},{96,64},{128,160},{160,128},{192,224},{224,1... | collective-permute-start | bytes 24584 | tf_op jit(solution)/shard_map/ppermute | solution.py:99
  84.0 1.1 collective-permute-done
  85.2 3.3 %collective-permute-start.1 = (f32[16,128]{1,0:T(8,128)S(1)}, f32[16,128]{1,0:T(8,128)S(1)}, u32[]{:S(2)}, u32[]{:S(2)}) collective-permute-start(f32[16,128]{1,0:T(8,128)S(1)} %add.18), channel_id=1, source_target_pairs={{0,64},{32,96},{64,0},{96,32},{128,192},{160,224},{192,128},{224,1... | collective-permute-start | bytes 24584 | tf_op jit(solution)/shard_map/ppermute | solution.py:99
  88.5 2.2 %collective-permute-done.1 = f32[16,128]{1,0:T(8,128)S(1)} collective-permute-done((f32[16,128]{1,0:T(8,128)S(1)}, f32[16,128]{1,0:T(8,128)S(1)}, u32[]{:S(2)}, u32[]{:S(2)}) %collective-permute-start.1) | collective-permute-done | bytes 8224 | tf_op jit(solution)/shard_map/ppermute | solution.py:99
  90.7 5.5 %collective-permute-start.2 = (f32[16,128]{1,0:T(8,128)S(1)}, f32[16,128]{1,0:T(8,128)S(1)}, u32[]{:S(2)}, u32[]{:S(2)}) collective-permute-start(f32[16,128]{1,0:T(8,128)S(1)} %add.19), channel_id=1, source_target_pairs={{0,256},{32,288},{64,320},{96,352},{128,384},{160,416},{192,448},{... | collective-permute-start | bytes 24584 | tf_op jit(solution)/shard_map/ppermute | solution.py:99
  96.2 4.3 %collective-permute-start.3 = (f32[16,128]{1,0:T(8,128)S(1)}, f32[16,128]{1,0:T(8,128)S(1)}, u32[]{:S(2)}, u32[]{:S(2)}) collective-permute-start(f32[16,128]{1,0:T(8,128)S(1)} %add.19), channel_id=1, source_target_pairs={{0,512},{32,544},{64,576},{96,608},{128,640},{160,672},{192,704},{... | collective-permute-start | bytes 24584 | tf_op jit(solution)/shard_map/ppermute | solution.py:99
  100.5 0.0 collective-permute-done.2
  100.5 5.2 %collective-permute-done.3 = f32[16,128]{1,0:T(8,128)S(1)} collective-permute-done((f32[16,128]{1,0:T(8,128)S(1)}, f32[16,128]{1,0:T(8,128)S(1)}, u32[]{:S(2)}, u32[]{:S(2)}) %collective-permute-start.3) | collective-permute-done | bytes 8224 | tf_op jit(solution)/shard_map/ppermute | solution.py:99
  105.7 5.7 %collective-permute-start.4 = (f32[16,128]{1,0:T(8,128)S(1)}, f32[16,128]{1,0:T(8,128)S(1)}, u32[]{:S(2)}, u32[]{:S(2)}) collective-permute-start(f32[16,128]{1,0:T(8,128)S(1)} %select_add_fusion), channel_id=1, source_target_pairs={{0,384},{32,416},{64,448},{96,480},{128,512},{160,544},{192,576},{... | collective-permute-start | bytes 24584 | tf_op jit(solution)/shard_map/ppermute | solution.py:99
  111.3 6.2 %collective-permute-done.4 = f32[16,128]{1,0:T(8,128)S(1)} collective-permute-done((f32[16,128]{1,0:T(8,128)S(1)}, f32[16,128]{1,0:T(8,128)S(1)}, u32[]{:S(2)}, u32[]{:S(2)}) %collective-permute-start.4) | collective-permute-done | bytes 8224 | tf_op jit(solution)/shard_map/ppermute | solution.py:99
  117.5 0.7 broadcast_dynamic-update-slice_fusion
  118.2 0.0 all-to-all-done.2
  118.2 9.8 %all-to-all-start.3 = ((bf16[32,80,128]{2,1,0:T(8,128)(2,1)}), bf16[32,80,128]{2,1,0:T(8,128)(2,1)S(1)}, u32[]{:S(2)}, u32[]{:S(2)}) async-start(bf16[32,80,128]{2,1,0:T(8,128)(2,1)} %broadcast_dynamic-update-slice_fusion), calls=%async_computation.3 | async-start | bytes 1310720 | tf_op jit(solution)/shard_map/all_to_all | solution.py:176
  128.0 0.1 slice_reduce_fusion.sums_ref
  128.0 0.2 reduce_sum.34.middle_ref
  128.2 16.6 %all-to-all-done.3.last_ref = bf16[32,80,128]{2,1,0:T(8,128)(2,1)S(1)} async-done(((bf16[32,80,128]{2,1,0:T(8,128)(2,1)}), bf16[32,80,128]{2,1,0:T(8,128)(2,1)S(1)}, u32[]{:S(2)}, u32[]{:S(2)}) %all-to-all-start.3) | async-done | bytes 655392 | tf_op jit(solution)/shard_map/all_to_all | solution.py:176
  144.8 0.0 copy-done
  144.8 0.9 shard_map.106
  (5 shorter events, 0.1 us)
Async XLA Ops:
  3.4 36.1 %all-to-all-start = ((bf16[24,32,256]{2,1,0:T(8,128)(2,1)}), bf16[24,32,256]{2,1,0:T(8,128)(2,1)S(1)}, u32[]{:S(2)}, u32[]{:S(2)}) async-start(bf16[24,32,256]{2,1,0:T(8,128)(2,1)} %convolution_convert_fusion), calls=%async_computation | async-start | bytes 786432 | tf_op jit(solution)/shard_map/all_to_all | solution.py:138
  39.4 0.8 copy-start.1
  48.5 96.3 %copy-start = (bf16[256,256]{1,0:T(8,128)(2,1)S(1)}, bf16[256,256]{1,0:T(8,128)(2,1)}, u32[]{:S(2)}) copy-start(bf16[256,256]{1,0:T(8,128)(2,1)} %weight_ref.1) | copy-start | bytes 393220
  76.7 41.5 %all-to-all-start.2 = ((bf16[32,128,128]{2,1,0:T(8,128)(2,1)}), bf16[32,128,128]{2,1,0:T(8,128)(2,1)S(1)}, u32[]{:S(2)}, u32[]{:S(2)}) async-start(bf16[32,128,128]{2,1,0:T(8,128)(2,1)} %get-tuple-element.22), calls=%async_computation.2 | async-start | bytes 2097152 | tf_op jit(solution)/shard_map/all_to_all | solution.py:173
  82.1 3.1 %collective-permute-start = (f32[16,128]{1,0:T(8,128)S(1)}, f32[16,128]{1,0:T(8,128)S(1)}, u32[]{:S(2)}, u32[]{:S(2)}) collective-permute-start(f32[16,128]{1,0:T(8,128)S(1)} %convert_reduce_fusion), channel_id=1, source_target_pairs={{0,32},{32,0},{64,96},{96,64},{128,160},{160,128},{192,224},{224,1... | collective-permute-start | bytes 24584 | tf_op jit(solution)/shard_map/ppermute | solution.py:99
  85.2 5.5 %collective-permute-start.1 = (f32[16,128]{1,0:T(8,128)S(1)}, f32[16,128]{1,0:T(8,128)S(1)}, u32[]{:S(2)}, u32[]{:S(2)}) collective-permute-start(f32[16,128]{1,0:T(8,128)S(1)} %add.18), channel_id=1, source_target_pairs={{0,64},{32,96},{64,0},{96,32},{128,192},{160,224},{192,128},{224,1... | collective-permute-start | bytes 24584 | tf_op jit(solution)/shard_map/ppermute | solution.py:99
  90.7 9.8 %collective-permute-start.2 = (f32[16,128]{1,0:T(8,128)S(1)}, f32[16,128]{1,0:T(8,128)S(1)}, u32[]{:S(2)}, u32[]{:S(2)}) collective-permute-start(f32[16,128]{1,0:T(8,128)S(1)} %add.19), channel_id=1, source_target_pairs={{0,256},{32,288},{64,320},{96,352},{128,384},{160,416},{192,448},{... | collective-permute-start | bytes 24584 | tf_op jit(solution)/shard_map/ppermute | solution.py:99
  96.2 9.5 %collective-permute-start.3 = (f32[16,128]{1,0:T(8,128)S(1)}, f32[16,128]{1,0:T(8,128)S(1)}, u32[]{:S(2)}, u32[]{:S(2)}) collective-permute-start(f32[16,128]{1,0:T(8,128)S(1)} %add.19), channel_id=1, source_target_pairs={{0,512},{32,544},{64,576},{96,608},{128,640},{160,672},{192,704},{... | collective-permute-start | bytes 24584 | tf_op jit(solution)/shard_map/ppermute | solution.py:99
  105.7 11.8 %collective-permute-start.4 = (f32[16,128]{1,0:T(8,128)S(1)}, f32[16,128]{1,0:T(8,128)S(1)}, u32[]{:S(2)}, u32[]{:S(2)}) collective-permute-start(f32[16,128]{1,0:T(8,128)S(1)} %select_add_fusion), channel_id=1, source_target_pairs={{0,384},{32,416},{64,448},{96,480},{128,512},{160,544},{192,576},{... | collective-permute-start | bytes 24584 | tf_op jit(solution)/shard_map/ppermute | solution.py:99
  118.2 26.6 %all-to-all-start.3 = ((bf16[32,80,128]{2,1,0:T(8,128)(2,1)}), bf16[32,80,128]{2,1,0:T(8,128)(2,1)S(1)}, u32[]{:S(2)}, u32[]{:S(2)}) async-start(bf16[32,80,128]{2,1,0:T(8,128)(2,1)} %broadcast_dynamic-update-slice_fusion), calls=%async_computation.3 | async-start | bytes 1310720 | tf_op jit(solution)/shard_map/all_to_all | solution.py:176

commit v4 on v1

v4 whole, which is shorter than its diff:
```python
import functools

import jax
import jax.numpy as jnp
from jax import lax
from jax.experimental import pallas as pl
from jax.experimental.pallas import tpu as pltpu
from jax.sharding import PartitionSpec as P

VMEM_BYTES = 24000000
SMEM = pl.BlockSpec(memory_space=pltpu.SMEM)
VMEM = pl.BlockSpec(memory_space=pltpu.VMEM)
HBM = pl.BlockSpec(memory_space=pltpu.HBM)


def place_tiles(index_ref, count_ref, tiles_ref, features_ref, turned_ref, mixed_ref, dense, turned, total, sem):
    col_blocks, row_blocks, size, _ = dense.shape
    dense[...] = jnp.zeros_like(dense)
    turned[...] = jnp.zeros_like(turned)
    total[...] = jnp.zeros_like(total)
    count = count_ref[0]

    def place(t, carry):
        k = index_ref[t]
        c, r = lax.rem(k, col_blocks), lax.div(k, col_blocks)
        tile = jnp.where(t < count, tiles_ref[t], jnp.zeros_like(tiles_ref[t]))
        dense[c, r] = tile
        first = pl.multiple_of(c * size, size)
        turned[pl.ds(first, size), pl.ds(pl.multiple_of(r * size, size), size)] = tile.T
        return carry

    lax.fori_loop(0, tiles_ref.shape[0], place, 0, unroll=4)
    copy = pltpu.make_async_copy(turned, turned_ref, sem)
    copy.start()

    def mix(j, carry):
        left = dense[2 * j].reshape(row_blocks * size, size)
        right = dense[2 * j + 1].reshape(row_blocks * size, size)
        total[...] += jnp.dot(
            jnp.concatenate([left, right], axis=1),
            features_ref[pl.ds(pl.multiple_of(2 * j * size, 2 * size), 2 * size), :],
            preferred_element_type=jnp.float32,
        )
        return carry

    lax.fori_loop(0, col_blocks // 2, mix, 0)
    mixed_ref[...] = total[...].astype(mixed_ref.dtype).T
    copy.wait()


def weight_terms(mixed_ref, rows_ref, out_ref):
    depth, width = out_ref.shape[1:]
    slices = mixed_ref.shape[0] // depth
    term = jnp.dot(mixed_ref[...], rows_ref[...], preferred_element_type=jnp.float32)
    out_ref[:slices] = term.reshape(slices, depth, width)
    out_ref[slices:] = jnp.zeros((out_ref.shape[0] - slices, depth, width), jnp.float32)


def products(odd_ref, rows_ref, turned_ref, keep_ref, near_ref, far_ref, turned, sems):
    blocks, size, _ = keep_ref.shape
    half = size // 2
    odd = odd_ref[0]

    def fetch(g):
        span = pl.ds(pl.multiple_of(2 * g * size, 2 * size), 2 * size)
        return pltpu.make_async_copy(turned_ref.at[span], turned.at[span], sems.at[g])

    def start(g, carry):
        fetch(g).start()
        return carry

    def pair(g, carry):
        fetch(g).wait()
        kept = turned[pl.ds(pl.multiple_of((2 * g + odd) * size, size), size), :]
        sent = turned[pl.ds(pl.multiple_of((2 * g + 1 - odd) * size, size), size), :]
        part = jnp.dot(
            jnp.concatenate([kept, sent], axis=0), rows_ref[...], preferred_element_type=jnp.float32
        )
        keep_ref[g] = part[:size]
        near_ref[g] = part[size : size + half].astype(near_ref.dtype)
        far_ref[g] = part[size + half :].astype(far_ref.dtype)
        return carry

    lax.fori_loop(0, blocks, start, 0)
    lax.fori_loop(0, blocks, pair, 0)


def add_partners(keep_ref, near_ref, far_ref, share_ref, out_ref):
    blocks, size, _ = keep_ref.shape
    half = size // 2
    share = share_ref[...].astype(out_ref.dtype)

    def block(g, carry):
        out_ref[g, :half] = (keep_ref[g, :half] + near_ref[g].astype(jnp.float32)).astype(out_ref.dtype)
        out_ref[g, half:size] = (keep_ref[g, half:] + far_ref[g].astype(jnp.float32)).astype(out_ref.dtype)
        out_ref[g, size:] = share
        return carry

    lax.fori_loop(0, blocks, block, 0)


def per_device(
    out_grad, pre_relu, features, weight, send_rows, send_count, tile_index, tile_count, tile_values
):
    node_dev, width = out_grad.shape
    n_rows = lax.axis_size("rows")
    n_rep = lax.axis_size("rep")
    per_peer = send_rows.shape[2]
    size = tile_values.shape[2]
    col_blocks = features.shape[0] // size
    total_rows = n_rows * per_peer
    row_blocks = total_rows // size
    slices = 16
    depth = width // slices
    blocks = col_blocks // 2
    groups = [list(range(odd, n_rep, 2)) for odd in (0, 1)]
    exchange = functools.partial(lax.all_to_all, split_axis=0, concat_axis=0, tiled=True)
    params = pltpu.CompilerParams(vmem_limit_bytes=VMEM_BYTES)

    def swapped(value, mask):
        return lax.ppermute(value, "rep", [(i, i ^ mask) for i in range(n_rep)])

    grad_pre = jnp.where(pre_relu > 0, out_grad, jnp.zeros_like(out_grad))
    slot_iota = jnp.arange(per_peer, dtype=jnp.int32)
    wanted = jnp.where(slot_iota[None, :] < send_count[0][:, None], send_rows[0], -1)
    picks = (wanted[:, :, None] == jnp.arange(node_dev, dtype=jnp.int32)).astype(jnp.bfloat16)
    outgoing = lax.dot_general(
        picks, grad_pre, (((2,), (0,)), ((), ())), preferred_element_type=jnp.float32
    ).astype(jnp.bfloat16)
    received = exchange(outgoing, "rows").reshape(total_rows, width)

    turned, mixed = pl.pallas_call(
        place_tiles,
        out_shape=(
            pltpu.HBM((col_blocks * size, total_rows), jnp.bfloat16),
            jax.ShapeDtypeStruct((width, total_rows), jnp.bfloat16),
        ),
        in_specs=[SMEM, SMEM, VMEM, VMEM],
        out_specs=(HBM, VMEM),
        scratch_shapes=[
            pltpu.VMEM((col_blocks, row_blocks, size, size), jnp.bfloat16),
            pltpu.VMEM((col_blocks * size, total_rows), jnp.bfloat16),
            pltpu.VMEM((total_rows, width), jnp.float32),
            pltpu.SemaphoreType.DMA,
        ],
        compiler_params=params,
        cost_estimate=pl.CostEstimate(flops=1600000000, bytes_accessed=24000000, transcendentals=0),
    )(tile_index[0], tile_count, tile_values[0], features)

    term = pl.pallas_call(
        weight_terms,
        out_shape=jax.ShapeDtypeStruct((n_rows, depth, width), jnp.float32),
        in_specs=[VMEM, VMEM],
        out_specs=VMEM,
        compiler_params=params,
    )(mixed, received)
    share = jnp.sum(exchange(term, "rows"), axis=0)
    share = share + swapped(share, 1)

    odd = (lax.axis_index("rep") % 2).astype(jnp.int32)[None]
    half = jax.ShapeDtypeStruct((blocks, size // 2, width), jnp.bfloat16)
    keep, near, far = pl.pallas_call(
        products,
        out_shape=(jax.ShapeDtypeStruct((blocks, size, width), jnp.float32), half, half),
        in_specs=[SMEM, VMEM, HBM],
        out_specs=(VMEM, VMEM, VMEM),
        scratch_shapes=[
            pltpu.VMEM((col_blocks * size, total_rows), jnp.bfloat16),
            pltpu.SemaphoreType.DMA((blocks,)),
        ],
        compiler_params=params,
        cost_estimate=pl.CostEstimate(flops=1700000000, bytes_accessed=9000000, transcendentals=0),
    )(odd, received, pltpu.with_memory_space_constraint(turned, pltpu.HBM))
    near, far = swapped(near, 1), swapped(far, 3)

    parts = pl.pallas_call(
        add_partners,
        out_shape=jax.ShapeDtypeStruct((blocks, size + depth, width), jnp.bfloat16),
        in_specs=[VMEM, VMEM, VMEM, VMEM],
        out_specs=VMEM,
        compiler_params=params,
    )(keep, near, far, share)
    parts = exchange(parts, "rep", axis_index_groups=groups)

    own = jnp.sum(parts[:, size:].astype(jnp.float32), axis=0).astype(jnp.bfloat16)
    whole = exchange(jnp.broadcast_to(own[None], (n_rows, depth, width)), "rows")
    weight_grad = whole[:slices].reshape(width, width).astype(jnp.float32)

    grads = jnp.sum(parts[:, :size].astype(jnp.float32), axis=0)
    feature_grad = lax.dot_general(
        grads.astype(jnp.bfloat16),
        weight,
        (((1,), (1,)), ((), ())),
        preferred_element_type=jnp.float32,
    ).astype(jnp.bfloat16)
    return (feature_grad, weight_grad)


def solution(mesh):
    return jax.shard_map(
        per_device,
        mesh=mesh,
        in_specs=(
            P(("rows", "rep"), None),
            P(("rows", "rep"), None),
            P("rows", None),
            P(),
            P(("rows", "rep"), None, None),
            P(("rows", "rep"), None),
            P(("rows", "rep"), None),
            P(("rows", "rep")),
            P(("rows", "rep"), None, None, None),
        ),
        out_specs=(P(("rows", "rep"), None), P()),
        check_vma=False,
    )
```

time: 166 us -> 140 us (0.84)
  the two profiles are of different devices: /device:TPU:6 before, /device:TPU:1 now
where the time goes in v4:
time: 140 us
  starting transfers between devices  46.2 us (33%)
  blocking collectives  38.2 us (27%)
  waiting for transfers between devices  27 us (19%)
  Pallas kernels  17.4 us (12%)
  local copies, waits for them, and re-layouts  4.84 us (3%)
  matrix products  2.77 us (2%)
  other arithmetic  1.75 us (1%)
    all_to_all x1, blocking collectives, per_device(): parts = exchange(parts, 'rep', axis_index_groups=groups)  38.2 us
    all_to_all x1, starting transfers between devices, per_device(): received = exchange(outgoing, 'rows').reshape(total_rows, width)  16.7 us
    all_to_all x1, starting transfers between devices, per_device(): exchange(jnp.broadcast_to(own[None], (n_rows, depth, width)), 'rows')  13.4 us
    all_to_all x1, waiting for transfers between devices, per_device(): exchange(jnp.broadcast_to(own[None], (n_rows, depth, width)), 'rows')  12.7 us
    ppermute x3, starting transfers between devices, swapped(): return lax.ppermute(value, 'rep', [(i, i ^ mask) for i in range(n_rep)])  9.96 us
    pallas_call x1, Pallas kernels, per_device(): pl.pallas_call(place_tiles, out_shape=(pltpu.HBM((col_blocks * size, tota...  8.57 us
    pallas_call x1, Pallas kernels, per_device(): pl.pallas_call(products, out_shape=(jax.ShapeDtypeStruct((blocks, size, w...  6.49 us
    all_to_all x1, starting transfers between devices, per_device(): share = jnp.sum(exchange(term, 'rows'), axis=0)  6.22 us
  transfers between devices with their start and end apart: 6, of which 5 were waited for; matrix products, arithmetic and copies ran while one was open for 1% of the time, Pallas kernels for 11%

profile of v4, /device:TPU:1, one launch (start us, length us, event | category | flops | bytes accessed | tf_op | source)
XLA Modules:
  0.0 139.6 jit_solution(15564978149580310988)
XLA Ops:
  0.6 0.0 copy-start
  0.6 0.8 bitcast_select_fusion
  1.5 1.9 %convolution_convert_fusion = bf16[24,32,256]{2,1,0:T(8,128)(2,1)} fusion(s32[24,32]{1,0:T(8,128)S(1)} %bitcast_select_fusion, bf16[128,256]{1,0:T(8,128)(2,1)} %param.9, bf16[128,256]{1,0:T(8,128)(2,1)} %param.10), kind=kOutput, calls=%fused_computation | convolution fusion | flops 50692096 | bytes 527360 | tf_op jit(solution)/shard_map/dot_general | solution.py:127
  3.4 16.7 %all-to-all-start = ((bf16[24,32,256]{2,1,0:T(8,128)(2,1)}), bf16[24,32,256]{2,1,0:T(8,128)(2,1)S(1)}, u32[]{:S(2)}, u32[]{:S(2)}) async-start(bf16[24,32,256]{2,1,0:T(8,128)(2,1)} %convolution_convert_fusion), calls=%async_computation | async-start | bytes 786432 | tf_op jit(solution)/shard_map/all_to_all | solution.py:130
  20.7 0.0 copy-start.1
  20.8 1.9 %copy-done.1 = bf16[1,96,128,128]{3,2,1,0:T(8,128)(2,1)S(1)} copy-done((bf16[1,96,128,128]{3,2,1,0:T(8,128)(2,1)S(1)}, bf16[1,96,128,128]{3,2,1,0:T(8,128)(2,1)}, u32[]{:S(2)}) %copy-start.1) | copy-done | bytes 3145752
  22.6 0.0 copy-start.2
  22.6 1.6 %copy-done.2 = bf16[4096,256]{1,0:T(8,128)(2,1)S(1)} copy-done((bf16[4096,256]{1,0:T(8,128)(2,1)S(1)}, bf16[4096,256]{1,0:T(8,128)(2,1)}, u32[]{:S(2)}) %copy-start.2) | copy-done | bytes 2097176
  24.2 0.0 copy-start.3
  24.2 0.7 copy-done.3
  24.9 8.6 %shard_map.104 = (bf16[4096,768]{1,0:T(8,128)(2,1)}, bf16[256,768]{1,0:T(8,128)(2,1)S(1)}) custom-call(s32[96]{0:T(128)S(1)} %bitcast.18, s32[1]{0:T(128)S(6)} %copy.11.count_ref, bf16[96,128,128]{2,1,0:T(8,128)(2,1)S(1)} %bitcast.17, bf16[4096,256]{1,0:T(8,128)(2,1)S(1)} %copy-done.2), custom_call_target="tpu_custom_call" | custom-call | flops 1600000000 | bytes 24000000 | tf_op jit(solution)/shard_map/pallas_call | solution.py:132
  33.5 4.9 %all-to-all-done = bf16[24,32,256]{2,1,0:T(8,128)(2,1)S(1)} async-done(((bf16[24,32,256]{2,1,0:T(8,128)(2,1)}), bf16[24,32,256]{2,1,0:T(8,128)(2,1)S(1)}, u32[]{:S(2)}, u32[]{:S(2)}) %all-to-all-start) | async-done | bytes 393248 | tf_op jit(solution)/shard_map/all_to_all | solution.py:130
  38.3 1.0 shard_map.106
  39.3 6.2 %all-to-all-start.1 = ((f32[24,16,256]{2,1,0:T(8,128)}), f32[24,16,256]{2,1,0:T(8,128)S(1)}, u32[]{:S(2)}, u32[]{:S(2)}) async-start(f32[24,16,256]{2,1,0:T(8,128)} %shard_map.106), calls=%async_computation.1 | async-start | bytes 786432 | tf_op jit(solution)/shard_map/all_to_all | solution.py:157
  45.6 6.5 %shard_map.105 = (f32[16,128,256]{2,1,0:T(8,128)S(1)}, bf16[16,64,256]{2,1,0:T(8,128)(2,1)}, bf16[16,64,256]{2,1,0:T(8,128)(2,1)}) custom-call(s32[1]{0:T(128)} %bitcast.odd_ref, bf16[768,256]{1,0:T(8,128)(2,1)S(1)} %bitcast.16, bf16[4096,768]{1,0:T(8,128)(2,1)} %get-tuple-element.7.turned_ref), custom_call_target="tpu_custom_call" | custom-call | flops 1700000000 | bytes 9000000 | tf_op jit(solution)/shard_map/pallas_call | solution.py:162
  52.1 3.1 %collective-permute-start = (bf16[16,64,256]{2,1,0:T(8,128)(2,1)}, bf16[16,64,256]{2,1,0:T(8,128)(2,1)S(1)}, u32[]{:S(2)}, u32[]{:S(2)}) collective-permute-start(bf16[16,64,256]{2,1,0:T(8,128)(2,1)} %get-tuple-element.9), channel_id=1, source_target_pairs={{0,1},{1,0},{2,3},{3,2},{4,5},{5,4},{6,7},{7,6},{8,9},{9,8},{10,11... | collective-permute-start | bytes 1572872 | tf_op jit(solution)/shard_map/ppermute | solution.py:121
  55.2 3.7 %collective-permute-start.1 = (bf16[16,64,256]{2,1,0:T(8,128)(2,1)}, bf16[16,64,256]{2,1,0:T(8,128)(2,1)}, u32[]{:S(2)}, u32[]{:S(2)}) collective-permute-start(bf16[16,64,256]{2,1,0:T(8,128)(2,1)} %get-tuple-element.10), channel_id=1, source_target_pairs={{0,3},{1,2},{2,1},{3,0},{4,7},{5,6},{6,5},{7,4},{8,11},{9,10},{10,... | collective-permute-start | bytes 1572872 | tf_op jit(solution)/shard_map/ppermute | solution.py:121
  58.9 4.8 %all-to-all-done.1 = f32[24,16,256]{2,1,0:T(8,128)S(1)} async-done(((f32[24,16,256]{2,1,0:T(8,128)}), f32[24,16,256]{2,1,0:T(8,128)S(1)}, u32[]{:S(2)}, u32[]{:S(2)}) %all-to-all-start.1) | async-done | bytes 393248 | tf_op jit(solution)/shard_map/all_to_all | solution.py:157
  63.8 3.1 %collective-permute-start.2 = (f32[16,256]{1,0:T(8,128)S(1)}, f32[16,256]{1,0:T(8,128)S(1)}, u32[]{:S(2)}, u32[]{:S(2)}) collective-permute-start(f32[16,256]{1,0:T(8,128)S(1)} %reduce_sum.33), channel_id=1, source_target_pairs={{0,1},{1,0},{2,3},{3,2},{4,5},{5,4},{6,7},{7,6},{8,9},{9,8},{10,11... | collective-permute-start | bytes 49160 | tf_op jit(solution)/shard_map/ppermute | solution.py:121
  66.9 1.8 %collective-permute-done.2 = f32[16,256]{1,0:T(8,128)S(1)} collective-permute-done((f32[16,256]{1,0:T(8,128)S(1)}, f32[16,256]{1,0:T(8,128)S(1)}, u32[]{:S(2)}, u32[]{:S(2)}) %collective-permute-start.2) | collective-permute-done | bytes 16416 | tf_op jit(solution)/shard_map/ppermute | solution.py:121
  68.7 0.0 collective-permute-done.near_ref
  68.7 2.8 %collective-permute-done.1.far_ref = bf16[16,64,256]{2,1,0:T(8,128)(2,1)} collective-permute-done((bf16[16,64,256]{2,1,0:T(8,128)(2,1)}, bf16[16,64,256]{2,1,0:T(8,128)(2,1)}, u32[]{:S(2)}, u32[]{:S(2)}) %collective-permute-start.1) | collective-permute-done | bytes 524320 | tf_op jit(solution)/shard_map/ppermute | solution.py:121
  71.5 1.3 shard_map.107
  72.8 38.2 %all_to_all.20 = bf16[16,144,256]{2,1,0:T(8,128)(2,1)S(1)} all-to-all(bf16[16,144,256]{2,1,0:T(8,128)(2,1)S(1)} %shard_map.107), channel_id=1, replica_groups={{0,2,4,6,8,10,12,14,16,18,20,22,24,26,28,30},{1,3,5,7,9,11,13,15,17,19,..., dimensions={0} | all-to-all | bytes 2359296 | tf_op jit(solution)/shard_map/all_to_all | solution.py:183
  111.0 0.7 broadcast_in_dim.18
  111.7 13.4 %all-to-all-start.3 = ((bf16[24,16,256]{2,1,0:T(8,128)(2,1)}), bf16[24,16,256]{2,1,0:T(8,128)(2,1)S(1)}, u32[]{:S(2)}, u32[]{:S(2)}) async-start(bf16[24,16,256]{2,1,0:T(8,128)(2,1)} %broadcast_in_dim.18), calls=%async_computation.3 | async-start | bytes 393216 | tf_op jit(solution)/shard_map/all_to_all | solution.py:186
  125.1 0.1 slice_reduce_fusion
  125.2 0.0 copy-done
  125.2 0.8 convolution_convert_fusion.1
  126.1 12.7 %all-to-all-done.3 = bf16[24,16,256]{2,1,0:T(8,128)(2,1)S(1)} async-done(((bf16[24,16,256]{2,1,0:T(8,128)(2,1)}), bf16[24,16,256]{2,1,0:T(8,128)(2,1)S(1)}, u32[]{:S(2)}, u32[]{:S(2)}) %all-to-all-start.3) | async-done | bytes 196640 | tf_op jit(solution)/shard_map/all_to_all | solution.py:186
  138.8 0.7 bitcast_convert_fusion
  (4 shorter events, 0.1 us)
Async XLA Ops:
  0.6 124.6 %copy-start = (bf16[256,256]{1,0:T(8,128)(2,1)S(1)}, bf16[256,256]{1,0:T(8,128)(2,1)}, u32[]{:S(2)}) copy-start(bf16[256,256]{1,0:T(8,128)(2,1)} %param.12) | copy-start | bytes 393220
  3.4 34.9 %all-to-all-start = ((bf16[24,32,256]{2,1,0:T(8,128)(2,1)}), bf16[24,32,256]{2,1,0:T(8,128)(2,1)S(1)}, u32[]{:S(2)}, u32[]{:S(2)}) async-start(bf16[24,32,256]{2,1,0:T(8,128)(2,1)} %convolution_convert_fusion), calls=%async_computation | async-start | bytes 786432 | tf_op jit(solution)/shard_map/all_to_all | solution.py:130
  20.7 1.9 %copy-start.1 = (bf16[1,96,128,128]{3,2,1,0:T(8,128)(2,1)S(1)}, bf16[1,96,128,128]{3,2,1,0:T(8,128)(2,1)}, u32[]{:S(2)}) copy-start(bf16[1,96,128,128]{3,2,1,0:T(8,128)(2,1)} %param.17) | copy-start | bytes 9437188
  22.6 1.6 %copy-start.2 = (bf16[4096,256]{1,0:T(8,128)(2,1)S(1)}, bf16[4096,256]{1,0:T(8,128)(2,1)}, u32[]{:S(2)}) copy-start(bf16[4096,256]{1,0:T(8,128)(2,1)} %features_ref.1) | copy-start | bytes 6291460
  24.2 0.7 copy-start.3
  39.3 24.4 %all-to-all-start.1 = ((f32[24,16,256]{2,1,0:T(8,128)}), f32[24,16,256]{2,1,0:T(8,128)S(1)}, u32[]{:S(2)}, u32[]{:S(2)}) async-start(f32[24,16,256]{2,1,0:T(8,128)} %shard_map.106), calls=%async_computation.1 | async-start | bytes 786432 | tf_op jit(solution)/shard_map/all_to_all | solution.py:157
  52.1 16.6 %collective-permute-start = (bf16[16,64,256]{2,1,0:T(8,128)(2,1)}, bf16[16,64,256]{2,1,0:T(8,128)(2,1)S(1)}, u32[]{:S(2)}, u32[]{:S(2)}) collective-permute-start(bf16[16,64,256]{2,1,0:T(8,128)(2,1)} %get-tuple-element.9), channel_id=1, source_target_pairs={{0,1},{1,0},{2,3},{3,2},{4,5},{5,4},{6,7},{7,6},{8,9},{9,8},{10,11... | collective-permute-start | bytes 1572872 | tf_op jit(solution)/shard_map/ppermute | solution.py:121
  55.2 16.3 %collective-permute-start.1 = (bf16[16,64,256]{2,1,0:T(8,128)(2,1)}, bf16[16,64,256]{2,1,0:T(8,128)(2,1)}, u32[]{:S(2)}, u32[]{:S(2)}) collective-permute-start(bf16[16,64,256]{2,1,0:T(8,128)(2,1)} %get-tuple-element.10), channel_id=1, source_target_pairs={{0,3},{1,2},{2,1},{3,0},{4,7},{5,6},{6,5},{7,4},{8,11},{9,10},{10,... | collective-permute-start | bytes 1572872 | tf_op jit(solution)/shard_map/ppermute | solution.py:121
  63.8 4.9 %collective-permute-start.2 = (f32[16,256]{1,0:T(8,128)S(1)}, f32[16,256]{1,0:T(8,128)S(1)}, u32[]{:S(2)}, u32[]{:S(2)}) collective-permute-start(f32[16,256]{1,0:T(8,128)S(1)} %reduce_sum.33), channel_id=1, source_target_pairs={{0,1},{1,0},{2,3},{3,2},{4,5},{5,4},{6,7},{7,6},{8,9},{9,8},{10,11... | collective-permute-start | bytes 49160 | tf_op jit(solution)/shard_map/ppermute | solution.py:121
  111.7 27.1 %all-to-all-start.3 = ((bf16[24,16,256]{2,1,0:T(8,128)(2,1)}), bf16[24,16,256]{2,1,0:T(8,128)(2,1)S(1)}, u32[]{:S(2)}, u32[]{:S(2)}) async-start(bf16[24,16,256]{2,1,0:T(8,128)(2,1)} %broadcast_in_dim.18), calls=%async_computation.3 | async-start | bytes 393216 | tf_op jit(solution)/shard_map/all_to_all | solution.py:186

commit v5 on v4

--- a/solution.py
+++ b/solution.py
@@ -8,6 +8,8 @@
 from jax.sharding import PartitionSpec as P
 
 VMEM_BYTES = 24000000
+SLICES = 8
+PAIRS = 4
 SMEM = pl.BlockSpec(memory_space=pltpu.SMEM)
 VMEM = pl.BlockSpec(memory_space=pltpu.VMEM)
 HBM = pl.BlockSpec(memory_space=pltpu.HBM)
@@ -52,51 +54,64 @@
     depth, width = out_ref.shape[1:]
     slices = mixed_ref.shape[0] // depth
     term = jnp.dot(mixed_ref[...], rows_ref[...], preferred_element_type=jnp.float32)
-    out_ref[:slices] = term.reshape(slices, depth, width)
-    out_ref[slices:] = jnp.zeros((out_ref.shape[0] - slices, depth, width), jnp.float32)
+    term = term.astype(out_ref.dtype).reshape(slices, depth, width)
+    for first in range(0, out_ref.shape[0], slices):
+        out_ref[first : first + slices] = term
+
+
+def spread_sum(terms_ref, after_ref, out_ref):
+    del after_ref
+    total = terms_ref[0].astype(jnp.float32)
+    for i in range(1, terms_ref.shape[0]):
+        total += terms_ref[i].astype(jnp.float32)
+    total = total.astype(out_ref.dtype)
+    for p in range(out_ref.shape[0]):
+        out_ref[p] = total
 
 
 def products(odd_ref, rows_ref, turned_ref, keep_ref, near_ref, far_ref, turned, sems):
     blocks, size, _ = keep_ref.shape
     half = size // 2
     odd = odd_ref[0]
-
-    def fetch(g):
-        span = pl.ds(pl.multiple_of(2 * g * size, 2 * size), 2 * size)
-        return pltpu.make_async_copy(turned_ref.at[span], turned.at[span], sems.at[g])
-
-    def start(g, carry):
-        fetch(g).start()
-        return carry
-
-    def pair(g, carry):
-        fetch(g).wait()
-        kept = turned[pl.ds(pl.multiple_of((2 * g + odd) * size, size), size), :]
-        sent = turned[pl.ds(pl.multiple_of((2 * g + 1 - odd) * size, size), size), :]
-        part = jnp.dot(
-            jnp.concatenate([kept, sent], axis=0), rows_ref[...], preferred_element_type=jnp.float32
-        )
-        keep_ref[g] = part[:size]
-        near_ref[g] = part[size : size + half].astype(near_ref.dtype)
-        far_ref[g] = part[size + half :].astype(far_ref.dtype)
-        return carry
-
-    lax.fori_loop(0, blocks, start, 0)
-    lax.fori_loop(0, blocks, pair, 0)
-
-
-def add_partners(keep_ref, near_ref, far_ref, share_ref, out_ref):
+    copies = []
+    for g in range(blocks):
+        span = pl.ds(2 * g * size, 2 * size)
+        copies.append(pltpu.make_async_copy(turned_ref.at[span], turned.at[span], sems.at[g]))
+        copies[-1].start()
+    for first in range(0, blocks, PAIRS):
+        taken = []
+        for g in range(first, first + PAIRS):
+            copies[g].wait()
+            for c in (2 * g + odd, 2 * g + 1 - odd):
+                taken.append(turned[pl.ds(pl.multiple_of(c * size, size), size), :])
+        part = jnp.dot(jnp.concatenate(taken, axis=0), rows_ref[...], preferred_element_type=jnp.float32)
+        for i in range(PAIRS):
+            kept, sent = part[2 * i * size : (2 * i + 1) * size], part[(2 * i + 1) * size : (2 * i + 2) * size]
+            keep_ref[first + i] = kept
+            near_ref[first + i] = sent[:half].astype(near_ref.dtype)
+            far_ref[first + i] = sent[half:].astype(far_ref.dtype)
+
+
+def add_partners(keep_ref, near_ref, far_ref, out_ref):
     blocks, size, _ = keep_ref.shape
     half = size // 2
-    share = share_ref[...].astype(out_ref.dtype)
 
     def block(g, carry):
         out_ref[g, :half] = (keep_ref[g, :half] + near_ref[g].astype(jnp.float32)).astype(out_ref.dtype)
         out_ref[g, half:size] = (keep_ref[g, half:] + far_ref[g].astype(jnp.float32)).astype(out_ref.dtype)
-        out_ref[g, size:] = share
         return carry
 
-    lax.fori_loop(0, blocks, block, 0)
+    lax.fori_loop(0, blocks, block, 0, unroll=2)
+
+
+def put_in_order(place_ref, own_ref, one_ref, two_ref, four_ref, out_ref):
+    depth = own_ref.shape[0]
+    pieces = [own_ref[...], one_ref[...]]
+    pieces += [two_ref[i * depth : (i + 1) * depth] for i in range(2)]
+    pieces += [four_ref[i * depth : (i + 1) * depth] for i in range(4)]
+    for j, piece in enumerate(pieces):
+        first = pl.multiple_of((place_ref[0] ^ j) * depth, depth)
+        out_ref[pl.ds(first, depth), :] = piece
 
 
 def per_device(
@@ -110,15 +125,14 @@
     col_blocks = features.shape[0] // size
     total_rows = n_rows * per_peer
     row_blocks = total_rows // size
-    slices = 16
-    depth = width // slices
+    depth = width // SLICES
     blocks = col_blocks // 2
     groups = [list(range(odd, n_rep, 2)) for odd in (0, 1)]
     exchange = functools.partial(lax.all_to_all, split_axis=0, concat_axis=0, tiled=True)
     params = pltpu.CompilerParams(vmem_limit_bytes=VMEM_BYTES)
 
-    def swapped(value, mask):
-        return lax.ppermute(value, "rep", [(i, i ^ mask) for i in range(n_rep)])
+    def swapped(value, mask, axis="rep"):
+        return lax.ppermute(value, axis, [(i, i ^ mask) for i in range(lax.axis_size(axis))])
 
     grad_pre = jnp.where(pre_relu > 0, out_grad, jnp.zeros_like(out_grad))
     slot_iota = jnp.arange(per_peer, dtype=jnp.int32)
@@ -149,13 +163,12 @@
 
     term = pl.pallas_call(
         weight_terms,
-        out_shape=jax.ShapeDtypeStruct((n_rows, depth, width), jnp.float32),
+        out_shape=jax.ShapeDtypeStruct((n_rows, depth, width), jnp.bfloat16),
         in_specs=[VMEM, VMEM],
         out_specs=VMEM,
         compiler_params=params,
     )(mixed, received)
-    share = jnp.sum(exchange(term, "rows"), axis=0)
-    share = share + swapped(share, 1)
+    terms = exchange(term, "rows")
 
     odd = (lax.axis_index("rep") % 2).astype(jnp.int32)[None]
     half = jax.ShapeDtypeStruct((blocks, size // 2, width), jnp.bfloat16)
@@ -171,22 +184,37 @@
         compiler_params=params,
         cost_estimate=pl.CostEstimate(flops=1700000000, bytes_accessed=9000000, transcendentals=0),
     )(odd, received, pltpu.with_memory_space_constraint(turned, pltpu.HBM))
+    share = pl.pallas_call(
+        spread_sum,
+        out_shape=jax.ShapeDtypeStruct((n_rep, depth, width), jnp.bfloat16),
+        in_specs=[VMEM, pl.BlockSpec(memory_space=pl.ANY)],
+        out_specs=VMEM,
+        compiler_params=params,
+    )(terms, near)
+    own = jnp.sum(exchange(share, "rep").astype(jnp.float32), axis=0)
     near, far = swapped(near, 1), swapped(far, 3)
 
     parts = pl.pallas_call(
         add_partners,
-        out_shape=jax.ShapeDtypeStruct((blocks, size + depth, width), jnp.bfloat16),
-        in_specs=[VMEM, VMEM, VMEM, VMEM],
-        out_specs=VMEM,
-        compiler_params=params,
-    )(keep, near, far, share)
+        out_shape=jax.ShapeDtypeStruct((blocks, size, width), jnp.bfloat16),
+        in_specs=[VMEM, VMEM, VMEM],
+        out_specs=VMEM,
+        compiler_params=params,
+    )(keep, near, far)
     parts = exchange(parts, "rep", axis_index_groups=groups)
 
-    own = jnp.sum(parts[:, size:].astype(jnp.float32), axis=0).astype(jnp.bfloat16)
-    whole = exchange(jnp.broadcast_to(own[None], (n_rows, depth, width)), "rows")
-    weight_grad = whole[:slices].reshape(width, width).astype(jnp.float32)
-
-    grads = jnp.sum(parts[:, :size].astype(jnp.float32), axis=0)
+    one = swapped(own, 1, "rows")
+    two = swapped(jnp.concatenate([own, one], axis=0), 2, "rows")
+    four = swapped(jnp.concatenate([own, one, two], axis=0), 4, "rows")
+    weight_grad = pl.pallas_call(
+        put_in_order,
+        out_shape=jax.ShapeDtypeStruct((width, width), jnp.float32),
+        in_specs=[SMEM, VMEM, VMEM, VMEM, VMEM],
+        out_specs=VMEM,
+        compiler_params=params,
+    )((lax.axis_index("rows") % SLICES).astype(jnp.int32)[None], own, one, two, four)
+
+    grads = jnp.sum(parts.astype(jnp.float32), axis=0)
     feature_grad = lax.dot_general(
         grads.astype(jnp.bfloat16),
         weight,

time: 140 us -> 136 us (0.971)
  the two profiles are of different devices: /device:TPU:1 before, /device:TPU:128 now
where the time goes in v5:
time: 136 us; the launch traced here: 135 us
  starting transfers between devices  53.8 us (40%)
  waiting for transfers between devices  51.5 us (38%)
  Pallas kernels  18 us (13%)
  local copies, waits for them, and re-layouts  5.75 us (4%)
  matrix products  2.79 us (2%)
  other arithmetic  2.1 us (2%)
  between operations  1.44 us (1%)
    ppermute x5, waiting for transfers between devices, swapped(): lax.ppermute(value, axis, [(i, i ^ mask) for i in range(lax.axis_size(axi...  25.8 us
    ppermute x5, starting transfers between devices, swapped(): lax.ppermute(value, axis, [(i, i ^ mask) for i in range(lax.axis_size(axi...  14.9 us
    all_to_all x1, starting transfers between devices, per_device(): received = exchange(outgoing, 'rows').reshape(total_rows, width)  13.9 us
    all_to_all x1, waiting for transfers between devices, per_device(): parts = exchange(parts, 'rep', axis_index_groups=groups)  11.6 us
    all_to_all x1, waiting for transfers between devices, per_device(): terms = exchange(term, 'rows')  10.5 us
    all_to_all x1, starting transfers between devices, per_device(): own = jnp.sum(exchange(share, 'rep').astype(jnp.float32), axis=0)  9.95 us
    pallas_call x1, Pallas kernels, per_device(): pl.pallas_call(place_tiles, out_shape=(pltpu.HBM((col_blocks * size, tota...  8.53 us
    all_to_all x1, starting transfers between devices, per_device(): terms = exchange(term, 'rows')  7.56 us
  transfers between devices with their start and end apart: 9, of which 8 were waited for; matrix products, arithmetic and copies ran while one was open for 1% of the time, Pallas kernels for 12%

profile of v5, /device:TPU:128, one launch (start us, length us, event | category | flops | bytes accessed | tf_op | source)
XLA Modules:
  0.0 135.4 jit_solution(3908550361366316576)
XLA Ops:
  0.6 0.0 copy-start
  0.6 0.8 bitcast_select_fusion
  1.5 2.0 %convolution_convert_fusion = bf16[24,32,256]{2,1,0:T(8,128)(2,1)} fusion(s32[24,32]{1,0:T(8,128)S(1)} %bitcast_select_fusion, bf16[128,256]{1,0:T(8,128)(2,1)} %param.9, bf16[128,256]{1,0:T(8,128)(2,1)} %param.10), kind=kOutput, calls=%fused_computation | convolution fusion | flops 50692096 | bytes 527360 | tf_op jit(solution)/shard_map/dot_general | solution.py:141
  3.4 13.9 %all-to-all-start = ((bf16[24,32,256]{2,1,0:T(8,128)(2,1)}), bf16[24,32,256]{2,1,0:T(8,128)(2,1)S(1)}, u32[]{:S(2)}, u32[]{:S(2)}) async-start(bf16[24,32,256]{2,1,0:T(8,128)(2,1)} %convolution_convert_fusion), calls=%async_computation | async-start | bytes 786432 | tf_op jit(solution)/shard_map/all_to_all | solution.py:144
  18.0 0.0 copy-start.1
  18.0 1.9 %copy-done.1 = bf16[1,96,128,128]{3,2,1,0:T(8,128)(2,1)S(1)} copy-done((bf16[1,96,128,128]{3,2,1,0:T(8,128)(2,1)S(1)}, bf16[1,96,128,128]{3,2,1,0:T(8,128)(2,1)}, u32[]{:S(2)}) %copy-start.1) | copy-done | bytes 3145752
  19.9 0.0 copy-start.2
  19.9 1.6 %copy-done.2 = bf16[4096,256]{1,0:T(8,128)(2,1)S(1)} copy-done((bf16[4096,256]{1,0:T(8,128)(2,1)S(1)}, bf16[4096,256]{1,0:T(8,128)(2,1)}, u32[]{:S(2)}) %copy-start.2) | copy-done | bytes 2097176
  21.5 0.0 copy-start.4
  21.5 0.7 copy-done.4
  22.2 8.5 %shard_map.104 = (bf16[4096,768]{1,0:T(8,128)(2,1)}, bf16[256,768]{1,0:T(8,128)(2,1)S(1)}) custom-call(s32[96]{0:T(128)S(1)} %bitcast.16, s32[1]{0:T(128)S(6)} %copy.11.count_ref, bf16[96,128,128]{2,1,0:T(8,128)(2,1)S(1)} %bitcast.15, bf16[4096,256]{1,0:T(8,128)(2,1)S(1)} %copy-done.2), custom_call_target="tpu_custom_call" | custom-call | flops 1600000000 | bytes 24000000 | tf_op jit(solution)/shard_map/pallas_call | solution.py:146
  30.7 3.6 %all-to-all-done = bf16[24,32,256]{2,1,0:T(8,128)(2,1)S(1)} async-done(((bf16[24,32,256]{2,1,0:T(8,128)(2,1)}), bf16[24,32,256]{2,1,0:T(8,128)(2,1)S(1)}, u32[]{:S(2)}, u32[]{:S(2)}) %all-to-all-start) | async-done | bytes 393248 | tf_op jit(solution)/shard_map/all_to_all | solution.py:144
  34.3 1.0 shard_map.107
  35.3 7.6 %all-to-all-start.2 = ((bf16[24,32,256]{2,1,0:T(8,128)(2,1)}), bf16[24,32,256]{2,1,0:T(8,128)(2,1)S(1)}, u32[]{:S(2)}, u32[]{:S(2)}) async-start(bf16[24,32,256]{2,1,0:T(8,128)(2,1)} %shard_map.107), calls=%async_computation.2 | async-start | bytes 786432 | tf_op jit(solution)/shard_map/all_to_all | solution.py:171
  42.9 5.6 %shard_map.105 = (f32[16,128,256]{2,1,0:T(8,128)S(1)}, bf16[16,64,256]{2,1,0:T(8,128)(2,1)S(1)}, bf16[16,64,256]{2,1,0:T(8,128)(2,1)S(1)}) custom-call(s32[1]{0:T(128)} %bitcast.odd_ref, bf16[768,256]{1,0:T(8,128)(2,1)S(1)} %bitcast.14, bf16[4096,768]{1,0:T(8,128)(2,1)} %get-tuple-element.7.turned_ref), custom_call_target="tpu_custom_call" | custom-call | flops 1700000000 | bytes 9000000 | tf_op jit(solution)/shard_map/pallas_call | solution.py:175
  48.5 0.0 copy-start.3
  48.5 0.8 copy-done.3
  49.3 10.5 %all-to-all-done.2.terms_ref = bf16[24,32,256]{2,1,0:T(8,128)(2,1)S(1)} async-done(((bf16[24,32,256]{2,1,0:T(8,128)(2,1)}), bf16[24,32,256]{2,1,0:T(8,128)(2,1)S(1)}, u32[]{:S(2)}, u32[]{:S(2)}) %all-to-all-start.2) | async-done | bytes 393248 | tf_op jit(solution)/shard_map/all_to_all | solution.py:171
  59.8 0.9 shard_map.108
  60.7 10.0 %all-to-all-start.3 = ((bf16[32,32,256]{2,1,0:T(8,128)(2,1)}), bf16[32,32,256]{2,1,0:T(8,128)(2,1)S(1)}, u32[]{:S(2)}, u32[]{:S(2)}) async-start(bf16[32,32,256]{2,1,0:T(8,128)(2,1)} %shard_map.108), calls=%async_computation.3 | async-start | bytes 1048576 | tf_op jit(solution)/shard_map/all_to_all | solution.py:194
  70.7 4.9 %collective-permute-start.1 = (bf16[16,64,256]{2,1,0:T(8,128)(2,1)}, bf16[16,64,256]{2,1,0:T(8,128)(2,1)S(1)}, u32[]{:S(2)}, u32[]{:S(2)}) collective-permute-start(bf16[16,64,256]{2,1,0:T(8,128)(2,1)} %copy-done.3), channel_id=1, source_target_pairs={{0,3},{1,2},{2,1},{3,0},{4,7},{5,6},{6,5},{7,4},{8,11},{9,10},{10,... | collective-permute-start | bytes 1572872 | tf_op jit(solution)/shard_map/ppermute | solution.py:135
  75.6 2.2 %collective-permute-start = (bf16[16,64,256]{2,1,0:T(8,128)(2,1)S(1)}, bf16[16,64,256]{2,1,0:T(8,128)(2,1)S(1)}, u32[]{:S(2)}, u32[]{:S(2)}) collective-permute-start(bf16[16,64,256]{2,1,0:T(8,128)(2,1)S(1)} %get-tuple-element.9.after_ref), channel_id=1, source_target_pairs={{0,1},{1,0},{2,3},{3,2},{4,5},{5,4},{6,7},{7,6},{8,9},{9,8},{10,11... | collective-permute-start | bytes 1572872 | tf_op jit(solution)/shard_map/ppermute | solution.py:135
  77.8 15.5 %collective-permute-done.1.far_ref = bf16[16,64,256]{2,1,0:T(8,128)(2,1)S(1)} collective-permute-done((bf16[16,64,256]{2,1,0:T(8,128)(2,1)}, bf16[16,64,256]{2,1,0:T(8,128)(2,1)S(1)}, u32[]{:S(2)}, u32[]{:S(2)}) %collective-permute-start.1) | collective-permute-done | bytes 524320 | tf_op jit(solution)/shard_map/ppermute | solution.py:135
  93.3 1.1 collective-permute-done.near_ref
  94.4 1.2 shard_map.106
  95.5 0.0 all-to-all-done.3
  95.6 0.0 copy-start.5
  95.6 0.8 copy-done.5
  96.4 7.5 %all-to-all-start.1 = ((bf16[16,128,256]{2,1,0:T(8,128)(2,1)}), bf16[16,128,256]{2,1,0:T(8,128)(2,1)S(1)}, u32[]{:S(2)}, u32[]{:S(2)}) async-start(bf16[16,128,256]{2,1,0:T(8,128)(2,1)} %shard_map.106), calls=%async_computation.1 | async-start | bytes 2097152 | tf_op jit(solution)/shard_map/all_to_all | solution.py:204
  103.9 1.1 convert_reduce_fusion.own_ref
  105.0 1.9 %collective-permute-start.2 = (f32[32,256]{1,0:T(8,128)S(1)}, f32[32,256]{1,0:T(8,128)S(1)}, u32[]{:S(2)}, u32[]{:S(2)}) collective-permute-start(f32[32,256]{1,0:T(8,128)S(1)} %convert_reduce_fusion.own_ref), channel_id=1, source_target_pairs={{0,32},{32,0},{64,96},{96,64},{128,160},{160,128},{192,224},{224,1... | collective-permute-start | bytes 98312 | tf_op jit(solution)/shard_map/ppermute | solution.py:135
  106.9 1.2 collective-permute-done.2.one_ref
  108.1 3.6 %collective-permute-start.3 = (f32[64,256]{1,0:T(8,128)S(1)}, f32[64,256]{1,0:T(8,128)S(1)}, u32[]{:S(2)}, u32[]{:S(2)}) collective-permute-start(f32[64,256]{1,0:T(8,128)S(1)} %pad_maximum_fusion.1), channel_id=1, source_target_pairs={{0,64},{32,96},{64,0},{96,32},{128,192},{160,224},{192,128},{224,1... | collective-permute-start | bytes 196616 | tf_op jit(solution)/shard_map/ppermute | solution.py:135
  111.7 2.6 %collective-permute-done.3.two_ref = f32[64,256]{1,0:T(8,128)S(1)} collective-permute-done((f32[64,256]{1,0:T(8,128)S(1)}, f32[64,256]{1,0:T(8,128)S(1)}, u32[]{:S(2)}, u32[]{:S(2)}) %collective-permute-start.3) | collective-permute-done | bytes 65568 | tf_op jit(solution)/shard_map/ppermute | solution.py:135
  114.3 2.3 %collective-permute-start.4 = (f32[128,256]{1,0:T(8,128)S(1)}, f32[128,256]{1,0:T(8,128)S(1)}, u32[]{:S(2)}, u32[]{:S(2)}) collective-permute-start(f32[128,256]{1,0:T(8,128)S(1)} %pad_maximum_fusion), channel_id=1, source_target_pairs={{0,128},{32,160},{64,192},{96,224},{128,0},{160,32},{192,64},{224,... | collective-permute-start | bytes 393224 | tf_op jit(solution)/shard_map/ppermute | solution.py:135
  116.6 5.5 %collective-permute-done.4.four_ref = f32[128,256]{1,0:T(8,128)S(1)} collective-permute-done((f32[128,256]{1,0:T(8,128)S(1)}, f32[128,256]{1,0:T(8,128)S(1)}, u32[]{:S(2)}, u32[]{:S(2)}) %collective-permute-start.4) | collective-permute-done | bytes 131104 | tf_op jit(solution)/shard_map/ppermute | solution.py:135
  122.0 0.7 shard_map.109
  122.8 11.6 %all-to-all-done.1 = bf16[16,128,256]{2,1,0:T(8,128)(2,1)S(1)} async-done(((bf16[16,128,256]{2,1,0:T(8,128)(2,1)}), bf16[16,128,256]{2,1,0:T(8,128)(2,1)S(1)}, u32[]{:S(2)}, u32[]{:S(2)}) %all-to-all-start.1) | async-done | bytes 1048608 | tf_op jit(solution)/shard_map/all_to_all | solution.py:204
  134.4 0.1 reduce_sum.21
  134.5 0.0 copy-done
  134.5 0.8 convolution_convert_fusion.1
  (2 shorter events, 0.0 us)
Async XLA Ops:
  0.6 133.9 %copy-start = (bf16[256,256]{1,0:T(8,128)(2,1)S(1)}, bf16[256,256]{1,0:T(8,128)(2,1)}, u32[]{:S(2)}) copy-start(bf16[256,256]{1,0:T(8,128)(2,1)} %param.12) | copy-start | bytes 393220
  3.4 30.8 %all-to-all-start = ((bf16[24,32,256]{2,1,0:T(8,128)(2,1)}), bf16[24,32,256]{2,1,0:T(8,128)(2,1)S(1)}, u32[]{:S(2)}, u32[]{:S(2)}) async-start(bf16[24,32,256]{2,1,0:T(8,128)(2,1)} %convolution_convert_fusion), calls=%async_computation | async-start | bytes 786432 | tf_op jit(solution)/shard_map/all_to_all | solution.py:144
  18.0 1.9 %copy-start.1 = (bf16[1,96,128,128]{3,2,1,0:T(8,128)(2,1)S(1)}, bf16[1,96,128,128]{3,2,1,0:T(8,128)(2,1)}, u32[]{:S(2)}) copy-start(bf16[1,96,128,128]{3,2,1,0:T(8,128)(2,1)} %param.17) | copy-start | bytes 9437188
  19.9 1.6 %copy-start.2 = (bf16[4096,256]{1,0:T(8,128)(2,1)S(1)}, bf16[4096,256]{1,0:T(8,128)(2,1)}, u32[]{:S(2)}) copy-start(bf16[4096,256]{1,0:T(8,128)(2,1)} %features_ref.1) | copy-start | bytes 6291460
  21.5 0.7 copy-start.4
  35.3 24.5 %all-to-all-start.2 = ((bf16[24,32,256]{2,1,0:T(8,128)(2,1)}), bf16[24,32,256]{2,1,0:T(8,128)(2,1)S(1)}, u32[]{:S(2)}, u32[]{:S(2)}) async-start(bf16[24,32,256]{2,1,0:T(8,128)(2,1)} %shard_map.107), calls=%async_computation.2 | async-start | bytes 786432 | tf_op jit(solution)/shard_map/all_to_all | solution.py:171
  48.5 0.8 copy-start.3
  60.7 34.8 %all-to-all-start.3 = ((bf16[32,32,256]{2,1,0:T(8,128)(2,1)}), bf16[32,32,256]{2,1,0:T(8,128)(2,1)S(1)}, u32[]{:S(2)}, u32[]{:S(2)}) async-start(bf16[32,32,256]{2,1,0:T(8,128)(2,1)} %shard_map.108), calls=%async_computation.3 | async-start | bytes 1048576 | tf_op jit(solution)/shard_map/all_to_all | solution.py:194
  70.7 22.6 %collective-permute-start.1 = (bf16[16,64,256]{2,1,0:T(8,128)(2,1)}, bf16[16,64,256]{2,1,0:T(8,128)(2,1)S(1)}, u32[]{:S(2)}, u32[]{:S(2)}) collective-permute-start(bf16[16,64,256]{2,1,0:T(8,128)(2,1)} %copy-done.3), channel_id=1, source_target_pairs={{0,3},{1,2},{2,1},{3,0},{4,7},{5,6},{6,5},{7,4},{8,11},{9,10},{10,... | collective-permute-start | bytes 1572872 | tf_op jit(solution)/shard_map/ppermute | solution.py:135
  75.6 18.8 %collective-permute-start = (bf16[16,64,256]{2,1,0:T(8,128)(2,1)S(1)}, bf16[16,64,256]{2,1,0:T(8,128)(2,1)S(1)}, u32[]{:S(2)}, u32[]{:S(2)}) collective-permute-start(bf16[16,64,256]{2,1,0:T(8,128)(2,1)S(1)} %get-tuple-element.9.after_ref), channel_id=1, source_target_pairs={{0,1},{1,0},{2,3},{3,2},{4,5},{5,4},{6,7},{7,6},{8,9},{9,8},{10,11... | collective-permute-start | bytes 1572872 | tf_op jit(solution)/shard_map/ppermute | solution.py:135
  95.6 0.8 copy-start.5
  96.4 38.0 %all-to-all-start.1 = ((bf16[16,128,256]{2,1,0:T(8,128)(2,1)}), bf16[16,128,256]{2,1,0:T(8,128)(2,1)S(1)}, u32[]{:S(2)}, u32[]{:S(2)}) async-start(bf16[16,128,256]{2,1,0:T(8,128)(2,1)} %shard_map.106), calls=%async_computation.1 | async-start | bytes 2097152 | tf_op jit(solution)/shard_map/all_to_all | solution.py:204
  105.0 3.1 %collective-permute-start.2 = (f32[32,256]{1,0:T(8,128)S(1)}, f32[32,256]{1,0:T(8,128)S(1)}, u32[]{:S(2)}, u32[]{:S(2)}) collective-permute-start(f32[32,256]{1,0:T(8,128)S(1)} %convert_reduce_fusion.own_ref), channel_id=1, source_target_pairs={{0,32},{32,0},{64,96},{96,64},{128,160},{160,128},{192,224},{224,1... | collective-permute-start | bytes 98312 | tf_op jit(solution)/shard_map/ppermute | solution.py:135
  108.1 6.1 %collective-permute-start.3 = (f32[64,256]{1,0:T(8,128)S(1)}, f32[64,256]{1,0:T(8,128)S(1)}, u32[]{:S(2)}, u32[]{:S(2)}) collective-permute-start(f32[64,256]{1,0:T(8,128)S(1)} %pad_maximum_fusion.1), channel_id=1, source_target_pairs={{0,64},{32,96},{64,0},{96,32},{128,192},{160,224},{192,128},{224,1... | collective-permute-start | bytes 196616 | tf_op jit(solution)/shard_map/ppermute | solution.py:135
  114.3 7.8 %collective-permute-start.4 = (f32[128,256]{1,0:T(8,128)S(1)}, f32[128,256]{1,0:T(8,128)S(1)}, u32[]{:S(2)}, u32[]{:S(2)}) collective-permute-start(f32[128,256]{1,0:T(8,128)S(1)} %pad_maximum_fusion), channel_id=1, source_target_pairs={{0,128},{32,160},{64,192},{96,224},{128,0},{160,32},{192,64},{224,... | collective-permute-start | bytes 393224 | tf_op jit(solution)/shard_map/ppermute | solution.py:135

commit v6 on v5

--- a/solution.py
+++ b/solution.py
@@ -9,7 +9,8 @@
 
 VMEM_BYTES = 24000000
 SLICES = 8
-PAIRS = 4
+RING = 4
+GROUPS = 2
 SMEM = pl.BlockSpec(memory_space=pltpu.SMEM)
 VMEM = pl.BlockSpec(memory_space=pltpu.VMEM)
 HBM = pl.BlockSpec(memory_space=pltpu.HBM)
@@ -69,39 +70,50 @@
         out_ref[p] = total
 
 
-def products(odd_ref, rows_ref, turned_ref, keep_ref, near_ref, far_ref, turned, sems):
-    blocks, size, _ = keep_ref.shape
+def products(place_ref, rows_ref, turned_ref, keep_ref, up_ref, down_ref, next_ref, last_ref, turned, sems):
+    groups, size, _ = keep_ref.shape
     half = size // 2
-    odd = odd_ref[0]
+    place = place_ref[0]
     copies = []
-    for g in range(blocks):
-        span = pl.ds(2 * g * size, 2 * size)
+    for g in range(groups):
+        span = pl.ds(RING * g * size, RING * size)
         copies.append(pltpu.make_async_copy(turned_ref.at[span], turned.at[span], sems.at[g]))
         copies[-1].start()
-    for first in range(0, blocks, PAIRS):
+    for first in range(0, groups, GROUPS):
         taken = []
-        for g in range(first, first + PAIRS):
+        for g in range(first, first + GROUPS):
             copies[g].wait()
-            for c in (2 * g + odd, 2 * g + 1 - odd):
+            for ahead in range(RING):
+                c = RING * g + ((place + ahead) & (RING - 1))
                 taken.append(turned[pl.ds(pl.multiple_of(c * size, size), size), :])
         part = jnp.dot(jnp.concatenate(taken, axis=0), rows_ref[...], preferred_element_type=jnp.float32)
-        for i in range(PAIRS):
-            kept, sent = part[2 * i * size : (2 * i + 1) * size], part[(2 * i + 1) * size : (2 * i + 2) * size]
-            keep_ref[first + i] = kept
-            near_ref[first + i] = sent[:half].astype(near_ref.dtype)
-            far_ref[first + i] = sent[half:].astype(far_ref.dtype)
-
-
-def add_partners(keep_ref, near_ref, far_ref, out_ref):
-    blocks, size, _ = keep_ref.shape
+        for i in range(GROUPS):
+            own, one, two, three = [part[(RING * i + j) * size : (RING * i + j + 1) * size] for j in range(RING)]
+            g = first + i
+            keep_ref[g] = own
+            up_ref[g] = two[:half].astype(up_ref.dtype)
+            up_ref[groups + g] = one[half:].astype(up_ref.dtype)
+            down_ref[g] = two[half:].astype(down_ref.dtype)
+            down_ref[groups + g] = three[:half].astype(down_ref.dtype)
+            next_ref[g] = one[:half]
+            last_ref[g] = three[half:]
+
+
+def relay(next_ref, last_ref, up_ref, down_ref, next_out_ref, last_out_ref):
+    groups = next_ref.shape[0]
+    for g in range(groups):
+        next_out_ref[g] = (next_ref[g] + up_ref[g].astype(jnp.float32)).astype(next_out_ref.dtype)
+        last_out_ref[g] = (last_ref[g] + down_ref[g].astype(jnp.float32)).astype(last_out_ref.dtype)
+
+
+def add_ring(keep_ref, up_ref, down_ref, next_ref, last_ref, out_ref):
+    groups, size, _ = keep_ref.shape
     half = size // 2
-
-    def block(g, carry):
-        out_ref[g, :half] = (keep_ref[g, :half] + near_ref[g].astype(jnp.float32)).astype(out_ref.dtype)
-        out_ref[g, half:size] = (keep_ref[g, half:] + far_ref[g].astype(jnp.float32)).astype(out_ref.dtype)
-        return carry
-
-    lax.fori_loop(0, blocks, block, 0, unroll=2)
+    for g in range(groups):
+        low = keep_ref[g, :half] + down_ref[groups + g].astype(jnp.float32) + next_ref[g].astype(jnp.float32)
+        high = keep_ref[g, half:] + up_ref[groups + g].astype(jnp.float32) + last_ref[g].astype(jnp.float32)
+        out_ref[g, :half] = low.astype(out_ref.dtype)
+        out_ref[g, half:] = high.astype(out_ref.dtype)
 
 
 def put_in_order(place_ref, own_ref, one_ref, two_ref, four_ref, out_ref):
@@ -126,13 +138,16 @@
     total_rows = n_rows * per_peer
     row_blocks = total_rows // size
     depth = width // SLICES
-    blocks = col_blocks // 2
-    groups = [list(range(odd, n_rep, 2)) for odd in (0, 1)]
+    columns = col_blocks // RING
+    groups = [list(range(x, n_rep, RING)) for x in range(RING)]
     exchange = functools.partial(lax.all_to_all, split_axis=0, concat_axis=0, tiled=True)
     params = pltpu.CompilerParams(vmem_limit_bytes=VMEM_BYTES)
 
     def swapped(value, mask, axis="rep"):
         return lax.ppermute(value, axis, [(i, i ^ mask) for i in range(lax.axis_size(axis))])
+
+    def passed(value, step):
+        return lax.ppermute(value, "rep", [(i, i - i % RING + (i + step) % RING) for i in range(n_rep)])
 
     grad_pre = jnp.where(pre_relu > 0, out_grad, jnp.zeros_like(out_grad))
     slot_iota = jnp.arange(per_peer, dtype=jnp.int32)
@@ -170,37 +185,47 @@
     )(mixed, received)
     terms = exchange(term, "rows")
 
-    odd = (lax.axis_index("rep") % 2).astype(jnp.int32)[None]
-    half = jax.ShapeDtypeStruct((blocks, size // 2, width), jnp.bfloat16)
-    keep, near, far = pl.pallas_call(
+    place = (lax.axis_index("rep") % RING).astype(jnp.int32)[None]
+    full = jax.ShapeDtypeStruct((columns, size, width), jnp.float32)
+    half = jax.ShapeDtypeStruct((columns, size // 2, width), jnp.float32)
+    half_out = jax.ShapeDtypeStruct((columns, size // 2, width), jnp.bfloat16)
+    sent = jax.ShapeDtypeStruct((2 * columns, size // 2, width), jnp.bfloat16)
+    keep, up, down, ahead, behind = pl.pallas_call(
         products,
-        out_shape=(jax.ShapeDtypeStruct((blocks, size, width), jnp.float32), half, half),
+        out_shape=(full, sent, sent, half, half),
         in_specs=[SMEM, VMEM, HBM],
-        out_specs=(VMEM, VMEM, VMEM),
+        out_specs=(VMEM,) * 5,
         scratch_shapes=[
             pltpu.VMEM((col_blocks * size, total_rows), jnp.bfloat16),
-            pltpu.SemaphoreType.DMA((blocks,)),
+            pltpu.SemaphoreType.DMA((columns,)),
         ],
         compiler_params=params,
         cost_estimate=pl.CostEstimate(flops=1700000000, bytes_accessed=9000000, transcendentals=0),
-    )(odd, received, pltpu.with_memory_space_constraint(turned, pltpu.HBM))
+    )(place, received, pltpu.with_memory_space_constraint(turned, pltpu.HBM))
+    up, down = passed(up, 1), passed(down, -1)
+    ahead, behind = pl.pallas_call(
+        relay,
+        out_shape=(half_out, half_out),
+        in_specs=[VMEM] * 4,
+        out_specs=(VMEM, VMEM),
+        compiler_params=params,
+    )(ahead, behind, up, down)
     share = pl.pallas_call(
         spread_sum,
         out_shape=jax.ShapeDtypeStruct((n_rep, depth, width), jnp.bfloat16),
         in_specs=[VMEM, pl.BlockSpec(memory_space=pl.ANY)],
         out_specs=VMEM,
         compiler_params=params,
-    )(terms, near)
+    )(terms, ahead)
     own = jnp.sum(exchange(share, "rep").astype(jnp.float32), axis=0)
-    near, far = swapped(near, 1), swapped(far, 3)
-
+    ahead, behind = passed(ahead, 1), passed(behind, -1)
     parts = pl.pallas_call(
-        add_partners,
-        out_shape=jax.ShapeDtypeStruct((blocks, size, width), jnp.bfloat16),
-        in_specs=[VMEM, VMEM, VMEM],
-        out_specs=VMEM,
-        compiler_params=params,
-    )(keep, near, far)
+        add_ring,
+        out_shape=jax.ShapeDtypeStruct((columns, size, width), jnp.bfloat16),
+        in_specs=[VMEM] * 5,
+        out_specs=VMEM,
+        compiler_params=params,
+    )(keep, up, down, ahead, behind)
     parts = exchange(parts, "rep", axis_index_groups=groups)
 
     one = swapped(own, 1, "rows")

time: 136 us -> 131 us (0.963)
  the two profiles are of different devices: /device:TPU:128 before, /device:TPU:1 now
where the time goes in v6:
time: 131 us; the launch traced here: 129 us
  starting transfers between devices  62.1 us (47%)
  waiting for transfers between devices  38.4 us (29%)
  Pallas kernels  17.7 us (14%)
  local copies, waits for them, and re-layouts  4.14 us (3%)
  matrix products  2.79 us (2%)
  other arithmetic  2.03 us (2%)
  between operations  1.47 us (1%)
    ppermute x4, waiting for transfers between devices, passed(): lax.ppermute(value, 'rep', [(i, i - i % RING + (i + step) % RING) for i i...  22.8 us
    all_to_all x1, starting transfers between devices, per_device(): received = exchange(outgoing, 'rows').reshape(total_rows, width)  16.7 us
    ppermute x4, starting transfers between devices, passed(): lax.ppermute(value, 'rep', [(i, i - i % RING + (i + step) % RING) for i i...  12.7 us
    ppermute x3, starting transfers between devices, swapped(): lax.ppermute(value, axis, [(i, i ^ mask) for i in range(lax.axis_size(axi...  11.2 us
    all_to_all x1, starting transfers between devices, per_device(): own = jnp.sum(exchange(share, 'rep').astype(jnp.float32), axis=0)  9.73 us
    pallas_call x1, Pallas kernels, per_device(): pl.pallas_call(place_tiles, out_shape=(pltpu.HBM((col_blocks * size, tota...  8.57 us
    all_to_all x1, waiting for transfers between devices, per_device(): parts = exchange(parts, 'rep', axis_index_groups=groups)  6.76 us
    all_to_all x1, starting transfers between devices, per_device(): terms = exchange(term, 'rows')  6.22 us
  transfers between devices with their start and end apart: 11, of which 8 were waited for; matrix products, arithmetic and copies ran while one was open for 2% of the time, Pallas kernels for 12%

profile of v6, /device:TPU:1, one launch (start us, length us, event | category | flops | bytes accessed | tf_op | source)
XLA Modules:
  0.0 128.6 jit_solution(2549942161367830250)
XLA Ops:
  0.6 0.0 copy-start
  0.6 0.8 bitcast_select_fusion
  1.5 2.0 %convolution_convert_fusion = bf16[24,32,256]{2,1,0:T(8,128)(2,1)} fusion(s32[24,32]{1,0:T(8,128)S(1)} %bitcast_select_fusion, bf16[128,256]{1,0:T(8,128)(2,1)} %param.9, bf16[128,256]{1,0:T(8,128)(2,1)} %param.10), kind=kOutput, calls=%fused_computation | convolution fusion | flops 50692096 | bytes 527360 | tf_op jit(solution)/shard_map/dot_general | solution.py:156
  3.4 16.7 %all-to-all-start = ((bf16[24,32,256]{2,1,0:T(8,128)(2,1)}), bf16[24,32,256]{2,1,0:T(8,128)(2,1)S(1)}, u32[]{:S(2)}, u32[]{:S(2)}) async-start(bf16[24,32,256]{2,1,0:T(8,128)(2,1)} %convolution_convert_fusion), calls=%async_computation | async-start | bytes 786432 | tf_op jit(solution)/shard_map/all_to_all | solution.py:159
  20.8 0.0 copy-start.1
  20.8 1.9 %copy-done.1 = bf16[1,96,128,128]{3,2,1,0:T(8,128)(2,1)S(1)} copy-done((bf16[1,96,128,128]{3,2,1,0:T(8,128)(2,1)S(1)}, bf16[1,96,128,128]{3,2,1,0:T(8,128)(2,1)}, u32[]{:S(2)}) %copy-start.1) | copy-done | bytes 3145752
  22.7 0.0 copy-start.2
  22.7 1.6 %copy-done.2 = bf16[4096,256]{1,0:T(8,128)(2,1)S(1)} copy-done((bf16[4096,256]{1,0:T(8,128)(2,1)S(1)}, bf16[4096,256]{1,0:T(8,128)(2,1)}, u32[]{:S(2)}) %copy-start.2) | copy-done | bytes 2097176
  24.2 0.0 copy-start.3
  24.2 0.7 copy-done.3
  24.9 8.6 %shard_map.104 = (bf16[4096,768]{1,0:T(8,128)(2,1)}, bf16[256,768]{1,0:T(8,128)(2,1)S(1)}) custom-call(s32[96]{0:T(128)S(1)} %bitcast.16, s32[1]{0:T(128)S(6)} %copy.11.count_ref, bf16[96,128,128]{2,1,0:T(8,128)(2,1)S(1)} %bitcast.15, bf16[4096,256]{1,0:T(8,128)(2,1)S(1)} %copy-done.2), custom_call_target="tpu_custom_call" | custom-call | flops 1600000000 | bytes 24000000 | tf_op jit(solution)/shard_map/pallas_call | solution.py:161
  33.5 4.9 %all-to-all-done = bf16[24,32,256]{2,1,0:T(8,128)(2,1)S(1)} async-done(((bf16[24,32,256]{2,1,0:T(8,128)(2,1)}), bf16[24,32,256]{2,1,0:T(8,128)(2,1)S(1)}, u32[]{:S(2)}, u32[]{:S(2)}) %all-to-all-start) | async-done | bytes 393248 | tf_op jit(solution)/shard_map/all_to_all | solution.py:159
  38.3 1.0 shard_map.108
  39.4 6.2 %all-to-all-start.2 = ((bf16[24,32,256]{2,1,0:T(8,128)(2,1)}), bf16[24,32,256]{2,1,0:T(8,128)(2,1)S(1)}, u32[]{:S(2)}, u32[]{:S(2)}) async-start(bf16[24,32,256]{2,1,0:T(8,128)(2,1)} %shard_map.108), calls=%async_computation.2 | async-start | bytes 786432 | tf_op jit(solution)/shard_map/all_to_all | solution.py:186
  45.6 5.5 %shard_map.105 = (f32[8,128,256]{2,1,0:T(8,128)S(1)}, bf16[16,64,256]{2,1,0:T(8,128)(2,1)S(1)}, bf16[16,64,256]{2,1,0:T(8,128)(2,1)S(1)}, f32[8,64,256]{2,1,0:T(8,128)S(1)}, f32[8,64,256]{2,1,0:T(8,128)S(1)}) custom-call(s32[1]{0:T(128)} %bitcast.place_ref, bf16[768,256]{1,0:T(8,128)(2,1)S(1)} %bitcast.14, bf16[4096,768]{1,0:T(8,128)(2,1)} %get-tuple-element.11.turned_ref), custom_call_target="tpu_custom_call" | custom-call | flops 1700000000 | bytes 9000000 | tf_op jit(solution)/shard_map/pallas_call | solution.py:193
  51.1 3.1 %collective-permute-start = (bf16[16,64,256]{2,1,0:T(8,128)(2,1)S(1)}, bf16[16,64,256]{2,1,0:T(8,128)(2,1)S(1)}, u32[]{:S(2)}, u32[]{:S(2)}) collective-permute-start(bf16[16,64,256]{2,1,0:T(8,128)(2,1)S(1)} %get-tuple-element.13), channel_id=1, source_target_pairs={{0,1},{1,2},{2,3},{3,0},{4,5},{5,6},{6,7},{7,4},{8,9},{9,10},{10,1... | collective-permute-start | bytes 1572872 | tf_op jit(solution)/shard_map/ppermute | solution.py:150
  54.2 3.4 %collective-permute-start.1 = (bf16[16,64,256]{2,1,0:T(8,128)(2,1)S(1)}, bf16[16,64,256]{2,1,0:T(8,128)(2,1)S(1)}, u32[]{:S(2)}, u32[]{:S(2)}) collective-permute-start(bf16[16,64,256]{2,1,0:T(8,128)(2,1)S(1)} %get-tuple-element.14), channel_id=1, source_target_pairs={{0,3},{1,0},{2,1},{3,2},{4,7},{5,4},{6,5},{7,6},{8,11},{9,8},{10,9... | collective-permute-start | bytes 1572872 | tf_op jit(solution)/shard_map/ppermute | solution.py:150
  57.6 9.8 %collective-permute-done.up_ref = bf16[16,64,256]{2,1,0:T(8,128)(2,1)S(1)} collective-permute-done((bf16[16,64,256]{2,1,0:T(8,128)(2,1)S(1)}, bf16[16,64,256]{2,1,0:T(8,128)(2,1)S(1)}, u32[]{:S(2)}, u32[]{:S(2)}) %collective-permute-start) | collective-permute-done | bytes 524320 | tf_op jit(solution)/shard_map/ppermute | solution.py:150
  67.4 1.6 %collective-permute-done.1.down_ref = bf16[16,64,256]{2,1,0:T(8,128)(2,1)S(1)} collective-permute-done((bf16[16,64,256]{2,1,0:T(8,128)(2,1)S(1)}, bf16[16,64,256]{2,1,0:T(8,128)(2,1)S(1)}, u32[]{:S(2)}, u32[]{:S(2)}) %collective-permute-start.1) | collective-permute-done | bytes 524320 | tf_op jit(solution)/shard_map/ppermute | solution.py:150
  69.0 0.1 shard_map.106
  69.1 0.0 all-to-all-done.2.terms_ref
  69.1 0.9 shard_map.109
  70.0 9.7 %all-to-all-start.3 = ((bf16[32,32,256]{2,1,0:T(8,128)(2,1)}), bf16[32,32,256]{2,1,0:T(8,128)(2,1)}, u32[]{:S(2)}, u32[]{:S(2)}) async-start(bf16[32,32,256]{2,1,0:T(8,128)(2,1)} %shard_map.109), calls=%async_computation.3 | async-start | bytes 1048576 | tf_op jit(solution)/shard_map/all_to_all | solution.py:220
  79.8 4.3 %collective-permute-start.3 = (bf16[8,64,256]{2,1,0:T(8,128)(2,1)S(1)}, bf16[8,64,256]{2,1,0:T(8,128)(2,1)S(1)}, u32[]{:S(2)}, u32[]{:S(2)}) collective-permute-start(bf16[8,64,256]{2,1,0:T(8,128)(2,1)S(1)} %get-tuple-element.18), channel_id=1, source_target_pairs={{0,3},{1,0},{2,1},{3,2},{4,7},{5,4},{6,5},{7,6},{8,11},{9,8},{10,9... | collective-permute-start | bytes 786440 | tf_op jit(solution)/shard_map/ppermute | solution.py:150
  84.1 1.9 %collective-permute-start.2 = (bf16[8,64,256]{2,1,0:T(8,128)(2,1)S(1)}, bf16[8,64,256]{2,1,0:T(8,128)(2,1)S(1)}, u32[]{:S(2)}, u32[]{:S(2)}) collective-permute-start(bf16[8,64,256]{2,1,0:T(8,128)(2,1)S(1)} %get-tuple-element.17.after_ref), channel_id=1, source_target_pairs={{0,1},{1,2},{2,3},{3,0},{4,5},{5,6},{6,7},{7,4},{8,9},{9,10},{10,1... | collective-permute-start | bytes 786440 | tf_op jit(solution)/shard_map/ppermute | solution.py:150
  86.0 6.9 %collective-permute-done.3.last_ref = bf16[8,64,256]{2,1,0:T(8,128)(2,1)S(1)} collective-permute-done((bf16[8,64,256]{2,1,0:T(8,128)(2,1)S(1)}, bf16[8,64,256]{2,1,0:T(8,128)(2,1)S(1)}, u32[]{:S(2)}, u32[]{:S(2)}) %collective-permute-start.3) | collective-permute-done | bytes 262176 | tf_op jit(solution)/shard_map/ppermute | solution.py:150
  92.9 4.5 %collective-permute-done.2.next_ref = bf16[8,64,256]{2,1,0:T(8,128)(2,1)S(1)} collective-permute-done((bf16[8,64,256]{2,1,0:T(8,128)(2,1)S(1)}, bf16[8,64,256]{2,1,0:T(8,128)(2,1)S(1)}, u32[]{:S(2)}, u32[]{:S(2)}) %collective-permute-start.2) | collective-permute-done | bytes 262176 | tf_op jit(solution)/shard_map/ppermute | solution.py:150
  97.4 0.9 shard_map.107
  98.3 0.0 all-to-all-done.3
  98.3 5.6 %all-to-all-start.1 = ((bf16[8,128,256]{2,1,0:T(8,128)(2,1)}), bf16[8,128,256]{2,1,0:T(8,128)(2,1)S(1)}, u32[]{:S(2)}, u32[]{:S(2)}) async-start(bf16[8,128,256]{2,1,0:T(8,128)(2,1)} %shard_map.107), calls=%async_computation.1 | async-start | bytes 1048576 | tf_op jit(solution)/shard_map/all_to_all | solution.py:229
  104.0 1.1 convert_reduce_fusion.own_ref
  105.1 3.8 %collective-permute-start.4 = (f32[32,256]{1,0:T(8,128)S(1)}, f32[32,256]{1,0:T(8,128)S(1)}, u32[]{:S(2)}, u32[]{:S(2)}) collective-permute-start(f32[32,256]{1,0:T(8,128)S(1)} %convert_reduce_fusion.own_ref), channel_id=1, source_target_pairs={{0,32},{32,0},{64,96},{96,64},{128,160},{160,128},{192,224},{224,1... | collective-permute-start | bytes 98312 | tf_op jit(solution)/shard_map/ppermute | solution.py:147
  108.9 0.8 collective-permute-done.4.one_ref
  109.8 3.2 %collective-permute-start.5 = (f32[64,256]{1,0:T(8,128)S(1)}, f32[64,256]{1,0:T(8,128)S(1)}, u32[]{:S(2)}, u32[]{:S(2)}) collective-permute-start(f32[64,256]{1,0:T(8,128)S(1)} %pad_maximum_fusion.1), channel_id=1, source_target_pairs={{0,64},{32,96},{64,0},{96,32},{128,192},{160,224},{192,128},{224,1... | collective-permute-start | bytes 196616 | tf_op jit(solution)/shard_map/ppermute | solution.py:147
  113.0 6.8 %all-to-all-done.1 = bf16[8,128,256]{2,1,0:T(8,128)(2,1)S(1)} async-done(((bf16[8,128,256]{2,1,0:T(8,128)(2,1)}), bf16[8,128,256]{2,1,0:T(8,128)(2,1)S(1)}, u32[]{:S(2)}, u32[]{:S(2)}) %all-to-all-start.1) | async-done | bytes 524320 | tf_op jit(solution)/shard_map/all_to_all | solution.py:229
  119.8 0.1 reduce_sum.21
  119.9 0.0 collective-permute-done.5.two_ref
  119.9 4.1 %collective-permute-start.6 = (f32[128,256]{1,0:T(8,128)S(1)}, f32[128,256]{1,0:T(8,128)S(1)}, u32[]{:S(2)}, u32[]{:S(2)}) collective-permute-start(f32[128,256]{1,0:T(8,128)S(1)} %pad_maximum_fusion), channel_id=1, source_target_pairs={{0,128},{32,160},{64,192},{96,224},{128,0},{160,32},{192,64},{224,... | collective-permute-start | bytes 393224 | tf_op jit(solution)/shard_map/ppermute | solution.py:147
  124.0 0.0 copy-done
  124.0 0.8 convolution_convert_fusion.1
  124.9 3.1 %collective-permute-done.6.four_ref = f32[128,256]{1,0:T(8,128)S(1)} collective-permute-done((f32[128,256]{1,0:T(8,128)S(1)}, f32[128,256]{1,0:T(8,128)S(1)}, u32[]{:S(2)}, u32[]{:S(2)}) %collective-permute-start.6) | collective-permute-done | bytes 131104 | tf_op jit(solution)/shard_map/ppermute | solution.py:147
  127.9 0.7 shard_map.110
  (2 shorter events, 0.0 us)
Async XLA Ops:
  0.6 123.4 %copy-start = (bf16[256,256]{1,0:T(8,128)(2,1)S(1)}, bf16[256,256]{1,0:T(8,128)(2,1)}, u32[]{:S(2)}) copy-start(bf16[256,256]{1,0:T(8,128)(2,1)} %param.12) | copy-start | bytes 393220
  3.4 34.9 %all-to-all-start = ((bf16[24,32,256]{2,1,0:T(8,128)(2,1)}), bf16[24,32,256]{2,1,0:T(8,128)(2,1)S(1)}, u32[]{:S(2)}, u32[]{:S(2)}) async-start(bf16[24,32,256]{2,1,0:T(8,128)(2,1)} %convolution_convert_fusion), calls=%async_computation | async-start | bytes 786432 | tf_op jit(solution)/shard_map/all_to_all | solution.py:159
  20.8 1.9 %copy-start.1 = (bf16[1,96,128,128]{3,2,1,0:T(8,128)(2,1)S(1)}, bf16[1,96,128,128]{3,2,1,0:T(8,128)(2,1)}, u32[]{:S(2)}) copy-start(bf16[1,96,128,128]{3,2,1,0:T(8,128)(2,1)} %param.17) | copy-start | bytes 9437188
  22.7 1.6 %copy-start.2 = (bf16[4096,256]{1,0:T(8,128)(2,1)S(1)}, bf16[4096,256]{1,0:T(8,128)(2,1)}, u32[]{:S(2)}) copy-start(bf16[4096,256]{1,0:T(8,128)(2,1)} %features_ref.1) | copy-start | bytes 6291460
  24.2 0.7 copy-start.3
  39.4 29.7 %all-to-all-start.2 = ((bf16[24,32,256]{2,1,0:T(8,128)(2,1)}), bf16[24,32,256]{2,1,0:T(8,128)(2,1)S(1)}, u32[]{:S(2)}, u32[]{:S(2)}) async-start(bf16[24,32,256]{2,1,0:T(8,128)(2,1)} %shard_map.108), calls=%async_computation.2 | async-start | bytes 786432 | tf_op jit(solution)/shard_map/all_to_all | solution.py:186
  51.1 16.3 %collective-permute-start = (bf16[16,64,256]{2,1,0:T(8,128)(2,1)S(1)}, bf16[16,64,256]{2,1,0:T(8,128)(2,1)S(1)}, u32[]{:S(2)}, u32[]{:S(2)}) collective-permute-start(bf16[16,64,256]{2,1,0:T(8,128)(2,1)S(1)} %get-tuple-element.13), channel_id=1, source_target_pairs={{0,1},{1,2},{2,3},{3,0},{4,5},{5,6},{6,7},{7,4},{8,9},{9,10},{10,1... | collective-permute-start | bytes 1572872 | tf_op jit(solution)/shard_map/ppermute | solution.py:150
  54.2 14.8 %collective-permute-start.1 = (bf16[16,64,256]{2,1,0:T(8,128)(2,1)S(1)}, bf16[16,64,256]{2,1,0:T(8,128)(2,1)S(1)}, u32[]{:S(2)}, u32[]{:S(2)}) collective-permute-start(bf16[16,64,256]{2,1,0:T(8,128)(2,1)S(1)} %get-tuple-element.14), channel_id=1, source_target_pairs={{0,3},{1,0},{2,1},{3,2},{4,7},{5,4},{6,5},{7,6},{8,11},{9,8},{10,9... | collective-permute-start | bytes 1572872 | tf_op jit(solution)/shard_map/ppermute | solution.py:150
  70.0 28.3 %all-to-all-start.3 = ((bf16[32,32,256]{2,1,0:T(8,128)(2,1)}), bf16[32,32,256]{2,1,0:T(8,128)(2,1)}, u32[]{:S(2)}, u32[]{:S(2)}) async-start(bf16[32,32,256]{2,1,0:T(8,128)(2,1)} %shard_map.109), calls=%async_computation.3 | async-start | bytes 1048576 | tf_op jit(solution)/shard_map/all_to_all | solution.py:220
  79.8 13.1 %collective-permute-start.3 = (bf16[8,64,256]{2,1,0:T(8,128)(2,1)S(1)}, bf16[8,64,256]{2,1,0:T(8,128)(2,1)S(1)}, u32[]{:S(2)}, u32[]{:S(2)}) collective-permute-start(bf16[8,64,256]{2,1,0:T(8,128)(2,1)S(1)} %get-tuple-element.18), channel_id=1, source_target_pairs={{0,3},{1,0},{2,1},{3,2},{4,7},{5,4},{6,5},{7,6},{8,11},{9,8},{10,9... | collective-permute-start | bytes 786440 | tf_op jit(solution)/shard_map/ppermute | solution.py:150
  84.1 13.3 %collective-permute-start.2 = (bf16[8,64,256]{2,1,0:T(8,128)(2,1)S(1)}, bf16[8,64,256]{2,1,0:T(8,128)(2,1)S(1)}, u32[]{:S(2)}, u32[]{:S(2)}) collective-permute-start(bf16[8,64,256]{2,1,0:T(8,128)(2,1)S(1)} %get-tuple-element.17.after_ref), channel_id=1, source_target_pairs={{0,1},{1,2},{2,3},{3,0},{4,5},{5,6},{6,7},{7,4},{8,9},{9,10},{10,1... | collective-permute-start | bytes 786440 | tf_op jit(solution)/shard_map/ppermute | solution.py:150
  98.3 21.5 %all-to-all-start.1 = ((bf16[8,128,256]{2,1,0:T(8,128)(2,1)}), bf16[8,128,256]{2,1,0:T(8,128)(2,1)S(1)}, u32[]{:S(2)}, u32[]{:S(2)}) async-start(bf16[8,128,256]{2,1,0:T(8,128)(2,1)} %shard_map.107), calls=%async_computation.1 | async-start | bytes 1048576 | tf_op jit(solution)/shard_map/all_to_all | solution.py:229
  105.1 4.7 %collective-permute-start.4 = (f32[32,256]{1,0:T(8,128)S(1)}, f32[32,256]{1,0:T(8,128)S(1)}, u32[]{:S(2)}, u32[]{:S(2)}) collective-permute-start(f32[32,256]{1,0:T(8,128)S(1)} %convert_reduce_fusion.own_ref), channel_id=1, source_target_pairs={{0,32},{32,0},{64,96},{96,64},{128,160},{160,128},{192,224},{224,1... | collective-permute-start | bytes 98312 | tf_op jit(solution)/shard_map/ppermute | solution.py:147
  109.8 10.1 %collective-permute-start.5 = (f32[64,256]{1,0:T(8,128)S(1)}, f32[64,256]{1,0:T(8,128)S(1)}, u32[]{:S(2)}, u32[]{:S(2)}) collective-permute-start(f32[64,256]{1,0:T(8,128)S(1)} %pad_maximum_fusion.1), channel_id=1, source_target_pairs={{0,64},{32,96},{64,0},{96,32},{128,192},{160,224},{192,128},{224,1... | collective-permute-start | bytes 196616 | tf_op jit(solution)/shard_map/ppermute | solution.py:147
  119.9 8.0 %collective-permute-start.6 = (f32[128,256]{1,0:T(8,128)S(1)}, f32[128,256]{1,0:T(8,128)S(1)}, u32[]{:S(2)}, u32[]{:S(2)}) collective-permute-start(f32[128,256]{1,0:T(8,128)S(1)} %pad_maximum_fusion), channel_id=1, source_target_pairs={{0,128},{32,160},{64,192},{96,224},{128,0},{160,32},{192,64},{224,... | collective-permute-start | bytes 393224 | tf_op jit(solution)/shard_map/ppermute | solution.py:147

commit v7 on v6

--- a/solution.py
+++ b/solution.py
@@ -8,12 +8,30 @@
 from jax.sharding import PartitionSpec as P
 
 VMEM_BYTES = 24000000
+PICK_VMEM_BYTES = 60000000
 SLICES = 8
 RING = 4
 GROUPS = 2
 SMEM = pl.BlockSpec(memory_space=pltpu.SMEM)
 VMEM = pl.BlockSpec(memory_space=pltpu.VMEM)
 HBM = pl.BlockSpec(memory_space=pltpu.HBM)
+
+
+def pick_rows(count_ref, out_grad_ref, pre_relu_ref, send_rows_ref, out_ref):
+    peers, slots = send_rows_ref.shape
+    nodes = out_grad_ref.shape[0]
+    grad_pre = jnp.where(pre_relu_ref[...] > 0, out_grad_ref[...], jnp.zeros_like(out_grad_ref))
+    slot = lax.broadcasted_iota(jnp.int32, (1, slots), 1)
+    node = lax.broadcasted_iota(jnp.int32, (nodes, nodes), 0)
+    together = nodes // slots
+    for first in range(0, peers, together):
+        wanted = [
+            jnp.where(slot < count_ref[q], send_rows_ref[q : q + 1, :], -1) for q in range(first, first + together)
+        ]
+        picks = jnp.where(node == jnp.concatenate(wanted, axis=1), 1.0, 0.0).astype(jnp.bfloat16)
+        out_ref[first * slots : (first + together) * slots] = lax.dot_general(
+            picks, grad_pre, (((0,), (0,)), ((), ())), preferred_element_type=jnp.float32
+        ).astype(out_ref.dtype)
 
 
 def place_tiles(index_ref, count_ref, tiles_ref, features_ref, turned_ref, mixed_ref, dense, turned, total, sem):
@@ -70,7 +88,9 @@
         out_ref[p] = total
 
 
-def products(place_ref, rows_ref, turned_ref, keep_ref, up_ref, down_ref, next_ref, last_ref, turned, sems):
+def products(
+    place_ref, rows_ref, turned_ref, keep_ref, up_ref, down_ref, up_two_ref, down_two_ref, next_ref, last_ref, turned, sems
+):
     groups, size, _ = keep_ref.shape
     half = size // 2
     place = place_ref[0]
@@ -91,10 +111,10 @@
             own, one, two, three = [part[(RING * i + j) * size : (RING * i + j + 1) * size] for j in range(RING)]
             g = first + i
             keep_ref[g] = own
-            up_ref[g] = two[:half].astype(up_ref.dtype)
-            up_ref[groups + g] = one[half:].astype(up_ref.dtype)
-            down_ref[g] = two[half:].astype(down_ref.dtype)
-            down_ref[groups + g] = three[:half].astype(down_ref.dtype)
+            up_two_ref[g] = two[:half].astype(up_ref.dtype)
+            up_ref[g] = one[half:].astype(up_ref.dtype)
+            down_two_ref[g] = two[half:].astype(down_ref.dtype)
+            down_ref[g] = three[:half].astype(down_ref.dtype)
             next_ref[g] = one[:half]
             last_ref[g] = three[half:]
 
@@ -110,20 +130,26 @@
     groups, size, _ = keep_ref.shape
     half = size // 2
     for g in range(groups):
-        low = keep_ref[g, :half] + down_ref[groups + g].astype(jnp.float32) + next_ref[g].astype(jnp.float32)
-        high = keep_ref[g, half:] + up_ref[groups + g].astype(jnp.float32) + last_ref[g].astype(jnp.float32)
+        low = keep_ref[g, :half] + down_ref[g].astype(jnp.float32) + next_ref[g].astype(jnp.float32)
+        high = keep_ref[g, half:] + up_ref[g].astype(jnp.float32) + last_ref[g].astype(jnp.float32)
         out_ref[g, :half] = low.astype(out_ref.dtype)
         out_ref[g, half:] = high.astype(out_ref.dtype)
 
 
-def put_in_order(place_ref, own_ref, one_ref, two_ref, four_ref, out_ref):
+def finish(place_ref, parts_ref, weight_ref, own_ref, one_ref, two_ref, four_ref, feature_grad_ref, weight_grad_ref):
+    grads = parts_ref[0].astype(jnp.float32)
+    for y in range(1, parts_ref.shape[0]):
+        grads += parts_ref[y].astype(jnp.float32)
+    feature_grad_ref[...] = lax.dot_general(
+        grads.astype(jnp.bfloat16), weight_ref[...], (((1,), (1,)), ((), ())), preferred_element_type=jnp.float32
+    ).astype(feature_grad_ref.dtype)
     depth = own_ref.shape[0]
     pieces = [own_ref[...], one_ref[...]]
     pieces += [two_ref[i * depth : (i + 1) * depth] for i in range(2)]
     pieces += [four_ref[i * depth : (i + 1) * depth] for i in range(4)]
     for j, piece in enumerate(pieces):
         first = pl.multiple_of((place_ref[0] ^ j) * depth, depth)
-        out_ref[pl.ds(first, depth), :] = piece
+        weight_grad_ref[pl.ds(first, depth), :] = piece
 
 
 def per_device(
@@ -149,14 +175,14 @@
     def passed(value, step):
         return lax.ppermute(value, "rep", [(i, i - i % RING + (i + step) % RING) for i in range(n_rep)])
 
-    grad_pre = jnp.where(pre_relu > 0, out_grad, jnp.zeros_like(out_grad))
-    slot_iota = jnp.arange(per_peer, dtype=jnp.int32)
-    wanted = jnp.where(slot_iota[None, :] < send_count[0][:, None], send_rows[0], -1)
-    picks = (wanted[:, :, None] == jnp.arange(node_dev, dtype=jnp.int32)).astype(jnp.bfloat16)
-    outgoing = lax.dot_general(
-        picks, grad_pre, (((2,), (0,)), ((), ())), preferred_element_type=jnp.float32
-    ).astype(jnp.bfloat16)
-    received = exchange(outgoing, "rows").reshape(total_rows, width)
+    outgoing = pl.pallas_call(
+        pick_rows,
+        out_shape=jax.ShapeDtypeStruct((total_rows, width), jnp.bfloat16),
+        in_specs=[SMEM, VMEM, VMEM, VMEM],
+        out_specs=VMEM,
+        compiler_params=pltpu.CompilerParams(vmem_limit_bytes=PICK_VMEM_BYTES),
+    )(send_count[0], out_grad, pre_relu, send_rows[0])
+    received = exchange(outgoing.reshape(n_rows, per_peer, width), "rows").reshape(total_rows, width)
 
     turned, mixed = pl.pallas_call(
         place_tiles,
@@ -189,12 +215,11 @@
     full = jax.ShapeDtypeStruct((columns, size, width), jnp.float32)
     half = jax.ShapeDtypeStruct((columns, size // 2, width), jnp.float32)
     half_out = jax.ShapeDtypeStruct((columns, size // 2, width), jnp.bfloat16)
-    sent = jax.ShapeDtypeStruct((2 * columns, size // 2, width), jnp.bfloat16)
-    keep, up, down, ahead, behind = pl.pallas_call(
+    keep, up, down, up_two, down_two, ahead, behind = pl.pallas_call(
         products,
-        out_shape=(full, sent, sent, half, half),
+        out_shape=(full, half_out, half_out, half_out, half_out, half, half),
         in_specs=[SMEM, VMEM, HBM],
-        out_specs=(VMEM,) * 5,
+        out_specs=(VMEM,) * 7,
         scratch_shapes=[
             pltpu.VMEM((col_blocks * size, total_rows), jnp.bfloat16),
             pltpu.SemaphoreType.DMA((columns,)),
@@ -202,14 +227,14 @@
         compiler_params=params,
         cost_estimate=pl.CostEstimate(flops=1700000000, bytes_accessed=9000000, transcendentals=0),
     )(place, received, pltpu.with_memory_space_constraint(turned, pltpu.HBM))
-    up, down = passed(up, 1), passed(down, -1)
+    up_two, down_two = passed(up_two, 1), passed(down_two, -1)
     ahead, behind = pl.pallas_call(
         relay,
         out_shape=(half_out, half_out),
         in_specs=[VMEM] * 4,
         out_specs=(VMEM, VMEM),
         compiler_params=params,
-    )(ahead, behind, up, down)
+    )(ahead, behind, up_two, down_two)
     share = pl.pallas_call(
         spread_sum,
         out_shape=jax.ShapeDtypeStruct((n_rep, depth, width), jnp.bfloat16),
@@ -219,6 +244,7 @@
     )(terms, ahead)
     own = jnp.sum(exchange(share, "rep").astype(jnp.float32), axis=0)
     ahead, behind = passed(ahead, 1), passed(behind, -1)
+    up, down = passed(up, 1), passed(down, -1)
     parts = pl.pallas_call(
         add_ring,
         out_shape=jax.ShapeDtypeStruct((columns, size, width), jnp.bfloat16),
@@ -231,22 +257,16 @@
     one = swapped(own, 1, "rows")
     two = swapped(jnp.concatenate([own, one], axis=0), 2, "rows")
     four = swapped(jnp.concatenate([own, one, two], axis=0), 4, "rows")
-    weight_grad = pl.pallas_call(
-        put_in_order,
-        out_shape=jax.ShapeDtypeStruct((width, width), jnp.float32),
-        in_specs=[SMEM, VMEM, VMEM, VMEM, VMEM],
-        out_specs=VMEM,
-        compiler_params=params,
-    )((lax.axis_index("rows") % SLICES).astype(jnp.int32)[None], own, one, two, four)
-
-    grads = jnp.sum(parts.astype(jnp.float32), axis=0)
-    feature_grad = lax.dot_general(
-        grads.astype(jnp.bfloat16),
-        weight,
-        (((1,), (1,)), ((), ())),
-        preferred_element_type=jnp.float32,
-    ).astype(jnp.bfloat16)
-    return (feature_grad, weight_grad)
+    return pl.pallas_call(
+        finish,
+        out_shape=(
+            jax.ShapeDtypeStruct((node_dev, width), jnp.bfloat16),
+            jax.ShapeDtypeStruct((width, width), jnp.float32),
+        ),
+        in_specs=[SMEM] + [VMEM] * 6,
+        out_specs=(VMEM, VMEM),
+        compiler_params=params,
+    )((lax.axis_index("rows") % SLICES).astype(jnp.int32)[None], parts, weight, own, one, two, four)
 
 
 def solution(mesh):

time: 131 us -> 125 us (0.954); the launches traced: 129 us -> 125 us
  waiting for transfers between devices: 38.4 us -> 31.3 us
  starting transfers between devices: 62.1 us -> 67.7 us
  matrix products: 2.79 us -> 0 us
  Pallas kernels: 17.7 us -> 19.9 us
  other arithmetic: 2.03 us -> 0.1 us
    ppermute x4 -> x6, waiting for transfers between devices: 22.8 us -> 14.3 us  [passed(): lax.ppermute(value, 'rep', [(i, i - i % RING + (i + step) % RING) for i i...]
    ppermute x3, waiting for transfers between devices: 3.91 us -> 11.8 us  [swapped(): lax.ppermute(value, axis, [(i, i ^ mask) for i in range(lax.axis_size(axi...]
    all_to_all x1, waiting for transfers between devices: 6.76 us -> 0.01 us  [per_device(): parts = exchange(parts, 'rep', axis_index_groups=groups)]
    ppermute x4 -> x6, starting transfers between devices: 12.7 us -> 18.3 us  [passed(): lax.ppermute(value, 'rep', [(i, i - i % RING + (i + step) % RING) for i i...]
    dot_general x2 -> x0, matrix products: 2.79 us -> none  [the longest x1 1.95 us: per_device(): lax.dot_general(picks, grad_pre, (((2,), (0,)), ((), ())), preferred_elem...]
    pallas_call x2 -> x3, Pallas kernels: 6.17 us -> 8.32 us  [the longest x1 5.45 us: per_device(): pl.pallas_call(products, out_shape=(full, half_out, half_out, half_out, h...]
  transfers between devices with their start and end apart: 11 -> 13, of which waited for: 8 -> 10; matrix products, arithmetic and copies ran while one was open for 2% -> 0% of each run, Pallas kernels for 12% -> 12%
where the time goes in v7:
time: 125 us
  starting transfers between devices  67.7 us (54%)
  waiting for transfers between devices  31.3 us (25%)
  Pallas kernels  19.9 us (16%)
  local copies, waits for them, and re-layouts  4.13 us (3%)
  between operations  1.45 us (1%)
    ppermute x6, starting transfers between devices, passed(): lax.ppermute(value, 'rep', [(i, i - i % RING + (i + step) % RING) for i i...  18.3 us
    all_to_all x1, starting transfers between devices, per_device(): exchange(outgoing.reshape(n_rows, per_peer, width), 'rows')  16.7 us
    ppermute x6, waiting for transfers between devices, passed(): lax.ppermute(value, 'rep', [(i, i - i % RING + (i + step) % RING) for i i...  14.3 us
    ppermute x3, starting transfers between devices, swapped(): lax.ppermute(value, axis, [(i, i ^ mask) for i in range(lax.axis_size(axi...  12.1 us
    ppermute x3, waiting for transfers between devices, swapped(): lax.ppermute(value, axis, [(i, i ^ mask) for i in range(lax.axis_size(axi...  11.8 us
    all_to_all x1, starting transfers between devices, per_device(): own = jnp.sum(exchange(share, 'rep').astype(jnp.float32), axis=0)  9.81 us
    pallas_call x1, Pallas kernels, per_device(): pl.pallas_call(place_tiles, out_shape=(pltpu.HBM((col_blocks * size, tota...  8.59 us
    all_to_all x1, starting transfers between devices, per_device(): terms = exchange(term, 'rows')  6.22 us
  transfers between devices with their start and end apart: 13, of which 10 were waited for; matrix products, arithmetic and copies ran while one was open for 0% of the time, Pallas kernels for 12%

profile of v7, /device:TPU:1, one launch (start us, length us, event | category | flops | bytes accessed | tf_op | source)
XLA Modules:
  0.0 124.5 jit_solution(10679582970847629063)
XLA Ops:
  0.6 2.0 %shard_map.104 = bf16[768,256]{1,0:T(8,128)(2,1)} custom-call(s32[24]{0:T(128)} %bitcast.14, bf16[128,256]{1,0:T(8,128)(2,1)} %out_grad_ref.1, bf16[128,256]{1,0:T(8,128)(2,1)} %pre_relu_ref.1, s32[24,32]{1,0:T(8,128)} %bitcast.13), custom_call_target="tpu_custom_call" | custom-call | tf_op jit(solution)/shard_map/pallas_call | solution.py:178
  2.7 16.7 %all-to-all-start = ((bf16[24,32,256]{2,1,0:T(8,128)(2,1)}), bf16[24,32,256]{2,1,0:T(8,128)(2,1)S(1)}, u32[]{:S(2)}, u32[]{:S(2)}) async-start(bf16[24,32,256]{2,1,0:T(8,128)(2,1)} %bitcast.12), calls=%async_computation | async-start | bytes 786432 | tf_op jit(solution)/shard_map/all_to_all | solution.py:185
  20.0 0.0 copy-start.1
  20.0 1.9 %copy-done.1 = bf16[1,96,128,128]{3,2,1,0:T(8,128)(2,1)S(1)} copy-done((bf16[1,96,128,128]{3,2,1,0:T(8,128)(2,1)S(1)}, bf16[1,96,128,128]{3,2,1,0:T(8,128)(2,1)}, u32[]{:S(2)}) %copy-start.1) | copy-done | bytes 3145752
  21.9 0.0 copy-start.2
  21.9 1.6 %copy-done.2 = bf16[4096,256]{1,0:T(8,128)(2,1)S(1)} copy-done((bf16[4096,256]{1,0:T(8,128)(2,1)S(1)}, bf16[4096,256]{1,0:T(8,128)(2,1)}, u32[]{:S(2)}) %copy-start.2) | copy-done | bytes 2097176
  23.5 0.0 copy-start.3
  23.5 0.7 copy-done.3
  24.1 8.6 %shard_map.105 = (bf16[4096,768]{1,0:T(8,128)(2,1)}, bf16[256,768]{1,0:T(8,128)(2,1)S(1)}) custom-call(s32[96]{0:T(128)S(1)} %bitcast.11, s32[1]{0:T(128)S(6)} %copy.11.count_ref, bf16[96,128,128]{2,1,0:T(8,128)(2,1)S(1)} %bitcast.10, bf16[4096,256]{1,0:T(8,128)(2,1)S(1)} %copy-done.2), custom_call_target="tpu_custom_call" | custom-call | flops 1600000000 | bytes 24000000 | tf_op jit(solution)/shard_map/pallas_call | solution.py:187
  32.7 4.8 %all-to-all-done = bf16[24,32,256]{2,1,0:T(8,128)(2,1)S(1)} async-done(((bf16[24,32,256]{2,1,0:T(8,128)(2,1)}), bf16[24,32,256]{2,1,0:T(8,128)(2,1)S(1)}, u32[]{:S(2)}, u32[]{:S(2)}) %all-to-all-start) | async-done | bytes 393248 | tf_op jit(solution)/shard_map/all_to_all | solution.py:185
  37.6 1.0 shard_map.109
  38.6 6.2 %all-to-all-start.2 = ((bf16[24,32,256]{2,1,0:T(8,128)(2,1)}), bf16[24,32,256]{2,1,0:T(8,128)(2,1)S(1)}, u32[]{:S(2)}, u32[]{:S(2)}) async-start(bf16[24,32,256]{2,1,0:T(8,128)(2,1)} %shard_map.109), calls=%async_computation.2 | async-start | bytes 786432 | tf_op jit(solution)/shard_map/all_to_all | solution.py:212
  44.8 5.5 %shard_map.106 = (f32[8,128,256]{2,1,0:T(8,128)S(1)}, bf16[8,64,256]{2,1,0:T(8,128)(2,1)S(1)}, bf16[8,64,256]{2,1,0:T(8,128)(2,1)S(1)}, bf16[8,64,256]{2,1,0:T(8...) custom-call(s32[1]{0:T(128)} %bitcast.1.place_ref, ...), custom_call_target="tpu_custom_call" | custom-call | flops 1700000000 | bytes 9000000 | tf_op jit(solution)/shard_map/pallas_call | solution.py:218
  50.3 3.1 %collective-permute-start.2 = (bf16[8,64,256]{2,1,0:T(8,128)(2,1)S(1)}, bf16[8,64,256]{2,1,0:T(8,128)(2,1)S(1)}, u32[]{:S(2)}, u32[]{:S(2)}) collective-permute-start(bf16[8,64,256]{2,1,0:T(8,128)(2,1)S(1)} %get-tuple-element.19), channel_id=1, source_target_pairs={{0,1},{1,2},{2,3},{3,0},{4,5},{5,6},{6,7},{7,4},{8,9},{9,10},{10,1... | collective-permute-start | bytes 786440 | tf_op jit(solution)/shard_map/ppermute | solution.py:176
  53.4 3.4 %collective-permute-start.3 = (bf16[8,64,256]{2,1,0:T(8,128)(2,1)S(1)}, bf16[8,64,256]{2,1,0:T(8,128)(2,1)S(1)}, u32[]{:S(2)}, u32[]{:S(2)}) collective-permute-start(bf16[8,64,256]{2,1,0:T(8,128)(2,1)S(1)} %get-tuple-element.20), channel_id=1, source_target_pairs={{0,3},{1,0},{2,1},{3,2},{4,7},{5,4},{6,5},{7,6},{8,11},{9,8},{10,9... | collective-permute-start | bytes 786440 | tf_op jit(solution)/shard_map/ppermute | solution.py:176
  56.8 4.2 %collective-permute-done.2.up_ref = bf16[8,64,256]{2,1,0:T(8,128)(2,1)S(1)} collective-permute-done((bf16[8,64,256]{2,1,0:T(8,128)(2,1)S(1)}, bf16[8,64,256]{2,1,0:T(8,128)(2,1)S(1)}, u32[]{:S(2)}, u32[]{:S(2)}) %collective-permute-start.2) | collective-permute-done | bytes 262176 | tf_op jit(solution)/shard_map/ppermute | solution.py:176
  61.0 1.6 %collective-permute-done.3.down_ref = bf16[8,64,256]{2,1,0:T(8,128)(2,1)S(1)} collective-permute-done((bf16[8,64,256]{2,1,0:T(8,128)(2,1)S(1)}, bf16[8,64,256]{2,1,0:T(8,128)(2,1)S(1)}, u32[]{:S(2)}, u32[]{:S(2)}) %collective-permute-start.3) | collective-permute-done | bytes 262176 | tf_op jit(solution)/shard_map/ppermute | solution.py:176
  62.6 0.1 shard_map.107
  62.7 0.3 all-to-all-done.2.terms_ref
  63.0 0.9 shard_map.110
  63.9 0.0 copy-start
  63.9 9.8 %all-to-all-start.3 = ((bf16[32,32,256]{2,1,0:T(8,128)(2,1)}), bf16[32,32,256]{2,1,0:T(8,128)(2,1)S(1)}, u32[]{:S(2)}, u32[]{:S(2)}) async-start(bf16[32,32,256]{2,1,0:T(8,128)(2,1)} %shard_map.110), calls=%async_computation.3 | async-start | bytes 1048576 | tf_op jit(solution)/shard_map/all_to_all | solution.py:245
  73.7 3.1 %collective-permute-start = (bf16[8,64,256]{2,1,0:T(8,128)(2,1)S(1)}, bf16[8,64,256]{2,1,0:T(8,128)(2,1)S(1)}, u32[]{:S(2)}, u32[]{:S(2)}) collective-permute-start(bf16[8,64,256]{2,1,0:T(8,128)(2,1)S(1)} %get-tuple-element.15), channel_id=1, source_target_pairs={{0,1},{1,2},{2,3},{3,0},{4,5},{5,6},{6,7},{7,4},{8,9},{9,10},{10,1... | collective-permute-start | bytes 786440 | tf_op jit(solution)/shard_map/ppermute | solution.py:176
  76.9 3.4 %collective-permute-start.1 = (bf16[8,64,256]{2,1,0:T(8,128)(2,1)S(1)}, bf16[8,64,256]{2,1,0:T(8,128)(2,1)S(1)}, u32[]{:S(2)}, u32[]{:S(2)}) collective-permute-start(bf16[8,64,256]{2,1,0:T(8,128)(2,1)S(1)} %get-tuple-element.16), channel_id=1, source_target_pairs={{0,3},{1,0},{2,1},{3,2},{4,7},{5,4},{6,5},{7,6},{8,11},{9,8},{10,9... | collective-permute-start | bytes 786440 | tf_op jit(solution)/shard_map/ppermute | solution.py:176
  80.2 3.1 %collective-permute-start.5 = (bf16[8,64,256]{2,1,0:T(8,128)(2,1)S(1)}, bf16[8,64,256]{2,1,0:T(8,128)(2,1)S(1)}, u32[]{:S(2)}, u32[]{:S(2)}) collective-permute-start(bf16[8,64,256]{2,1,0:T(8,128)(2,1)S(1)} %get-tuple-element.22), channel_id=1, source_target_pairs={{0,3},{1,0},{2,1},{3,2},{4,7},{5,4},{6,5},{7,6},{8,11},{9,8},{10,9... | collective-permute-start | bytes 786440 | tf_op jit(solution)/shard_map/ppermute | solution.py:176
  83.4 2.1 %collective-permute-start.4 = (bf16[8,64,256]{2,1,0:T(8,128)(2,1)S(1)}, bf16[8,64,256]{2,1,0:T(8,128)(2,1)S(1)}, u32[]{:S(2)}, u32[]{:S(2)}) collective-permute-start(bf16[8,64,256]{2,1,0:T(8,128)(2,1)S(1)} %get-tuple-element.21.after_ref), channel_id=1, source_target_pairs={{0,1},{1,2},{2,3},{3,0},{4,5},{5,6},{6,7},{7,4},{8,9},{9,10},{10,1... | collective-permute-start | bytes 786440 | tf_op jit(solution)/shard_map/ppermute | solution.py:176
  85.5 1.2 collective-permute-done.up_ref
  86.8 1.3 %collective-permute-done.1.down_ref = bf16[8,64,256]{2,1,0:T(8,128)(2,1)S(1)} collective-permute-done((bf16[8,64,256]{2,1,0:T(8,128)(2,1)S(1)}, bf16[8,64,256]{2,1,0:T(8,128)(2,1)S(1)}, u32[]{:S(2)}, u32[]{:S(2)}) %collective-permute-start.1) | collective-permute-done | bytes 262176 | tf_op jit(solution)/shard_map/ppermute | solution.py:176
  88.1 6.0 %collective-permute-done.5.last_ref = bf16[8,64,256]{2,1,0:T(8,128)(2,1)S(1)} collective-permute-done((bf16[8,64,256]{2,1,0:T(8,128)(2,1)S(1)}, bf16[8,64,256]{2,1,0:T(8,128)(2,1)S(1)}, u32[]{:S(2)}, u32[]{:S(2)}) %collective-permute-start.5) | collective-permute-done | bytes 262176 | tf_op jit(solution)/shard_map/ppermute | solution.py:176
  94.1 0.0 collective-permute-done.4.next_ref
  94.1 1.0 shard_map.108
  95.0 0.0 all-to-all-done.3
  95.0 4.6 %all-to-all-start.1 = ((bf16[8,128,256]{2,1,0:T(8,128)(2,1)}), bf16[8,128,256]{2,1,0:T(8,128)(2,1)S(1)}, u32[]{:S(2)}, u32[]{:S(2)}) async-start(bf16[8,128,256]{2,1,0:T(8,128)(2,1)} %shard_map.108), calls=%async_computation.1 | async-start | bytes 1048576 | tf_op jit(solution)/shard_map/all_to_all | solution.py:255
  99.6 0.1 convert_reduce_fusion.own_ref
  99.7 7.0 %collective-permute-start.6 = (f32[32,256]{1,0:T(8,128)S(1)}, f32[32,256]{1,0:T(8,128)S(1)}, u32[]{:S(2)}, u32[]{:S(2)}) collective-permute-start(f32[32,256]{1,0:T(8,128)S(1)} %convert_reduce_fusion.own_ref), channel_id=1, source_target_pairs={{0,32},{32,0},{64,96},{96,64},{128,160},{160,128},{192,224},{224,1... | collective-permute-start | bytes 98312 | tf_op jit(solution)/shard_map/ppermute | solution.py:173
  106.7 0.8 collective-permute-done.6.one_ref
  107.5 1.9 %collective-permute-start.7 = (f32[64,256]{1,0:T(8,128)S(1)}, f32[64,256]{1,0:T(8,128)S(1)}, u32[]{:S(2)}, u32[]{:S(2)}) collective-permute-start(f32[64,256]{1,0:T(8,128)S(1)} %pad_maximum_fusion.1), channel_id=1, source_target_pairs={{0,64},{32,96},{64,0},{96,32},{128,192},{160,224},{192,128},{224,1... | collective-permute-start | bytes 196616 | tf_op jit(solution)/shard_map/ppermute | solution.py:173
  109.4 3.4 %collective-permute-done.7.two_ref = f32[64,256]{1,0:T(8,128)S(1)} collective-permute-done((f32[64,256]{1,0:T(8,128)S(1)}, f32[64,256]{1,0:T(8,128)S(1)}, u32[]{:S(2)}, u32[]{:S(2)}) %collective-permute-start.7) | collective-permute-done | bytes 65568 | tf_op jit(solution)/shard_map/ppermute | solution.py:173
  112.8 3.2 %collective-permute-start.8 = (f32[128,256]{1,0:T(8,128)S(1)}, f32[128,256]{1,0:T(8,128)S(1)}, u32[]{:S(2)}, u32[]{:S(2)}) collective-permute-start(f32[128,256]{1,0:T(8,128)S(1)} %pad_maximum_fusion), channel_id=1, source_target_pairs={{0,128},{32,160},{64,192},{96,224},{128,0},{160,32},{192,64},{224,... | collective-permute-start | bytes 393224 | tf_op jit(solution)/shard_map/ppermute | solution.py:173
  116.1 0.0 all-to-all-done.1.parts_ref
  116.1 7.6 %collective-permute-done.8.four_ref = f32[128,256]{1,0:T(8,128)S(1)} collective-permute-done((f32[128,256]{1,0:T(8,128)S(1)}, f32[128,256]{1,0:T(8,128)S(1)}, u32[]{:S(2)}, u32[]{:S(2)}) %collective-permute-start.8) | collective-permute-done | bytes 131104 | tf_op jit(solution)/shard_map/ppermute | solution.py:173
  123.7 0.0 copy-done
  123.7 0.8 shard_map.111
  (2 shorter events, 0.0 us)
Async XLA Ops:
  2.7 34.9 %all-to-all-start = ((bf16[24,32,256]{2,1,0:T(8,128)(2,1)}), bf16[24,32,256]{2,1,0:T(8,128)(2,1)S(1)}, u32[]{:S(2)}, u32[]{:S(2)}) async-start(bf16[24,32,256]{2,1,0:T(8,128)(2,1)} %bitcast.12), calls=%async_computation | async-start | bytes 786432 | tf_op jit(solution)/shard_map/all_to_all | solution.py:185
  20.0 1.9 %copy-start.1 = (bf16[1,96,128,128]{3,2,1,0:T(8,128)(2,1)S(1)}, bf16[1,96,128,128]{3,2,1,0:T(8,128)(2,1)}, u32[]{:S(2)}) copy-start(bf16[1,96,128,128]{3,2,1,0:T(8,128)(2,1)} %param.17) | copy-start | bytes 9437188
  21.9 1.6 %copy-start.2 = (bf16[4096,256]{1,0:T(8,128)(2,1)S(1)}, bf16[4096,256]{1,0:T(8,128)(2,1)}, u32[]{:S(2)}) copy-start(bf16[4096,256]{1,0:T(8,128)(2,1)} %features_ref.1) | copy-start | bytes 6291460
  23.5 0.7 copy-start.3
  38.6 24.4 %all-to-all-start.2 = ((bf16[24,32,256]{2,1,0:T(8,128)(2,1)}), bf16[24,32,256]{2,1,0:T(8,128)(2,1)S(1)}, u32[]{:S(2)}, u32[]{:S(2)}) async-start(bf16[24,32,256]{2,1,0:T(8,128)(2,1)} %shard_map.109), calls=%async_computation.2 | async-start | bytes 786432 | tf_op jit(solution)/shard_map/all_to_all | solution.py:212
  50.3 10.7 %collective-permute-start.2 = (bf16[8,64,256]{2,1,0:T(8,128)(2,1)S(1)}, bf16[8,64,256]{2,1,0:T(8,128)(2,1)S(1)}, u32[]{:S(2)}, u32[]{:S(2)}) collective-permute-start(bf16[8,64,256]{2,1,0:T(8,128)(2,1)S(1)} %get-tuple-element.19), channel_id=1, source_target_pairs={{0,1},{1,2},{2,3},{3,0},{4,5},{5,6},{6,7},{7,4},{8,9},{9,10},{10,1... | collective-permute-start | bytes 786440 | tf_op jit(solution)/shard_map/ppermute | solution.py:176
  53.4 9.2 %collective-permute-start.3 = (bf16[8,64,256]{2,1,0:T(8,128)(2,1)S(1)}, bf16[8,64,256]{2,1,0:T(8,128)(2,1)S(1)}, u32[]{:S(2)}, u32[]{:S(2)}) collective-permute-start(bf16[8,64,256]{2,1,0:T(8,128)(2,1)S(1)} %get-tuple-element.20), channel_id=1, source_target_pairs={{0,3},{1,0},{2,1},{3,2},{4,7},{5,4},{6,5},{7,6},{8,11},{9,8},{10,9... | collective-permute-start | bytes 786440 | tf_op jit(solution)/shard_map/ppermute | solution.py:176
  63.9 59.7 %copy-start = (bf16[256,256]{1,0:T(8,128)(2,1)S(1)}, bf16[256,256]{1,0:T(8,128)(2,1)}, u32[]{:S(2)}) copy-start(bf16[256,256]{1,0:T(8,128)(2,1)} %weight_ref.1) | copy-start | bytes 393220
  63.9 31.1 %all-to-all-start.3 = ((bf16[32,32,256]{2,1,0:T(8,128)(2,1)}), bf16[32,32,256]{2,1,0:T(8,128)(2,1)S(1)}, u32[]{:S(2)}, u32[]{:S(2)}) async-start(bf16[32,32,256]{2,1,0:T(8,128)(2,1)} %shard_map.110), calls=%async_computation.3 | async-start | bytes 1048576 | tf_op jit(solution)/shard_map/all_to_all | solution.py:245
  73.7 13.0 %collective-permute-start = (bf16[8,64,256]{2,1,0:T(8,128)(2,1)S(1)}, bf16[8,64,256]{2,1,0:T(8,128)(2,1)S(1)}, u32[]{:S(2)}, u32[]{:S(2)}) collective-permute-start(bf16[8,64,256]{2,1,0:T(8,128)(2,1)S(1)} %get-tuple-element.15), channel_id=1, source_target_pairs={{0,1},{1,2},{2,3},{3,0},{4,5},{5,6},{6,7},{7,4},{8,9},{9,10},{10,1... | collective-permute-start | bytes 786440 | tf_op jit(solution)/shard_map/ppermute | solution.py:176
  76.9 11.2 %collective-permute-start.1 = (bf16[8,64,256]{2,1,0:T(8,128)(2,1)S(1)}, bf16[8,64,256]{2,1,0:T(8,128)(2,1)S(1)}, u32[]{:S(2)}, u32[]{:S(2)}) collective-permute-start(bf16[8,64,256]{2,1,0:T(8,128)(2,1)S(1)} %get-tuple-element.16), channel_id=1, source_target_pairs={{0,3},{1,0},{2,1},{3,2},{4,7},{5,4},{6,5},{7,6},{8,11},{9,8},{10,9... | collective-permute-start | bytes 786440 | tf_op jit(solution)/shard_map/ppermute | solution.py:176
  80.2 13.8 %collective-permute-start.5 = (bf16[8,64,256]{2,1,0:T(8,128)(2,1)S(1)}, bf16[8,64,256]{2,1,0:T(8,128)(2,1)S(1)}, u32[]{:S(2)}, u32[]{:S(2)}) collective-permute-start(bf16[8,64,256]{2,1,0:T(8,128)(2,1)S(1)} %get-tuple-element.22), channel_id=1, source_target_pairs={{0,3},{1,0},{2,1},{3,2},{4,7},{5,4},{6,5},{7,6},{8,11},{9,8},{10,9... | collective-permute-start | bytes 786440 | tf_op jit(solution)/shard_map/ppermute | solution.py:176
  83.4 10.7 %collective-permute-start.4 = (bf16[8,64,256]{2,1,0:T(8,128)(2,1)S(1)}, bf16[8,64,256]{2,1,0:T(8,128)(2,1)S(1)}, u32[]{:S(2)}, u32[]{:S(2)}) collective-permute-start(bf16[8,64,256]{2,1,0:T(8,128)(2,1)S(1)} %get-tuple-element.21.after_ref), channel_id=1, source_target_pairs={{0,1},{1,2},{2,3},{3,0},{4,5},{5,6},{6,7},{7,4},{8,9},{9,10},{10,1... | collective-permute-start | bytes 786440 | tf_op jit(solution)/shard_map/ppermute | solution.py:176
  95.0 21.1 %all-to-all-start.1 = ((bf16[8,128,256]{2,1,0:T(8,128)(2,1)}), bf16[8,128,256]{2,1,0:T(8,128)(2,1)S(1)}, u32[]{:S(2)}, u32[]{:S(2)}) async-start(bf16[8,128,256]{2,1,0:T(8,128)(2,1)} %shard_map.108), calls=%async_computation.1 | async-start | bytes 1048576 | tf_op jit(solution)/shard_map/all_to_all | solution.py:255
  99.7 7.8 %collective-permute-start.6 = (f32[32,256]{1,0:T(8,128)S(1)}, f32[32,256]{1,0:T(8,128)S(1)}, u32[]{:S(2)}, u32[]{:S(2)}) collective-permute-start(f32[32,256]{1,0:T(8,128)S(1)} %convert_reduce_fusion.own_ref), channel_id=1, source_target_pairs={{0,32},{32,0},{64,96},{96,64},{128,160},{160,128},{192,224},{224,1... | collective-permute-start | bytes 98312 | tf_op jit(solution)/shard_map/ppermute | solution.py:173
  107.5 5.3 %collective-permute-start.7 = (f32[64,256]{1,0:T(8,128)S(1)}, f32[64,256]{1,0:T(8,128)S(1)}, u32[]{:S(2)}, u32[]{:S(2)}) collective-permute-start(f32[64,256]{1,0:T(8,128)S(1)} %pad_maximum_fusion.1), channel_id=1, source_target_pairs={{0,64},{32,96},{64,0},{96,32},{128,192},{160,224},{192,128},{224,1... | collective-permute-start | bytes 196616 | tf_op jit(solution)/shard_map/ppermute | solution.py:173
  112.8 10.9 %collective-permute-start.8 = (f32[128,256]{1,0:T(8,128)S(1)}, f32[128,256]{1,0:T(8,128)S(1)}, u32[]{:S(2)}, u32[]{:S(2)}) collective-permute-start(f32[128,256]{1,0:T(8,128)S(1)} %pad_maximum_fusion), channel_id=1, source_target_pairs={{0,128},{32,160},{64,192},{96,224},{128,0},{160,32},{192,64},{224,... | collective-permute-start | bytes 393224 | tf_op jit(solution)/shard_map/ppermute | solution.py:173

commit v8 on v7

--- a/solution.py
+++ b/solution.py
@@ -88,9 +88,7 @@
         out_ref[p] = total
 
 
-def products(
-    place_ref, rows_ref, turned_ref, keep_ref, up_ref, down_ref, up_two_ref, down_two_ref, next_ref, last_ref, turned, sems
-):
+def products(place_ref, rows_ref, turned_ref, keep_ref, up_ref, down_ref, next_ref, last_ref, turned, sems):
     groups, size, _ = keep_ref.shape
     half = size // 2
     place = place_ref[0]
@@ -111,45 +109,54 @@
             own, one, two, three = [part[(RING * i + j) * size : (RING * i + j + 1) * size] for j in range(RING)]
             g = first + i
             keep_ref[g] = own
-            up_two_ref[g] = two[:half].astype(up_ref.dtype)
-            up_ref[g] = one[half:].astype(up_ref.dtype)
-            down_two_ref[g] = two[half:].astype(down_ref.dtype)
-            down_ref[g] = three[:half].astype(down_ref.dtype)
+            up_ref[g] = two[:half].astype(up_ref.dtype)
+            down_ref[g] = two[half:].astype(down_ref.dtype)
             next_ref[g] = one[:half]
             last_ref[g] = three[half:]
-
-
-def relay(next_ref, last_ref, up_ref, down_ref, next_out_ref, last_out_ref):
-    groups = next_ref.shape[0]
+            if g < groups // 2:
+                up_ref[groups + g] = one[half:].astype(up_ref.dtype)
+                down_ref[groups + g] = three[:half].astype(down_ref.dtype)
+            else:
+                next_ref[groups // 2 + g] = one[half:]
+                last_ref[groups // 2 + g] = three[:half]
+
+
+def relay(groups, next_ref, last_ref, up_ref, down_ref, next_out_ref, last_out_ref):
     for g in range(groups):
         next_out_ref[g] = (next_ref[g] + up_ref[g].astype(jnp.float32)).astype(next_out_ref.dtype)
         last_out_ref[g] = (last_ref[g] + down_ref[g].astype(jnp.float32)).astype(last_out_ref.dtype)
+    for g in range(groups, next_ref.shape[0]):
+        next_out_ref[g] = next_ref[g].astype(next_out_ref.dtype)
+        last_out_ref[g] = last_ref[g].astype(last_out_ref.dtype)
 
 
 def add_ring(keep_ref, up_ref, down_ref, next_ref, last_ref, out_ref):
     groups, size, _ = keep_ref.shape
     half = size // 2
     for g in range(groups):
-        low = keep_ref[g, :half] + down_ref[g].astype(jnp.float32) + next_ref[g].astype(jnp.float32)
-        high = keep_ref[g, half:] + up_ref[g].astype(jnp.float32) + last_ref[g].astype(jnp.float32)
+        if g < groups // 2:
+            from_last, from_next = up_ref[groups + g], down_ref[groups + g]
+        else:
+            from_last, from_next = next_ref[groups // 2 + g], last_ref[groups // 2 + g]
+        low = keep_ref[g, :half] + from_next.astype(jnp.float32) + next_ref[g].astype(jnp.float32)
+        high = keep_ref[g, half:] + from_last.astype(jnp.float32) + last_ref[g].astype(jnp.float32)
         out_ref[g, :half] = low.astype(out_ref.dtype)
         out_ref[g, half:] = high.astype(out_ref.dtype)
 
 
-def finish(place_ref, parts_ref, weight_ref, own_ref, one_ref, two_ref, four_ref, feature_grad_ref, weight_grad_ref):
+def finish(place_ref, parts_ref, weight_ref, pair_ref, two_ref, four_ref, six_ref, feature_grad_ref, weight_grad_ref):
     grads = parts_ref[0].astype(jnp.float32)
     for y in range(1, parts_ref.shape[0]):
         grads += parts_ref[y].astype(jnp.float32)
     feature_grad_ref[...] = lax.dot_general(
         grads.astype(jnp.bfloat16), weight_ref[...], (((1,), (1,)), ((), ())), preferred_element_type=jnp.float32
     ).astype(feature_grad_ref.dtype)
-    depth = own_ref.shape[0]
-    pieces = [own_ref[...], one_ref[...]]
-    pieces += [two_ref[i * depth : (i + 1) * depth] for i in range(2)]
-    pieces += [four_ref[i * depth : (i + 1) * depth] for i in range(4)]
-    for j, piece in enumerate(pieces):
+    depth = pair_ref.shape[0] // 2
+    for j in range(SLICES):
+        piece_ref = (pair_ref, two_ref, four_ref, six_ref)[j // 2]
         first = pl.multiple_of((place_ref[0] ^ j) * depth, depth)
-        weight_grad_ref[pl.ds(first, depth), :] = piece
+        piece = piece_ref[(j % 2) * depth : (j % 2 + 1) * depth]
+        weight_grad_ref[pl.ds(first, depth), :] = piece.astype(weight_grad_ref.dtype)
 
 
 def per_device(
@@ -213,13 +220,13 @@
 
     place = (lax.axis_index("rep") % RING).astype(jnp.int32)[None]
     full = jax.ShapeDtypeStruct((columns, size, width), jnp.float32)
-    half = jax.ShapeDtypeStruct((columns, size // 2, width), jnp.float32)
-    half_out = jax.ShapeDtypeStruct((columns, size // 2, width), jnp.bfloat16)
-    keep, up, down, up_two, down_two, ahead, behind = pl.pallas_call(
+    waiting = jax.ShapeDtypeStruct((3 * columns // 2, size // 2, width), jnp.float32)
+    sent = jax.ShapeDtypeStruct((3 * columns // 2, size // 2, width), jnp.bfloat16)
+    keep, up, down, ahead, behind = pl.pallas_call(
         products,
-        out_shape=(full, half_out, half_out, half_out, half_out, half, half),
+        out_shape=(full, sent, sent, waiting, waiting),
         in_specs=[SMEM, VMEM, HBM],
-        out_specs=(VMEM,) * 7,
+        out_specs=(VMEM,) * 5,
         scratch_shapes=[
             pltpu.VMEM((col_blocks * size, total_rows), jnp.bfloat16),
             pltpu.SemaphoreType.DMA((columns,)),
@@ -227,14 +234,14 @@
         compiler_params=params,
         cost_estimate=pl.CostEstimate(flops=1700000000, bytes_accessed=9000000, transcendentals=0),
     )(place, received, pltpu.with_memory_space_constraint(turned, pltpu.HBM))
-    up_two, down_two = passed(up_two, 1), passed(down_two, -1)
+    up, down = passed(up, 1), passed(down, -1)
     ahead, behind = pl.pallas_call(
-        relay,
-        out_shape=(half_out, half_out),
+        functools.partial(relay, columns),
+        out_shape=(sent, sent),
         in_specs=[VMEM] * 4,
         out_specs=(VMEM, VMEM),
         compiler_params=params,
-    )(ahead, behind, up_two, down_two)
+    )(ahead, behind, up, down)
     share = pl.pallas_call(
         spread_sum,
         out_shape=jax.ShapeDtypeStruct((n_rep, depth, width), jnp.bfloat16),
@@ -244,7 +251,6 @@
     )(terms, ahead)
     own = jnp.sum(exchange(share, "rep").astype(jnp.float32), axis=0)
     ahead, behind = passed(ahead, 1), passed(behind, -1)
-    up, down = passed(up, 1), passed(down, -1)
     parts = pl.pallas_call(
         add_ring,
         out_shape=jax.ShapeDtypeStruct((columns, size, width), jnp.bfloat16),
@@ -254,9 +260,9 @@
     )(keep, up, down, ahead, behind)
     parts = exchange(parts, "rep", axis_index_groups=groups)
 
-    one = swapped(own, 1, "rows")
-    two = swapped(jnp.concatenate([own, one], axis=0), 2, "rows")
-    four = swapped(jnp.concatenate([own, one, two], axis=0), 4, "rows")
+    own = own.astype(jnp.bfloat16)
+    pair = jnp.concatenate([own, swapped(own, 1, "rows")], axis=0)
+    others = [swapped(pair, mask, "rows") for mask in (2, 4, 6)]
     return pl.pallas_call(
         finish,
         out_shape=(
@@ -266,7 +272,7 @@
         in_specs=[SMEM] + [VMEM] * 6,
         out_specs=(VMEM, VMEM),
         compiler_params=params,
-    )((lax.axis_index("rows") % SLICES).astype(jnp.int32)[None], parts, weight, own, one, two, four)
+    )((lax.axis_index("rows") % SLICES).astype(jnp.int32)[None], parts, weight, pair, *others)
 
 
 def solution(mesh):

time: 125 us -> 123 us (0.984)
  starting transfers between devices: 67.7 us -> 64.1 us
    ppermute x3 -> x4, waiting for transfers between devices: 11.8 us -> 3.03 us  [swapped(): lax.ppermute(value, axis, [(i, i ^ mask) for i in range(lax.axis_size(axi...]
    ppermute x6 -> x4, waiting for transfers between devices: 14.3 us -> 22.9 us  [passed(): lax.ppermute(value, 'rep', [(i, i - i % RING + (i + step) % RING) for i i...]
    ppermute x6 -> x4, starting transfers between devices: 18.3 us -> 12.7 us  [passed(): lax.ppermute(value, 'rep', [(i, i - i % RING + (i + step) % RING) for i i...]
    ppermute x3 -> x4, starting transfers between devices: 12.1 us -> 13.1 us  [swapped(): lax.ppermute(value, axis, [(i, i ^ mask) for i in range(lax.axis_size(axi...]
  transfers between devices with their start and end apart: 13 -> 12, of which waited for: 10 -> 9; matrix products, arithmetic and copies ran while one was open for 0% -> 1% of each run, Pallas kernels for 12% -> 12%
where the time goes in v8:
time: 123 us; the launch traced here: 122 us
  starting transfers between devices  64.1 us (52%)
  waiting for transfers between devices  31.6 us (26%)
  Pallas kernels  19.9 us (16%)
  local copies, waits for them, and re-layouts  4.13 us (3%)
  between operations  1.44 us (1%)
    ppermute x4, waiting for transfers between devices, passed(): lax.ppermute(value, 'rep', [(i, i - i % RING + (i + step) % RING) for i i...  22.9 us
    all_to_all x1, starting transfers between devices, per_device(): exchange(outgoing.reshape(n_rows, per_peer, width), 'rows')  16.7 us
    ppermute x4, starting transfers between devices, swapped(): lax.ppermute(value, axis, [(i, i ^ mask) for i in range(lax.axis_size(axi...  13.1 us
    ppermute x4, starting transfers between devices, passed(): lax.ppermute(value, 'rep', [(i, i - i % RING + (i + step) % RING) for i i...  12.7 us
    all_to_all x1, starting transfers between devices, per_device(): own = jnp.sum(exchange(share, 'rep').astype(jnp.float32), axis=0)  9.86 us
    pallas_call x1, Pallas kernels, per_device(): pl.pallas_call(place_tiles, out_shape=(pltpu.HBM((col_blocks * size, tota...  8.53 us
    all_to_all x1, starting transfers between devices, per_device(): terms = exchange(term, 'rows')  6.22 us
    all_to_all x1, starting transfers between devices, per_device(): parts = exchange(parts, 'rep', axis_index_groups=groups)  5.56 us
  transfers between devices with their start and end apart: 12, of which 9 were waited for; matrix products, arithmetic and copies ran while one was open for 1% of the time, Pallas kernels for 12%

profile of v8, /device:TPU:1, one launch (start us, length us, event | category | flops | bytes accessed | tf_op | source)
XLA Modules:
  0.0 122.2 jit_solution(15734023367412174145)
XLA Ops:
  0.6 2.0 %shard_map.104 = bf16[768,256]{1,0:T(8,128)(2,1)} custom-call(s32[24]{0:T(128)} %bitcast.14, bf16[128,256]{1,0:T(8,128)(2,1)} %out_grad_ref.1, bf16[128,256]{1,0:T(8,128)(2,1)} %pre_relu_ref.1, s32[24,32]{1,0:T(8,128)} %bitcast.13), custom_call_target="tpu_custom_call" | custom-call | tf_op jit(solution)/shard_map/pallas_call | solution.py:185
  2.7 16.7 %all-to-all-start = ((bf16[24,32,256]{2,1,0:T(8,128)(2,1)}), bf16[24,32,256]{2,1,0:T(8,128)(2,1)S(1)}, u32[]{:S(2)}, u32[]{:S(2)}) async-start(bf16[24,32,256]{2,1,0:T(8,128)(2,1)} %bitcast.12), calls=%async_computation | async-start | bytes 786432 | tf_op jit(solution)/shard_map/all_to_all | solution.py:192
  20.0 0.0 copy-start.1
  20.0 1.9 %copy-done.1 = bf16[1,96,128,128]{3,2,1,0:T(8,128)(2,1)S(1)} copy-done((bf16[1,96,128,128]{3,2,1,0:T(8,128)(2,1)S(1)}, bf16[1,96,128,128]{3,2,1,0:T(8,128)(2,1)}, u32[]{:S(2)}) %copy-start.1) | copy-done | bytes 3145752
  21.9 0.0 copy-start.2
  21.9 1.6 %copy-done.2 = bf16[4096,256]{1,0:T(8,128)(2,1)S(1)} copy-done((bf16[4096,256]{1,0:T(8,128)(2,1)S(1)}, bf16[4096,256]{1,0:T(8,128)(2,1)}, u32[]{:S(2)}) %copy-start.2) | copy-done | bytes 2097176
  23.5 0.0 copy-start.3
  23.5 0.7 copy-done.3
  24.2 8.5 %shard_map.105 = (bf16[4096,768]{1,0:T(8,128)(2,1)}, bf16[256,768]{1,0:T(8,128)(2,1)S(1)}) custom-call(s32[96]{0:T(128)S(1)} %bitcast.11, s32[1]{0:T(128)S(6)} %copy.11.count_ref, bf16[96,128,128]{2,1,0:T(8,128)(2,1)S(1)} %bitcast.10, bf16[4096,256]{1,0:T(8,128)(2,1)S(1)} %copy-done.2), custom_call_target="tpu_custom_call" | custom-call | flops 1600000000 | bytes 24000000 | tf_op jit(solution)/shard_map/pallas_call | solution.py:194
  32.7 4.9 %all-to-all-done = bf16[24,32,256]{2,1,0:T(8,128)(2,1)S(1)} async-done(((bf16[24,32,256]{2,1,0:T(8,128)(2,1)}), bf16[24,32,256]{2,1,0:T(8,128)(2,1)S(1)}, u32[]{:S(2)}, u32[]{:S(2)}) %all-to-all-start) | async-done | bytes 393248 | tf_op jit(solution)/shard_map/all_to_all | solution.py:192
  37.6 1.0 shard_map.109
  38.6 6.2 %all-to-all-start.2 = ((bf16[24,32,256]{2,1,0:T(8,128)(2,1)}), bf16[24,32,256]{2,1,0:T(8,128)(2,1)S(1)}, u32[]{:S(2)}, u32[]{:S(2)}) async-start(bf16[24,32,256]{2,1,0:T(8,128)(2,1)} %shard_map.109), calls=%async_computation.2 | async-start | bytes 786432 | tf_op jit(solution)/shard_map/all_to_all | solution.py:219
  44.9 5.5 %shard_map.106 = (f32[8,128,256]{2,1,0:T(8,128)S(1)}, bf16[12,64,256]{2,1,0:T(8,128)(2,1)S(1)}, bf16[12,64,256]{2,1,0:T(8,128)(2,1)S(1)}, f32[12,64,256]{2,1,0:T(8,128)S(1)}, f32[12,64,256]{2,1,0:T(8,128)S(1)}) custom-call(s32[1]{0:T(128)} %bitcast.1.place_ref, bf16[768,256]{1,0:T(8,128)(2,1)S(1)} %bitcast.9, bf16[4096,768]{1,0:T(8,128)(2,1)} %get-tuple-element.11.turned_ref), custom_call_target="tpu_custom_call" | custom-call | flops 1700000000 | bytes 9000000 | tf_op jit(solution)/shard_map/pallas_call | solution.py:225
  50.3 3.1 %collective-permute-start = (bf16[12,64,256]{2,1,0:T(8,128)(2,1)S(1)}, bf16[12,64,256]{2,1,0:T(8,128)(2,1)S(1)}, u32[]{:S(2)}, u32[]{:S(2)}) collective-permute-start(bf16[12,64,256]{2,1,0:T(8,128)(2,1)S(1)} %get-tuple-element.13), channel_id=1, source_target_pairs={{0,1},{1,2},{2,3},{3,0},{4,5},{5,6},{6,7},{7,4},{8,9},{9,10},{10,1... | collective-permute-start | bytes 1179656 | tf_op jit(solution)/shard_map/ppermute | solution.py:183
  53.4 3.4 %collective-permute-start.1 = (bf16[12,64,256]{2,1,0:T(8,128)(2,1)S(1)}, bf16[12,64,256]{2,1,0:T(8,128)(2,1)S(1)}, u32[]{:S(2)}, u32[]{:S(2)}) collective-permute-start(bf16[12,64,256]{2,1,0:T(8,128)(2,1)S(1)} %get-tuple-element.14), channel_id=1, source_target_pairs={{0,3},{1,0},{2,1},{3,2},{4,7},{5,4},{6,5},{7,6},{8,11},{9,8},{10,9... | collective-permute-start | bytes 1179656 | tf_op jit(solution)/shard_map/ppermute | solution.py:183
  56.8 7.0 %collective-permute-done.up_ref = bf16[12,64,256]{2,1,0:T(8,128)(2,1)S(1)} collective-permute-done((bf16[12,64,256]{2,1,0:T(8,128)(2,1)S(1)}, bf16[12,64,256]{2,1,0:T(8,128)(2,1)S(1)}, u32[]{:S(2)}, u32[]{:S(2)}) %collective-permute-start) | collective-permute-done | bytes 393248 | tf_op jit(solution)/shard_map/ppermute | solution.py:183
  63.8 1.6 %collective-permute-done.1.down_ref = bf16[12,64,256]{2,1,0:T(8,128)(2,1)S(1)} collective-permute-done((bf16[12,64,256]{2,1,0:T(8,128)(2,1)S(1)}, bf16[12,64,256]{2,1,0:T(8,128)(2,1)S(1)}, u32[]{:S(2)}, u32[]{:S(2)}) %collective-permute-start.1) | collective-permute-done | bytes 393248 | tf_op jit(solution)/shard_map/ppermute | solution.py:183
  65.4 0.1 shard_map.107
  65.6 0.0 all-to-all-done.2.terms_ref
  65.6 0.9 shard_map.110
  66.5 0.0 copy-start
  66.5 9.9 %all-to-all-start.3 = ((bf16[32,32,256]{2,1,0:T(8,128)(2,1)}), bf16[32,32,256]{2,1,0:T(8,128)(2,1)}, u32[]{:S(2)}, u32[]{:S(2)}) async-start(bf16[32,32,256]{2,1,0:T(8,128)(2,1)} %shard_map.110), calls=%async_computation.3 | async-start | bytes 1048576 | tf_op jit(solution)/shard_map/all_to_all | solution.py:252
  76.3 4.3 %collective-permute-start.3 = (bf16[12,64,256]{2,1,0:T(8,128)(2,1)S(1)}, bf16[12,64,256]{2,1,0:T(8,128)(2,1)S(1)}, u32[]{:S(2)}, u32[]{:S(2)}) collective-permute-start(bf16[12,64,256]{2,1,0:T(8,128)(2,1)S(1)} %get-tuple-element.18), channel_id=1, source_target_pairs={{0,3},{1,0},{2,1},{3,2},{4,7},{5,4},{6,5},{7,6},{8,11},{9,8},{10,9... | collective-permute-start | bytes 1179656 | tf_op jit(solution)/shard_map/ppermute | solution.py:183
  80.6 1.9 %collective-permute-start.2 = (bf16[12,64,256]{2,1,0:T(8,128)(2,1)S(1)}, bf16[12,64,256]{2,1,0:T(8,128)(2,1)S(1)}, u32[]{:S(2)}, u32[]{:S(2)}) collective-permute-start(bf16[12,64,256]{2,1,0:T(8,128)(2,1)S(1)} %get-tuple-element.17.after_ref), channel_id=1, source_target_pairs={{0,1},{1,2},{2,3},{3,0},{4,5},{5,6},{6,7},{7,4},{8,9},{9,10},{10,1... | collective-permute-start | bytes 1179656 | tf_op jit(solution)/shard_map/ppermute | solution.py:183
  82.6 10.8 %collective-permute-done.3.last_ref = bf16[12,64,256]{2,1,0:T(8,128)(2,1)S(1)} collective-permute-done((bf16[12,64,256]{2,1,0:T(8,128)(2,1)S(1)}, bf16[12,64,256]{2,1,0:T(8,128)(2,1)S(1)}, u32[]{:S(2)}, u32[]{:S(2)}) %collective-permute-start.3) | collective-permute-done | bytes 393248 | tf_op jit(solution)/shard_map/ppermute | solution.py:183
  93.4 3.5 %collective-permute-done.2.next_ref = bf16[12,64,256]{2,1,0:T(8,128)(2,1)S(1)} collective-permute-done((bf16[12,64,256]{2,1,0:T(8,128)(2,1)S(1)}, bf16[12,64,256]{2,1,0:T(8,128)(2,1)S(1)}, u32[]{:S(2)}, u32[]{:S(2)}) %collective-permute-start.2) | collective-permute-done | bytes 393248 | tf_op jit(solution)/shard_map/ppermute | solution.py:183
  96.8 0.9 shard_map.108
  97.8 0.0 all-to-all-done.3
  97.8 5.6 %all-to-all-start.1 = ((bf16[8,128,256]{2,1,0:T(8,128)(2,1)}), bf16[8,128,256]{2,1,0:T(8,128)(2,1)S(1)}, u32[]{:S(2)}, u32[]{:S(2)}) async-start(bf16[8,128,256]{2,1,0:T(8,128)(2,1)} %shard_map.108), calls=%async_computation.1 | async-start | bytes 1048576 | tf_op jit(solution)/shard_map/all_to_all | solution.py:261
  103.3 1.1 reduce_sum.12
  104.5 3.8 %collective-permute-start.4 = (bf16[32,256]{1,0:T(8,128)(2,1)S(1)}, bf16[32,256]{1,0:T(8,128)(2,1)S(1)}, u32[]{:S(2)}, u32[]{:S(2)}) collective-permute-start(bf16[32,256]{1,0:T(8,128)(2,1)S(1)} %reduce_sum.12), channel_id=1, source_target_pairs={{0,32},{32,0},{64,96},{96,64},{128,160},{160,128},{192,224},{224,1... | collective-permute-start | bytes 49160 | tf_op jit(solution)/shard_map/ppermute | solution.py:180
  108.3 0.8 collective-permute-done.4
  109.1 5.1 %collective-permute-start.7 = (bf16[64,256]{1,0:T(8,128)(2,1)S(1)}, bf16[64,256]{1,0:T(8,128)(2,1)S(1)}, u32[]{:S(2)}, u32[]{:S(2)}) collective-permute-start(bf16[64,256]{1,0:T(8,128)(2,1)S(1)} %pad_maximum_fusion.pair_ref), channel_id=1, source_target_pairs={{0,192},{32,224},{64,128},{96,160},{128,64},{160,96},{192,0},{224,... | collective-permute-start | bytes 98312 | tf_op jit(solution)/shard_map/ppermute | solution.py:180
  114.2 1.9 %collective-permute-start.6 = (bf16[64,256]{1,0:T(8,128)(2,1)S(1)}, bf16[64,256]{1,0:T(8,128)(2,1)S(1)}, u32[]{:S(2)}, u32[]{:S(2)}) collective-permute-start(bf16[64,256]{1,0:T(8,128)(2,1)S(1)} %pad_maximum_fusion.pair_ref), channel_id=1, source_target_pairs={{0,128},{32,160},{64,192},{96,224},{128,0},{160,32},{192,64},{224,... | collective-permute-start | bytes 98312 | tf_op jit(solution)/shard_map/ppermute | solution.py:180
  116.1 2.3 %collective-permute-start.5 = (bf16[64,256]{1,0:T(8,128)(2,1)S(1)}, bf16[64,256]{1,0:T(8,128)(2,1)S(1)}, u32[]{:S(2)}, u32[]{:S(2)}) collective-permute-start(bf16[64,256]{1,0:T(8,128)(2,1)S(1)} %pad_maximum_fusion.pair_ref), channel_id=1, source_target_pairs={{0,64},{32,96},{64,0},{96,32},{128,192},{160,224},{192,128},{224,1... | collective-permute-start | bytes 98312 | tf_op jit(solution)/shard_map/ppermute | solution.py:180
  118.4 0.8 all-to-all-done.1.parts_ref
  119.2 0.0 collective-permute-done.7.six_ref
  119.2 1.2 collective-permute-done.6.four_ref
  120.4 1.0 collective-permute-done.5.two_ref
  121.4 0.0 copy-done
  121.4 0.8 shard_map.111
  (1 shorter events, 0.0 us)
Async XLA Ops:
  2.7 34.9 %all-to-all-start = ((bf16[24,32,256]{2,1,0:T(8,128)(2,1)}), bf16[24,32,256]{2,1,0:T(8,128)(2,1)S(1)}, u32[]{:S(2)}, u32[]{:S(2)}) async-start(bf16[24,32,256]{2,1,0:T(8,128)(2,1)} %bitcast.12), calls=%async_computation | async-start | bytes 786432 | tf_op jit(solution)/shard_map/all_to_all | solution.py:192
  20.0 1.9 %copy-start.1 = (bf16[1,96,128,128]{3,2,1,0:T(8,128)(2,1)S(1)}, bf16[1,96,128,128]{3,2,1,0:T(8,128)(2,1)}, u32[]{:S(2)}) copy-start(bf16[1,96,128,128]{3,2,1,0:T(8,128)(2,1)} %param.17) | copy-start | bytes 9437188
  21.9 1.6 %copy-start.2 = (bf16[4096,256]{1,0:T(8,128)(2,1)S(1)}, bf16[4096,256]{1,0:T(8,128)(2,1)}, u32[]{:S(2)}) copy-start(bf16[4096,256]{1,0:T(8,128)(2,1)} %features_ref.1) | copy-start | bytes 6291460
  23.5 0.7 copy-start.3
  38.6 26.9 %all-to-all-start.2 = ((bf16[24,32,256]{2,1,0:T(8,128)(2,1)}), bf16[24,32,256]{2,1,0:T(8,128)(2,1)S(1)}, u32[]{:S(2)}, u32[]{:S(2)}) async-start(bf16[24,32,256]{2,1,0:T(8,128)(2,1)} %shard_map.109), calls=%async_computation.2 | async-start | bytes 786432 | tf_op jit(solution)/shard_map/all_to_all | solution.py:219
  50.3 13.5 %collective-permute-start = (bf16[12,64,256]{2,1,0:T(8,128)(2,1)S(1)}, bf16[12,64,256]{2,1,0:T(8,128)(2,1)S(1)}, u32[]{:S(2)}, u32[]{:S(2)}) collective-permute-start(bf16[12,64,256]{2,1,0:T(8,128)(2,1)S(1)} %get-tuple-element.13), channel_id=1, source_target_pairs={{0,1},{1,2},{2,3},{3,0},{4,5},{5,6},{6,7},{7,4},{8,9},{9,10},{10,1... | collective-permute-start | bytes 1179656 | tf_op jit(solution)/shard_map/ppermute | solution.py:183
  53.4 12.0 %collective-permute-start.1 = (bf16[12,64,256]{2,1,0:T(8,128)(2,1)S(1)}, bf16[12,64,256]{2,1,0:T(8,128)(2,1)S(1)}, u32[]{:S(2)}, u32[]{:S(2)}) collective-permute-start(bf16[12,64,256]{2,1,0:T(8,128)(2,1)S(1)} %get-tuple-element.14), channel_id=1, source_target_pairs={{0,3},{1,0},{2,1},{3,2},{4,7},{5,4},{6,5},{7,6},{8,11},{9,8},{10,9... | collective-permute-start | bytes 1179656 | tf_op jit(solution)/shard_map/ppermute | solution.py:183
  66.5 54.9 %copy-start = (bf16[256,256]{1,0:T(8,128)(2,1)S(1)}, bf16[256,256]{1,0:T(8,128)(2,1)}, u32[]{:S(2)}) copy-start(bf16[256,256]{1,0:T(8,128)(2,1)} %weight_ref.1) | copy-start | bytes 393220
  66.5 31.3 %all-to-all-start.3 = ((bf16[32,32,256]{2,1,0:T(8,128)(2,1)}), bf16[32,32,256]{2,1,0:T(8,128)(2,1)}, u32[]{:S(2)}, u32[]{:S(2)}) async-start(bf16[32,32,256]{2,1,0:T(8,128)(2,1)} %shard_map.110), calls=%async_computation.3 | async-start | bytes 1048576 | tf_op jit(solution)/shard_map/all_to_all | solution.py:252
  76.3 17.0 %collective-permute-start.3 = (bf16[12,64,256]{2,1,0:T(8,128)(2,1)S(1)}, bf16[12,64,256]{2,1,0:T(8,128)(2,1)S(1)}, u32[]{:S(2)}, u32[]{:S(2)}) collective-permute-start(bf16[12,64,256]{2,1,0:T(8,128)(2,1)S(1)} %get-tuple-element.18), channel_id=1, source_target_pairs={{0,3},{1,0},{2,1},{3,2},{4,7},{5,4},{6,5},{7,6},{8,11},{9,8},{10,9... | collective-permute-start | bytes 1179656 | tf_op jit(solution)/shard_map/ppermute | solution.py:183
  80.6 16.2 %collective-permute-start.2 = (bf16[12,64,256]{2,1,0:T(8,128)(2,1)S(1)}, bf16[12,64,256]{2,1,0:T(8,128)(2,1)S(1)}, u32[]{:S(2)}, u32[]{:S(2)}) collective-permute-start(bf16[12,64,256]{2,1,0:T(8,128)(2,1)S(1)} %get-tuple-element.17.after_ref), channel_id=1, source_target_pairs={{0,1},{1,2},{2,3},{3,0},{4,5},{5,6},{6,7},{7,4},{8,9},{9,10},{10,1... | collective-permute-start | bytes 1179656 | tf_op jit(solution)/shard_map/ppermute | solution.py:183
  97.8 21.4 %all-to-all-start.1 = ((bf16[8,128,256]{2,1,0:T(8,128)(2,1)}), bf16[8,128,256]{2,1,0:T(8,128)(2,1)S(1)}, u32[]{:S(2)}, u32[]{:S(2)}) async-start(bf16[8,128,256]{2,1,0:T(8,128)(2,1)} %shard_map.108), calls=%async_computation.1 | async-start | bytes 1048576 | tf_op jit(solution)/shard_map/all_to_all | solution.py:261
  104.5 4.7 %collective-permute-start.4 = (bf16[32,256]{1,0:T(8,128)(2,1)S(1)}, bf16[32,256]{1,0:T(8,128)(2,1)S(1)}, u32[]{:S(2)}, u32[]{:S(2)}) collective-permute-start(bf16[32,256]{1,0:T(8,128)(2,1)S(1)} %reduce_sum.12), channel_id=1, source_target_pairs={{0,32},{32,0},{64,96},{96,64},{128,160},{160,128},{192,224},{224,1... | collective-permute-start | bytes 49160 | tf_op jit(solution)/shard_map/ppermute | solution.py:180
  109.1 10.1 %collective-permute-start.7 = (bf16[64,256]{1,0:T(8,128)(2,1)S(1)}, bf16[64,256]{1,0:T(8,128)(2,1)S(1)}, u32[]{:S(2)}, u32[]{:S(2)}) collective-permute-start(bf16[64,256]{1,0:T(8,128)(2,1)S(1)} %pad_maximum_fusion.pair_ref), channel_id=1, source_target_pairs={{0,192},{32,224},{64,128},{96,160},{128,64},{160,96},{192,0},{224,... | collective-permute-start | bytes 98312 | tf_op jit(solution)/shard_map/ppermute | solution.py:180
  114.2 6.2 %collective-permute-start.6 = (bf16[64,256]{1,0:T(8,128)(2,1)S(1)}, bf16[64,256]{1,0:T(8,128)(2,1)S(1)}, u32[]{:S(2)}, u32[]{:S(2)}) collective-permute-start(bf16[64,256]{1,0:T(8,128)(2,1)S(1)} %pad_maximum_fusion.pair_ref), channel_id=1, source_target_pairs={{0,128},{32,160},{64,192},{96,224},{128,0},{160,32},{192,64},{224,... | collective-permute-start | bytes 98312 | tf_op jit(solution)/shard_map/ppermute | solution.py:180
  116.1 5.3 %collective-permute-start.5 = (bf16[64,256]{1,0:T(8,128)(2,1)S(1)}, bf16[64,256]{1,0:T(8,128)(2,1)S(1)}, u32[]{:S(2)}, u32[]{:S(2)}) collective-permute-start(bf16[64,256]{1,0:T(8,128)(2,1)S(1)} %pad_maximum_fusion.pair_ref), channel_id=1, source_target_pairs={{0,64},{32,96},{64,0},{96,32},{128,192},{160,224},{192,128},{224,1... | collective-permute-start | bytes 98312 | tf_op jit(solution)/shard_map/ppermute | solution.py:180

commit v9 on v8

--- a/solution.py
+++ b/solution.py
@@ -78,17 +78,18 @@
         out_ref[first : first + slices] = term
 
 
-def spread_sum(terms_ref, after_ref, out_ref):
-    del after_ref
-    total = terms_ref[0].astype(jnp.float32)
-    for i in range(1, terms_ref.shape[0]):
-        total += terms_ref[i].astype(jnp.float32)
-    total = total.astype(out_ref.dtype)
-    for p in range(out_ref.shape[0]):
-        out_ref[p] = total
-
-
-def products(place_ref, rows_ref, turned_ref, keep_ref, up_ref, down_ref, next_ref, last_ref, turned, sems):
+def share_sum(place_ref, own_ref, behind_ref, ahead_ref, far_ref, out_ref, shares):
+    place = place_ref[0]
+    for distance, ref in enumerate((own_ref, ahead_ref, far_ref, behind_ref)):
+        shares[(place + distance) & (RING - 1)] = ref[...].astype(jnp.float32)
+    total = ((shares[0] + shares[1]) + (shares[2] + shares[3])).astype(out_ref.dtype)
+    for y in range(out_ref.shape[0]):
+        out_ref[y] = total
+
+
+def products(
+    place_ref, rows_ref, turned_ref, keep_ref, up_ref, down_ref, up_rest_ref, down_rest_ref, next_ref, last_ref, turned, sems
+):
     groups, size, _ = keep_ref.shape
     half = size // 2
     place = place_ref[0]
@@ -117,29 +118,36 @@
                 up_ref[groups + g] = one[half:].astype(up_ref.dtype)
                 down_ref[groups + g] = three[:half].astype(down_ref.dtype)
             else:
-                next_ref[groups // 2 + g] = one[half:]
-                last_ref[groups // 2 + g] = three[:half]
-
-
-def relay(groups, next_ref, last_ref, up_ref, down_ref, next_out_ref, last_out_ref):
+                up_rest_ref[g - groups // 2] = one[half:].astype(up_ref.dtype)
+                down_rest_ref[g - groups // 2] = three[:half].astype(down_ref.dtype)
+
+
+def relay(terms_ref, next_ref, last_ref, up_ref, down_ref, next_out_ref, last_out_ref, share_ref):
+    groups, half, _ = next_ref.shape
     for g in range(groups):
-        next_out_ref[g] = (next_ref[g] + up_ref[g].astype(jnp.float32)).astype(next_out_ref.dtype)
-        last_out_ref[g] = (last_ref[g] + down_ref[g].astype(jnp.float32)).astype(last_out_ref.dtype)
-    for g in range(groups, next_ref.shape[0]):
-        next_out_ref[g] = next_ref[g].astype(next_out_ref.dtype)
-        last_out_ref[g] = last_ref[g].astype(last_out_ref.dtype)
-
-
-def add_ring(keep_ref, up_ref, down_ref, next_ref, last_ref, out_ref):
+        rows = slice(g * half, (g + 1) * half)
+        next_out_ref[rows] = (next_ref[g] + up_ref[g].astype(jnp.float32)).astype(next_out_ref.dtype)
+        last_out_ref[rows] = (last_ref[g] + down_ref[g].astype(jnp.float32)).astype(last_out_ref.dtype)
+    total = terms_ref[0].astype(jnp.float32)
+    for i in range(1, terms_ref.shape[0]):
+        total += terms_ref[i].astype(jnp.float32)
+    total = total.astype(share_ref.dtype)
+    share_ref[...] = total
+    next_out_ref[groups * half :] = total
+    last_out_ref[groups * half :] = total
+
+
+def add_ring(keep_ref, up_ref, down_ref, up_rest_ref, down_rest_ref, next_ref, last_ref, out_ref):
     groups, size, _ = keep_ref.shape
     half = size // 2
     for g in range(groups):
         if g < groups // 2:
             from_last, from_next = up_ref[groups + g], down_ref[groups + g]
         else:
-            from_last, from_next = next_ref[groups // 2 + g], last_ref[groups // 2 + g]
-        low = keep_ref[g, :half] + from_next.astype(jnp.float32) + next_ref[g].astype(jnp.float32)
-        high = keep_ref[g, half:] + from_last.astype(jnp.float32) + last_ref[g].astype(jnp.float32)
+            from_last, from_next = up_rest_ref[g - groups // 2], down_rest_ref[g - groups // 2]
+        rows = slice(g * half, (g + 1) * half)
+        low = keep_ref[g, :half] + from_next.astype(jnp.float32) + next_ref[rows].astype(jnp.float32)
+        high = keep_ref[g, half:] + from_last.astype(jnp.float32) + last_ref[rows].astype(jnp.float32)
         out_ref[g, :half] = low.astype(out_ref.dtype)
         out_ref[g, half:] = high.astype(out_ref.dtype)
 
@@ -220,13 +228,16 @@
 
     place = (lax.axis_index("rep") % RING).astype(jnp.int32)[None]
     full = jax.ShapeDtypeStruct((columns, size, width), jnp.float32)
-    waiting = jax.ShapeDtypeStruct((3 * columns // 2, size // 2, width), jnp.float32)
+    waiting = jax.ShapeDtypeStruct((columns, size // 2, width), jnp.float32)
     sent = jax.ShapeDtypeStruct((3 * columns // 2, size // 2, width), jnp.bfloat16)
-    keep, up, down, ahead, behind = pl.pallas_call(
+    rest = jax.ShapeDtypeStruct((columns // 2, size // 2, width), jnp.bfloat16)
+    passed_on = jax.ShapeDtypeStruct((columns * size // 2 + depth, width), jnp.bfloat16)
+    share = jax.ShapeDtypeStruct((depth, width), jnp.bfloat16)
+    keep, up, down, up_rest, down_rest, ahead, behind = pl.pallas_call(
         products,
-        out_shape=(full, sent, sent, waiting, waiting),
+        out_shape=(full, sent, sent, rest, rest, waiting, waiting),
         in_specs=[SMEM, VMEM, HBM],
-        out_specs=(VMEM,) * 5,
+        out_specs=(VMEM,) * 7,
         scratch_shapes=[
             pltpu.VMEM((col_blocks * size, total_rows), jnp.bfloat16),
             pltpu.SemaphoreType.DMA((columns,)),
@@ -235,29 +246,34 @@
         cost_estimate=pl.CostEstimate(flops=1700000000, bytes_accessed=9000000, transcendentals=0),
     )(place, received, pltpu.with_memory_space_constraint(turned, pltpu.HBM))
     up, down = passed(up, 1), passed(down, -1)
-    ahead, behind = pl.pallas_call(
-        functools.partial(relay, columns),
-        out_shape=(sent, sent),
-        in_specs=[VMEM] * 4,
-        out_specs=(VMEM, VMEM),
-        compiler_params=params,
-    )(ahead, behind, up, down)
-    share = pl.pallas_call(
-        spread_sum,
-        out_shape=jax.ShapeDtypeStruct((n_rep, depth, width), jnp.bfloat16),
-        in_specs=[VMEM, pl.BlockSpec(memory_space=pl.ANY)],
-        out_specs=VMEM,
-        compiler_params=params,
-    )(terms, ahead)
-    own = jnp.sum(exchange(share, "rep").astype(jnp.float32), axis=0)
-    ahead, behind = passed(ahead, 1), passed(behind, -1)
+    ahead, behind, own = pl.pallas_call(
+        relay,
+        out_shape=(passed_on, passed_on, share),
+        in_specs=[VMEM] * 5,
+        out_specs=(VMEM,) * 3,
+        compiler_params=params,
+    )(terms, ahead, behind, up, down)
+    ahead, behind, far = passed(ahead, 1), passed(behind, -1), passed(own, 2)
+    share_spec = pl.BlockSpec((depth, width), lambda i: (0, 0))
+    tail_spec = pl.BlockSpec((depth, width), lambda i: (columns * size // 2 // depth, 0))
+    shares = pl.pallas_call(
+        share_sum,
+        grid=(1,),
+        out_shape=jax.ShapeDtypeStruct((columns, depth, width), jnp.bfloat16),
+        in_specs=[SMEM, share_spec, tail_spec, tail_spec, share_spec],
+        out_specs=pl.BlockSpec((columns, depth, width), lambda i: (0, 0, 0)),
+        scratch_shapes=[pltpu.VMEM((RING, depth, width), jnp.float32)],
+        compiler_params=params,
+    )(place, own, ahead, behind, far)
+    own = jnp.sum(exchange(shares, "rep", axis_index_groups=groups).astype(jnp.float32), axis=0)
+    up_rest, down_rest = passed(up_rest, 1), passed(down_rest, -1)
     parts = pl.pallas_call(
         add_ring,
         out_shape=jax.ShapeDtypeStruct((columns, size, width), jnp.bfloat16),
-        in_specs=[VMEM] * 5,
+        in_specs=[VMEM] * 7,
         out_specs=VMEM,
         compiler_params=params,
-    )(keep, up, down, ahead, behind)
+    )(keep, up, down, up_rest, down_rest, ahead, behind)
     parts = exchange(parts, "rep", axis_index_groups=groups)
 
     own = own.astype(jnp.bfloat16)

time: 123 us -> 126 us (1.024); the launches traced: 122 us -> 124 us
  starting transfers between devices: 64.1 us -> 75.2 us
  waiting for transfers between devices: 31.6 us -> 22.5 us
    ppermute x4 -> x7, starting transfers between devices: 12.7 us -> 22.7 us  [passed(): lax.ppermute(value, 'rep', [(i, i - i % RING + (i + step) % RING) for i i...]
    ppermute x4 -> x7, waiting for transfers between devices: 22.9 us -> 14.1 us  [passed(): lax.ppermute(value, 'rep', [(i, i - i % RING + (i + step) % RING) for i i...]
    ppermute x4, starting transfers between devices: 13.1 us -> 16.3 us  [swapped(): lax.ppermute(value, axis, [(i, i ^ mask) for i in range(lax.axis_size(axi...]
    all_to_all x1, starting transfers between devices: 9.86 us -> 6.82 us  [per_device(): exchange(shares, 'rep', axis_index_groups=groups).astype(jnp.float32)]
    unnamed x8 -> x12, local copies, waits for them, and re-layouts: 4.13 us -> 4.79 us
  transfers between devices with their start and end apart: 12 -> 15, of which waited for: 9 -> 9; matrix products, arithmetic and copies ran while one was open for 1% -> 0% of each run, Pallas kernels for 12% -> 12%
where the time goes in v9:
time: 126 us; the launch traced here: 124 us
  starting transfers between devices  75.2 us (60%)
  waiting for transfers between devices  22.5 us (18%)
  Pallas kernels  19.8 us (16%)
  local copies, waits for them, and re-layouts  4.79 us (4%)
  between operations  1.49 us (1%)
    ppermute x7, starting transfers between devices, passed(): lax.ppermute(value, 'rep', [(i, i - i % RING + (i + step) % RING) for i i...  22.7 us
    all_to_all x1, starting transfers between devices, per_device(): exchange(outgoing.reshape(n_rows, per_peer, width), 'rows')  16.7 us
    ppermute x4, starting transfers between devices, swapped(): lax.ppermute(value, axis, [(i, i ^ mask) for i in range(lax.axis_size(axi...  16.3 us
    ppermute x7, waiting for transfers between devices, passed(): lax.ppermute(value, 'rep', [(i, i - i % RING + (i + step) % RING) for i i...  14.1 us
    pallas_call x1, Pallas kernels, per_device(): pl.pallas_call(place_tiles, out_shape=(pltpu.HBM((col_blocks * size, tota...  8.59 us
    all_to_all x1, starting transfers between devices, per_device(): exchange(shares, 'rep', axis_index_groups=groups).astype(jnp.float32)  6.82 us
    all_to_all x1, starting transfers between devices, per_device(): parts = exchange(parts, 'rep', axis_index_groups=groups)  6.44 us
    all_to_all x1, starting transfers between devices, per_device(): terms = exchange(term, 'rows')  6.22 us
  transfers between devices with their start and end apart: 15, of which 9 were waited for; matrix products, arithmetic and copies ran while one was open for 0% of the time, Pallas kernels for 12%

profile of v9, /device:TPU:1, one launch (start us, length us, event | category | flops | bytes accessed | tf_op | source)
XLA Modules:
  0.0 123.7 jit_solution(16632474052695628273)
XLA Ops:
  0.6 2.0 %shard_map.104 = bf16[768,256]{1,0:T(8,128)(2,1)} custom-call(s32[24]{0:T(128)} %bitcast.14, bf16[128,256]{1,0:T(8,128)(2,1)} %out_grad_ref.1, bf16[128,256]{1,0:T(8,128)(2,1)} %pre_relu_ref.1, s32[24,32]{1,0:T(8,128)} %bitcast.13), custom_call_target="tpu_custom_call" | custom-call | tf_op jit(solution)/shard_map/pallas_call | solution.py:193
  2.7 16.7 %all-to-all-start = ((bf16[24,32,256]{2,1,0:T(8,128)(2,1)}), bf16[24,32,256]{2,1,0:T(8,128)(2,1)S(1)}, u32[]{:S(2)}, u32[]{:S(2)}) async-start(bf16[24,32,256]{2,1,0:T(8,128)(2,1)} %bitcast.12), calls=%async_computation | async-start | bytes 786432 | tf_op jit(solution)/shard_map/all_to_all | solution.py:200
  20.0 0.0 copy-start.1
  20.0 1.9 %copy-done.1 = bf16[1,96,128,128]{3,2,1,0:T(8,128)(2,1)S(1)} copy-done((bf16[1,96,128,128]{3,2,1,0:T(8,128)(2,1)S(1)}, bf16[1,96,128,128]{3,2,1,0:T(8,128)(2,1)}, u32[]{:S(2)}) %copy-start.1) | copy-done | bytes 3145752
  21.9 0.0 copy-start.2
  21.9 1.6 %copy-done.2 = bf16[4096,256]{1,0:T(8,128)(2,1)S(1)} copy-done((bf16[4096,256]{1,0:T(8,128)(2,1)S(1)}, bf16[4096,256]{1,0:T(8,128)(2,1)}, u32[]{:S(2)}) %copy-start.2) | copy-done | bytes 2097176
  23.5 0.0 copy-start.5
  23.5 0.7 copy-done.5
  24.2 8.6 %shard_map.105 = (bf16[4096,768]{1,0:T(8,128)(2,1)}, bf16[256,768]{1,0:T(8,128)(2,1)S(1)}) custom-call(s32[96]{0:T(128)S(1)} %bitcast.11, s32[1]{0:T(128)S(6)} %copy.11.count_ref, bf16[96,128,128]{2,1,0:T(8,128)(2,1)S(1)} %bitcast.10, bf16[4096,256]{1,0:T(8,128)(2,1)S(1)} %copy-done.2), custom_call_target="tpu_custom_call" | custom-call | flops 1600000000 | bytes 24000000 | tf_op jit(solution)/shard_map/pallas_call | solution.py:202
  32.8 4.8 %all-to-all-done = bf16[24,32,256]{2,1,0:T(8,128)(2,1)S(1)} async-done(((bf16[24,32,256]{2,1,0:T(8,128)(2,1)}), bf16[24,32,256]{2,1,0:T(8,128)(2,1)S(1)}, u32[]{:S(2)}, u32[]{:S(2)}) %all-to-all-start) | async-done | bytes 393248 | tf_op jit(solution)/shard_map/all_to_all | solution.py:200
  37.6 1.0 shard_map.107
  38.6 6.2 %all-to-all-start.1 = ((bf16[24,32,256]{2,1,0:T(8,128)(2,1)}), bf16[24,32,256]{2,1,0:T(8,128)(2,1)S(1)}, u32[]{:S(2)}, u32[]{:S(2)}) async-start(bf16[24,32,256]{2,1,0:T(8,128)(2,1)} %shard_map.107), calls=%async_computation.1 | async-start | bytes 786432 | tf_op jit(solution)/shard_map/all_to_all | solution.py:227
  44.9 5.5 %shard_map.106 = (f32[8,128,256]{2,1,0:T(8,128)S(1)}, bf16[12,64,256]{2,1,0:T(8,128)(2,1)S(1)}, bf16[12,64,256]{2,1,0:T(8,128)(2,1)S(1)}, bf16[4,64,256]{2,1,0:T...) custom-call(s32[1]{0:T(128)} %bitcast.1.place_ref, ...), custom_call_target="tpu_custom_call" | custom-call | flops 1700000000 | bytes 9000000 | tf_op jit(solution)/shard_map/pallas_call | solution.py:236
  50.3 0.0 copy-start.4
  50.3 0.6 copy-done.4
  51.0 0.0 copy-start.3
  51.0 3.1 %collective-permute-start = (bf16[12,64,256]{2,1,0:T(8,128)(2,1)S(1)}, bf16[12,64,256]{2,1,0:T(8,128)(2,1)S(1)}, u32[]{:S(2)}, u32[]{:S(2)}) collective-permute-start(bf16[12,64,256]{2,1,0:T(8,128)(2,1)S(1)} %get-tuple-element.16), channel_id=1, source_target_pairs={{0,1},{1,2},{2,3},{3,0},{4,5},{5,6},{6,7},{7,4},{8,9},{9,10},{10,1... | collective-permute-start | bytes 1179656 | tf_op jit(solution)/shard_map/ppermute | solution.py:191
  54.1 3.4 %collective-permute-start.1 = (bf16[12,64,256]{2,1,0:T(8,128)(2,1)S(1)}, bf16[12,64,256]{2,1,0:T(8,128)(2,1)S(1)}, u32[]{:S(2)}, u32[]{:S(2)}) collective-permute-start(bf16[12,64,256]{2,1,0:T(8,128)(2,1)S(1)} %get-tuple-element.17), channel_id=1, source_target_pairs={{0,3},{1,0},{2,1},{3,2},{4,7},{5,4},{6,5},{7,6},{8,11},{9,8},{10,9... | collective-permute-start | bytes 1179656 | tf_op jit(solution)/shard_map/ppermute | solution.py:191
  57.5 7.0 %collective-permute-done.up_ref = bf16[12,64,256]{2,1,0:T(8,128)(2,1)S(1)} collective-permute-done((bf16[12,64,256]{2,1,0:T(8,128)(2,1)S(1)}, bf16[12,64,256]{2,1,0:T(8,128)(2,1)S(1)}, u32[]{:S(2)}, u32[]{:S(2)}) %collective-permute-start) | collective-permute-done | bytes 393248 | tf_op jit(solution)/shard_map/ppermute | solution.py:191
  64.5 1.6 %collective-permute-done.1.down_ref = bf16[12,64,256]{2,1,0:T(8,128)(2,1)S(1)} collective-permute-done((bf16[12,64,256]{2,1,0:T(8,128)(2,1)S(1)}, bf16[12,64,256]{2,1,0:T(8,128)(2,1)S(1)}, u32[]{:S(2)}, u32[]{:S(2)}) %collective-permute-start.1) | collective-permute-done | bytes 393248 | tf_op jit(solution)/shard_map/ppermute | solution.py:191
  66.1 0.0 all-to-all-done.1.terms_ref
  66.1 0.1 shard_map.108
  66.3 0.0 copy-start
  66.3 3.3 %collective-permute-start.4 = (bf16[544,256]{1,0:T(8,128)(2,1)S(1)}, bf16[544,256]{1,0:T(8,128)(2,1)S(1)}, u32[]{:S(2)}, u32[]{:S(2)}) collective-permute-start(bf16[544,256]{1,0:T(8,128)(2,1)S(1)} %get-tuple-element.23), channel_id=1, source_target_pairs={{0,1},{1,2},{2,3},{3,0},{4,5},{5,6},{6,7},{7,4},{8,9},{9,10},{10,1... | collective-permute-start | bytes 835592 | tf_op jit(solution)/shard_map/ppermute | solution.py:191
  69.5 0.0 copy-done.3
  69.5 3.4 %collective-permute-start.5 = (bf16[544,256]{1,0:T(8,128)(2,1)S(1)}, bf16[544,256]{1,0:T(8,128)(2,1)S(1)}, u32[]{:S(2)}, u32[]{:S(2)}) collective-permute-start(bf16[544,256]{1,0:T(8,128)(2,1)S(1)} %get-tuple-element.24), channel_id=1, source_target_pairs={{0,3},{1,0},{2,1},{3,2},{4,7},{5,4},{6,5},{7,6},{8,11},{9,8},{10,9... | collective-permute-start | bytes 835592 | tf_op jit(solution)/shard_map/ppermute | solution.py:191
  72.9 3.1 %collective-permute-start.6 = (bf16[32,256]{1,0:T(8,128)(2,1)S(1)}, bf16[32,256]{1,0:T(8,128)(2,1)S(1)}, u32[]{:S(2)}, u32[]{:S(2)}) collective-permute-start(bf16[32,256]{1,0:T(8,128)(2,1)S(1)} %get-tuple-element.25.own_ref), channel_id=1, source_target_pairs={{0,2},{1,3},{2,0},{3,1},{4,6},{5,7},{6,4},{7,5},{8,10},{9,11},{10,... | collective-permute-start | bytes 49160 | tf_op jit(solution)/shard_map/ppermute | solution.py:191
  76.1 3.1 %collective-permute-done.6.far_ref = bf16[32,256]{1,0:T(8,128)(2,1)S(1)} collective-permute-done((bf16[32,256]{1,0:T(8,128)(2,1)S(1)}, bf16[32,256]{1,0:T(8,128)(2,1)S(1)}, u32[]{:S(2)}, u32[]{:S(2)}) %collective-permute-start.6) | collective-permute-done | bytes 16416 | tf_op jit(solution)/shard_map/ppermute | solution.py:191
  79.2 0.0 collective-permute-done.4.next_ref.behind_ref
  79.2 0.0 collective-permute-done.5.last_ref.ahead_ref
  79.2 0.7 shard_map.110
  79.8 6.8 %all-to-all-start.3 = ((bf16[8,32,256]{2,1,0:T(8,128)(2,1)}), bf16[8,32,256]{2,1,0:T(8,128)(2,1)S(1)}, u32[]{:S(2)}, u32[]{:S(2)}) async-start(bf16[8,32,256]{2,1,0:T(8,128)(2,1)} %shard_map.110), calls=%async_computation.3 | async-start | bytes 262144 | tf_op jit(solution)/shard_map/all_to_all | solution.py:268
  86.7 2.7 %collective-permute-start.2 = (bf16[4,64,256]{2,1,0:T(8,128)(2,1)}, bf16[4,64,256]{2,1,0:T(8,128)(2,1)S(1)}, u32[]{:S(2)}, u32[]{:S(2)}) collective-permute-start(bf16[4,64,256]{2,1,0:T(8,128)(2,1)} %copy-done.4), channel_id=1, source_target_pairs={{0,1},{1,2},{2,3},{3,0},{4,5},{5,6},{6,7},{7,4},{8,9},{9,10},{10,1... | collective-permute-start | bytes 393224 | tf_op jit(solution)/shard_map/ppermute | solution.py:191
  89.4 3.8 %collective-permute-start.3 = (bf16[4,64,256]{2,1,0:T(8,128)(2,1)}, bf16[4,64,256]{2,1,0:T(8,128)(2,1)S(1)}, u32[]{:S(2)}, u32[]{:S(2)}) collective-permute-start(bf16[4,64,256]{2,1,0:T(8,128)(2,1)} %copy-done.3), channel_id=1, source_target_pairs={{0,3},{1,0},{2,1},{3,2},{4,7},{5,4},{6,5},{7,6},{8,11},{9,8},{10,9... | collective-permute-start | bytes 393224 | tf_op jit(solution)/shard_map/ppermute | solution.py:191
  93.2 0.6 collective-permute-done.2.up_rest_ref
  93.8 1.8 %collective-permute-done.3.down_rest_ref = bf16[4,64,256]{2,1,0:T(8,128)(2,1)S(1)} collective-permute-done((bf16[4,64,256]{2,1,0:T(8,128)(2,1)}, bf16[4,64,256]{2,1,0:T(8,128)(2,1)S(1)}, u32[]{:S(2)}, u32[]{:S(2)}) %collective-permute-start.3) | collective-permute-done | bytes 131104 | tf_op jit(solution)/shard_map/ppermute | solution.py:191
  95.6 1.0 shard_map.109
  96.6 0.0 all-to-all-done.3
  96.6 6.4 %all-to-all-start.2 = ((bf16[8,128,256]{2,1,0:T(8,128)(2,1)}), bf16[8,128,256]{2,1,0:T(8,128)(2,1)S(1)}, u32[]{:S(2)}, u32[]{:S(2)}) async-start(bf16[8,128,256]{2,1,0:T(8,128)(2,1)} %shard_map.109), calls=%async_computation.2 | async-start | bytes 1048576 | tf_op jit(solution)/shard_map/all_to_all | solution.py:277
  103.0 7.0 %collective-permute-start.7 = (bf16[32,256]{1,0:T(8,128)(2,1)S(1)}, bf16[32,256]{1,0:T(8,128)(2,1)S(1)}, u32[]{:S(2)}, u32[]{:S(2)}) collective-permute-start(bf16[32,256]{1,0:T(8,128)(2,1)S(1)} %reduce_sum.12), channel_id=1, source_target_pairs={{0,32},{32,0},{64,96},{96,64},{128,160},{160,128},{192,224},{224,1... | collective-permute-start | bytes 49160 | tf_op jit(solution)/shard_map/ppermute | solution.py:188
  110.1 0.8 collective-permute-done.7
  110.9 5.0 %collective-permute-start.10 = (bf16[64,256]{1,0:T(8,128)(2,1)S(1)}, bf16[64,256]{1,0:T(8,128)(2,1)S(1)}, u32[]{:S(2)}, u32[]{:S(2)}) collective-permute-start(bf16[64,256]{1,0:T(8,128)(2,1)S(1)} %pad_maximum_fusion.pair_ref), channel_id=1, source_target_pairs={{0,192},{32,224},{64,128},{96,160},{128,64},{160,96},{192,0},{224,... | collective-permute-start | bytes 98312 | tf_op jit(solution)/shard_map/ppermute | solution.py:188
  115.9 1.9 %collective-permute-start.9 = (bf16[64,256]{1,0:T(8,128)(2,1)S(1)}, bf16[64,256]{1,0:T(8,128)(2,1)S(1)}, u32[]{:S(2)}, u32[]{:S(2)}) collective-permute-start(bf16[64,256]{1,0:T(8,128)(2,1)S(1)} %pad_maximum_fusion.pair_ref), channel_id=1, source_target_pairs={{0,128},{32,160},{64,192},{96,224},{128,0},{160,32},{192,64},{224,... | collective-permute-start | bytes 98312 | tf_op jit(solution)/shard_map/ppermute | solution.py:188
  117.8 2.3 %collective-permute-start.8 = (bf16[64,256]{1,0:T(8,128)(2,1)S(1)}, bf16[64,256]{1,0:T(8,128)(2,1)S(1)}, u32[]{:S(2)}, u32[]{:S(2)}) collective-permute-start(bf16[64,256]{1,0:T(8,128)(2,1)S(1)} %pad_maximum_fusion.pair_ref), channel_id=1, source_target_pairs={{0,64},{32,96},{64,0},{96,32},{128,192},{160,224},{192,128},{224,1... | collective-permute-start | bytes 98312 | tf_op jit(solution)/shard_map/ppermute | solution.py:188
  120.2 0.0 collective-permute-done.10.six_ref
  120.2 1.6 %collective-permute-done.9.four_ref = bf16[64,256]{1,0:T(8,128)(2,1)S(1)} collective-permute-done((bf16[64,256]{1,0:T(8,128)(2,1)S(1)}, bf16[64,256]{1,0:T(8,128)(2,1)S(1)}, u32[]{:S(2)}, u32[]{:S(2)}) %collective-permute-start.9) | collective-permute-done | bytes 32800 | tf_op jit(solution)/shard_map/ppermute | solution.py:188
  121.8 1.0 collective-permute-done.8.two_ref
  122.9 0.0 all-to-all-done.2.parts_ref
  122.9 0.0 copy-done
  122.9 0.8 shard_map.111
  (2 shorter events, 0.0 us)
Async XLA Ops:
  2.7 34.9 %all-to-all-start = ((bf16[24,32,256]{2,1,0:T(8,128)(2,1)}), bf16[24,32,256]{2,1,0:T(8,128)(2,1)S(1)}, u32[]{:S(2)}, u32[]{:S(2)}) async-start(bf16[24,32,256]{2,1,0:T(8,128)(2,1)} %bitcast.12), calls=%async_computation | async-start | bytes 786432 | tf_op jit(solution)/shard_map/all_to_all | solution.py:200
  20.0 1.9 %copy-start.1 = (bf16[1,96,128,128]{3,2,1,0:T(8,128)(2,1)S(1)}, bf16[1,96,128,128]{3,2,1,0:T(8,128)(2,1)}, u32[]{:S(2)}) copy-start(bf16[1,96,128,128]{3,2,1,0:T(8,128)(2,1)} %param.17) | copy-start | bytes 9437188
  21.9 1.6 %copy-start.2 = (bf16[4096,256]{1,0:T(8,128)(2,1)S(1)}, bf16[4096,256]{1,0:T(8,128)(2,1)}, u32[]{:S(2)}) copy-start(bf16[4096,256]{1,0:T(8,128)(2,1)} %features_ref.1) | copy-start | bytes 6291460
  23.5 0.7 copy-start.5
  38.6 27.5 %all-to-all-start.1 = ((bf16[24,32,256]{2,1,0:T(8,128)(2,1)}), bf16[24,32,256]{2,1,0:T(8,128)(2,1)S(1)}, u32[]{:S(2)}, u32[]{:S(2)}) async-start(bf16[24,32,256]{2,1,0:T(8,128)(2,1)} %shard_map.107), calls=%async_computation.1 | async-start | bytes 786432 | tf_op jit(solution)/shard_map/all_to_all | solution.py:227
  50.3 0.7 copy-start.4
  51.0 18.5 %copy-start.3 = (bf16[4,64,256]{2,1,0:T(8,128)(2,1)}, bf16[4,64,256]{2,1,0:T(8,128)(2,1)S(1)}, u32[]{:S(2)}) copy-start(bf16[4,64,256]{2,1,0:T(8,128)(2,1)S(1)} %get-tuple-element.19) | copy-start | bytes 393220
  51.0 13.5 %collective-permute-start = (bf16[12,64,256]{2,1,0:T(8,128)(2,1)S(1)}, bf16[12,64,256]{2,1,0:T(8,128)(2,1)S(1)}, u32[]{:S(2)}, u32[]{:S(2)}) collective-permute-start(bf16[12,64,256]{2,1,0:T(8,128)(2,1)S(1)} %get-tuple-element.16), channel_id=1, source_target_pairs={{0,1},{1,2},{2,3},{3,0},{4,5},{5,6},{6,7},{7,4},{8,9},{9,10},{10,1... | collective-permute-start | bytes 1179656 | tf_op jit(solution)/shard_map/ppermute | solution.py:191
  54.1 12.0 %collective-permute-start.1 = (bf16[12,64,256]{2,1,0:T(8,128)(2,1)S(1)}, bf16[12,64,256]{2,1,0:T(8,128)(2,1)S(1)}, u32[]{:S(2)}, u32[]{:S(2)}) collective-permute-start(bf16[12,64,256]{2,1,0:T(8,128)(2,1)S(1)} %get-tuple-element.17), channel_id=1, source_target_pairs={{0,3},{1,0},{2,1},{3,2},{4,7},{5,4},{6,5},{7,6},{8,11},{9,8},{10,9... | collective-permute-start | bytes 1179656 | tf_op jit(solution)/shard_map/ppermute | solution.py:191
  66.3 56.6 %copy-start = (bf16[256,256]{1,0:T(8,128)(2,1)S(1)}, bf16[256,256]{1,0:T(8,128)(2,1)}, u32[]{:S(2)}) copy-start(bf16[256,256]{1,0:T(8,128)(2,1)} %weight_ref.1) | copy-start | bytes 393220
  66.3 12.9 %collective-permute-start.4 = (bf16[544,256]{1,0:T(8,128)(2,1)S(1)}, bf16[544,256]{1,0:T(8,128)(2,1)S(1)}, u32[]{:S(2)}, u32[]{:S(2)}) collective-permute-start(bf16[544,256]{1,0:T(8,128)(2,1)S(1)} %get-tuple-element.23), channel_id=1, source_target_pairs={{0,1},{1,2},{2,3},{3,0},{4,5},{5,6},{6,7},{7,4},{8,9},{9,10},{10,1... | collective-permute-start | bytes 835592 | tf_op jit(solution)/shard_map/ppermute | solution.py:191
  69.5 9.6 %collective-permute-start.5 = (bf16[544,256]{1,0:T(8,128)(2,1)S(1)}, bf16[544,256]{1,0:T(8,128)(2,1)S(1)}, u32[]{:S(2)}, u32[]{:S(2)}) collective-permute-start(bf16[544,256]{1,0:T(8,128)(2,1)S(1)} %get-tuple-element.24), channel_id=1, source_target_pairs={{0,3},{1,0},{2,1},{3,2},{4,7},{5,4},{6,5},{7,6},{8,11},{9,8},{10,9... | collective-permute-start | bytes 835592 | tf_op jit(solution)/shard_map/ppermute | solution.py:191
  72.9 6.2 %collective-permute-start.6 = (bf16[32,256]{1,0:T(8,128)(2,1)S(1)}, bf16[32,256]{1,0:T(8,128)(2,1)S(1)}, u32[]{:S(2)}, u32[]{:S(2)}) collective-permute-start(bf16[32,256]{1,0:T(8,128)(2,1)S(1)} %get-tuple-element.25.own_ref), channel_id=1, source_target_pairs={{0,2},{1,3},{2,0},{3,1},{4,6},{5,7},{6,4},{7,5},{8,10},{9,11},{10,... | collective-permute-start | bytes 49160 | tf_op jit(solution)/shard_map/ppermute | solution.py:191
  79.8 16.7 %all-to-all-start.3 = ((bf16[8,32,256]{2,1,0:T(8,128)(2,1)}), bf16[8,32,256]{2,1,0:T(8,128)(2,1)S(1)}, u32[]{:S(2)}, u32[]{:S(2)}) async-start(bf16[8,32,256]{2,1,0:T(8,128)(2,1)} %shard_map.110), calls=%async_computation.3 | async-start | bytes 262144 | tf_op jit(solution)/shard_map/all_to_all | solution.py:268
  86.7 7.1 %collective-permute-start.2 = (bf16[4,64,256]{2,1,0:T(8,128)(2,1)}, bf16[4,64,256]{2,1,0:T(8,128)(2,1)S(1)}, u32[]{:S(2)}, u32[]{:S(2)}) collective-permute-start(bf16[4,64,256]{2,1,0:T(8,128)(2,1)} %copy-done.4), channel_id=1, source_target_pairs={{0,1},{1,2},{2,3},{3,0},{4,5},{5,6},{6,7},{7,4},{8,9},{9,10},{10,1... | collective-permute-start | bytes 393224 | tf_op jit(solution)/shard_map/ppermute | solution.py:191
  89.4 6.2 %collective-permute-start.3 = (bf16[4,64,256]{2,1,0:T(8,128)(2,1)}, bf16[4,64,256]{2,1,0:T(8,128)(2,1)S(1)}, u32[]{:S(2)}, u32[]{:S(2)}) collective-permute-start(bf16[4,64,256]{2,1,0:T(8,128)(2,1)} %copy-done.3), channel_id=1, source_target_pairs={{0,3},{1,0},{2,1},{3,2},{4,7},{5,4},{6,5},{7,6},{8,11},{9,8},{10,9... | collective-permute-start | bytes 393224 | tf_op jit(solution)/shard_map/ppermute | solution.py:191
  96.6 26.3 %all-to-all-start.2 = ((bf16[8,128,256]{2,1,0:T(8,128)(2,1)}), bf16[8,128,256]{2,1,0:T(8,128)(2,1)S(1)}, u32[]{:S(2)}, u32[]{:S(2)}) async-start(bf16[8,128,256]{2,1,0:T(8,128)(2,1)} %shard_map.109), calls=%async_computation.2 | async-start | bytes 1048576 | tf_op jit(solution)/shard_map/all_to_all | solution.py:277
  103.0 7.8 %collective-permute-start.7 = (bf16[32,256]{1,0:T(8,128)(2,1)S(1)}, bf16[32,256]{1,0:T(8,128)(2,1)S(1)}, u32[]{:S(2)}, u32[]{:S(2)}) collective-permute-start(bf16[32,256]{1,0:T(8,128)(2,1)S(1)} %reduce_sum.12), channel_id=1, source_target_pairs={{0,32},{32,0},{64,96},{96,64},{128,160},{160,128},{192,224},{224,1... | collective-permute-start | bytes 49160 | tf_op jit(solution)/shard_map/ppermute | solution.py:188
  110.9 9.3 %collective-permute-start.10 = (bf16[64,256]{1,0:T(8,128)(2,1)S(1)}, bf16[64,256]{1,0:T(8,128)(2,1)S(1)}, u32[]{:S(2)}, u32[]{:S(2)}) collective-permute-start(bf16[64,256]{1,0:T(8,128)(2,1)S(1)} %pad_maximum_fusion.pair_ref), channel_id=1, source_target_pairs={{0,192},{32,224},{64,128},{96,160},{128,64},{160,96},{192,0},{224,... | collective-permute-start | bytes 98312 | tf_op jit(solution)/shard_map/ppermute | solution.py:188
  115.9 5.9 %collective-permute-start.9 = (bf16[64,256]{1,0:T(8,128)(2,1)S(1)}, bf16[64,256]{1,0:T(8,128)(2,1)S(1)}, u32[]{:S(2)}, u32[]{:S(2)}) collective-permute-start(bf16[64,256]{1,0:T(8,128)(2,1)S(1)} %pad_maximum_fusion.pair_ref), channel_id=1, source_target_pairs={{0,128},{32,160},{64,192},{96,224},{128,0},{160,32},{192,64},{224,... | collective-permute-start | bytes 98312 | tf_op jit(solution)/shard_map/ppermute | solution.py:188
  117.8 5.0 %collective-permute-start.8 = (bf16[64,256]{1,0:T(8,128)(2,1)S(1)}, bf16[64,256]{1,0:T(8,128)(2,1)S(1)}, u32[]{:S(2)}, u32[]{:S(2)}) collective-permute-start(bf16[64,256]{1,0:T(8,128)(2,1)S(1)} %pad_maximum_fusion.pair_ref), channel_id=1, source_target_pairs={{0,64},{32,96},{64,0},{96,32},{128,192},{160,224},{192,128},{224,1... | collective-permute-start | bytes 98312 | tf_op jit(solution)/shard_map/ppermute | solution.py:188

commit v10 on v8

--- a/solution.py
+++ b/solution.py
@@ -78,14 +78,11 @@
         out_ref[first : first + slices] = term
 
 
-def spread_sum(terms_ref, after_ref, out_ref):
-    del after_ref
-    total = terms_ref[0].astype(jnp.float32)
-    for i in range(1, terms_ref.shape[0]):
-        total += terms_ref[i].astype(jnp.float32)
-    total = total.astype(out_ref.dtype)
-    for p in range(out_ref.shape[0]):
-        out_ref[p] = total
+def ring_sum(place_ref, own_ref, ahead_ref, far_ref, behind_ref, out_ref, shares):
+    place = place_ref[0]
+    for distance, ref in enumerate((own_ref, ahead_ref, far_ref, behind_ref)):
+        shares[(place + distance) & (RING - 1)] = ref[...]
+    out_ref[...] = ((shares[0] + shares[1]) + (shares[2] + shares[3])).astype(out_ref.dtype)
 
 
 def products(place_ref, rows_ref, turned_ref, keep_ref, up_ref, down_ref, next_ref, last_ref, turned, sems):
@@ -121,16 +118,23 @@
                 last_ref[groups // 2 + g] = three[:half]
 
 
-def relay(groups, next_ref, last_ref, up_ref, down_ref, next_out_ref, last_out_ref):
+def relay(terms_ref, next_ref, last_ref, up_ref, down_ref, next_out_ref, last_out_ref, share_ref):
+    groups = share_ref.shape[0]
     for g in range(groups):
         next_out_ref[g] = (next_ref[g] + up_ref[g].astype(jnp.float32)).astype(next_out_ref.dtype)
         last_out_ref[g] = (last_ref[g] + down_ref[g].astype(jnp.float32)).astype(last_out_ref.dtype)
     for g in range(groups, next_ref.shape[0]):
         next_out_ref[g] = next_ref[g].astype(next_out_ref.dtype)
         last_out_ref[g] = last_ref[g].astype(last_out_ref.dtype)
-
-
-def add_ring(keep_ref, up_ref, down_ref, next_ref, last_ref, out_ref):
+    total = terms_ref[0].astype(jnp.float32)
+    for i in range(1, terms_ref.shape[0]):
+        total += terms_ref[i].astype(jnp.float32)
+    for y in range(groups):
+        share_ref[y] = total.astype(share_ref.dtype)
+
+
+def add_ring(keep_ref, up_ref, down_ref, next_ref, last_ref, after_ref, out_ref):
+    del after_ref
     groups, size, _ = keep_ref.shape
     half = size // 2
     for g in range(groups):
@@ -235,32 +239,32 @@
         cost_estimate=pl.CostEstimate(flops=1700000000, bytes_accessed=9000000, transcendentals=0),
     )(place, received, pltpu.with_memory_space_constraint(turned, pltpu.HBM))
     up, down = passed(up, 1), passed(down, -1)
-    ahead, behind = pl.pallas_call(
-        functools.partial(relay, columns),
-        out_shape=(sent, sent),
-        in_specs=[VMEM] * 4,
-        out_specs=(VMEM, VMEM),
-        compiler_params=params,
-    )(ahead, behind, up, down)
-    share = pl.pallas_call(
-        spread_sum,
-        out_shape=jax.ShapeDtypeStruct((n_rep, depth, width), jnp.bfloat16),
-        in_specs=[VMEM, pl.BlockSpec(memory_space=pl.ANY)],
-        out_specs=VMEM,
-        compiler_params=params,
-    )(terms, ahead)
-    own = jnp.sum(exchange(share, "rep").astype(jnp.float32), axis=0)
+    ahead, behind, shares = pl.pallas_call(
+        relay,
+        out_shape=(sent, sent, jax.ShapeDtypeStruct((columns, depth, width), jnp.bfloat16)),
+        in_specs=[VMEM] * 5,
+        out_specs=(VMEM,) * 3,
+        compiler_params=params,
+    )(terms, ahead, behind, up, down)
+    own = jnp.sum(exchange(shares, "rep", axis_index_groups=groups).astype(jnp.float32), axis=0)
     ahead, behind = passed(ahead, 1), passed(behind, -1)
+    own = pl.pallas_call(
+        ring_sum,
+        out_shape=jax.ShapeDtypeStruct((depth, width), jnp.bfloat16),
+        in_specs=[SMEM] + [VMEM] * 4,
+        out_specs=VMEM,
+        scratch_shapes=[pltpu.VMEM((RING, depth, width), jnp.float32)],
+        compiler_params=params,
+    )(place, own, passed(own, -1), passed(own, 2), passed(own, 1))
     parts = pl.pallas_call(
         add_ring,
         out_shape=jax.ShapeDtypeStruct((columns, size, width), jnp.bfloat16),
-        in_specs=[VMEM] * 5,
-        out_specs=VMEM,
-        compiler_params=params,
-    )(keep, up, down, ahead, behind)
+        in_specs=[VMEM] * 5 + [pl.BlockSpec(memory_space=pl.ANY)],
+        out_specs=VMEM,
+        compiler_params=params,
+    )(keep, up, down, ahead, behind, own)
     parts = exchange(parts, "rep", axis_index_groups=groups)
 
-    own = own.astype(jnp.bfloat16)
     pair = jnp.concatenate([own, swapped(own, 1, "rows")], axis=0)
     others = [swapped(pair, mask, "rows") for mask in (2, 4, 6)]
     return pl.pallas_call(

time: 123 us -> 126 us (1.024)
  blocking collectives: 0 us -> 14.7 us
  waiting for transfers between devices: 31.6 us -> 19.4 us
  local copies, waits for them, and re-layouts: 4.13 us -> 6.15 us
    all_to_all x0 -> x1, blocking collectives: none -> 14.7 us  [per_device(): exchange(shares, 'rep', axis_index_groups=groups).astype(jnp.float32)]
    ppermute x4 -> x7, waiting for transfers between devices: 22.9 us -> 11 us  [passed(): lax.ppermute(value, 'rep', [(i, i - i % RING + (i + step) % RING) for i i...]
    all_to_all x1 -> x0, starting transfers between devices: 9.86 us -> none  [per_device(): own = jnp.sum(exchange(share, 'rep').astype(jnp.float32), axis=0)]
    ppermute x4 -> x7, starting transfers between devices: 12.7 us -> 22 us  [passed(): lax.ppermute(value, 'rep', [(i, i - i % RING + (i + step) % RING) for i i...]
    ppermute x4, starting transfers between devices: 13.1 us -> 15.9 us  [swapped(): lax.ppermute(value, axis, [(i, i ^ mask) for i in range(lax.axis_size(axi...]
    all_to_all x1, starting transfers between devices: 5.56 us -> 3.49 us  [per_device(): parts = exchange(parts, 'rep', axis_index_groups=groups)]
    unnamed x8 -> x12, local copies, waits for them, and re-layouts: 4.13 us -> 6.15 us
  transfers between devices with their start and end apart: 12 -> 14, of which waited for: 9 -> 7; matrix products, arithmetic and copies ran while one was open for 1% -> 0% of each run, Pallas kernels for 12% -> 11%
where the time goes in v10:
time: 126 us; the launch traced here: 125 us
  starting transfers between devices  64.3 us (51%)
  waiting for transfers between devices  19.4 us (15%)
  Pallas kernels  19.1 us (15%)
  blocking collectives  14.7 us (12%)
  local copies, waits for them, and re-layouts  6.15 us (5%)
  between operations  1.51 us (1%)
    ppermute x7, starting transfers between devices, passed(): lax.ppermute(value, 'rep', [(i, i - i % RING + (i + step) % RING) for i i...  22 us
    all_to_all x1, starting transfers between devices, per_device(): exchange(outgoing.reshape(n_rows, per_peer, width), 'rows')  16.7 us
    ppermute x4, starting transfers between devices, swapped(): lax.ppermute(value, axis, [(i, i ^ mask) for i in range(lax.axis_size(axi...  15.9 us
    all_to_all x1, blocking collectives, per_device(): exchange(shares, 'rep', axis_index_groups=groups).astype(jnp.float32)  14.7 us
    ppermute x7, waiting for transfers between devices, passed(): lax.ppermute(value, 'rep', [(i, i - i % RING + (i + step) % RING) for i i...  11 us
    pallas_call x1, Pallas kernels, per_device(): pl.pallas_call(place_tiles, out_shape=(pltpu.HBM((col_blocks * size, tota...  8.59 us
    all_to_all x1, starting transfers between devices, per_device(): terms = exchange(term, 'rows')  6.22 us
    unnamed x12, local copies, waits for them, and re-layouts  6.15 us
  transfers between devices with their start and end apart: 14, of which 7 were waited for; matrix products, arithmetic and copies ran while one was open for 0% of the time, Pallas kernels for 11%

profile of v10, /device:TPU:1, one launch (start us, length us, event | category | flops | bytes accessed | tf_op | source)
XLA Modules:
  0.0 125.1 jit_solution(7669747051115780540)
XLA Ops:
  0.6 2.0 %shard_map.104 = bf16[768,256]{1,0:T(8,128)(2,1)} custom-call(s32[24]{0:T(128)} %bitcast.14, bf16[128,256]{1,0:T(8,128)(2,1)} %out_grad_ref.1, bf16[128,256]{1,0:T(8,128)(2,1)} %pre_relu_ref.1, s32[24,32]{1,0:T(8,128)} %bitcast.13), custom_call_target="tpu_custom_call" | custom-call | tf_op jit(solution)/shard_map/pallas_call | solution.py:189
  2.7 16.7 %all-to-all-start = ((bf16[24,32,256]{2,1,0:T(8,128)(2,1)}), bf16[24,32,256]{2,1,0:T(8,128)(2,1)S(1)}, u32[]{:S(2)}, u32[]{:S(2)}) async-start(bf16[24,32,256]{2,1,0:T(8,128)(2,1)} %bitcast.12), calls=%async_computation | async-start | bytes 786432 | tf_op jit(solution)/shard_map/all_to_all | solution.py:196
  20.0 0.0 copy-start.3
  20.0 1.9 %copy-done.3 = bf16[1,96,128,128]{3,2,1,0:T(8,128)(2,1)S(1)} copy-done((bf16[1,96,128,128]{3,2,1,0:T(8,128)(2,1)S(1)}, bf16[1,96,128,128]{3,2,1,0:T(8,128)(2,1)}, u32[]{:S(2)}) %copy-start.3) | copy-done | bytes 3145752
  21.9 0.0 copy-start.4
  21.9 1.6 %copy-done.4 = bf16[4096,256]{1,0:T(8,128)(2,1)S(1)} copy-done((bf16[4096,256]{1,0:T(8,128)(2,1)S(1)}, bf16[4096,256]{1,0:T(8,128)(2,1)}, u32[]{:S(2)}) %copy-start.4) | copy-done | bytes 2097176
  23.5 0.0 copy-start.5
  23.5 0.7 copy-done.5
  24.2 8.6 %shard_map.105 = (bf16[4096,768]{1,0:T(8,128)(2,1)}, bf16[256,768]{1,0:T(8,128)(2,1)S(1)}) custom-call(s32[96]{0:T(128)S(1)} %bitcast.11, s32[1]{0:T(128)S(6)} %copy.11.count_ref, bf16[96,128,128]{2,1,0:T(8,128)(2,1)S(1)} %bitcast.10, bf16[4096,256]{1,0:T(8,128)(2,1)S(1)} %copy-done.4), custom_call_target="tpu_custom_call" | custom-call | flops 1600000000 | bytes 24000000 | tf_op jit(solution)/shard_map/pallas_call | solution.py:198
  32.8 4.8 %all-to-all-done = bf16[24,32,256]{2,1,0:T(8,128)(2,1)S(1)} async-done(((bf16[24,32,256]{2,1,0:T(8,128)(2,1)}), bf16[24,32,256]{2,1,0:T(8,128)(2,1)S(1)}, u32[]{:S(2)}, u32[]{:S(2)}) %all-to-all-start) | async-done | bytes 393248 | tf_op jit(solution)/shard_map/all_to_all | solution.py:196
  37.6 1.0 shard_map.107
  38.6 6.2 %all-to-all-start.1 = ((bf16[24,32,256]{2,1,0:T(8,128)(2,1)}), bf16[24,32,256]{2,1,0:T(8,128)(2,1)S(1)}, u32[]{:S(2)}, u32[]{:S(2)}) async-start(bf16[24,32,256]{2,1,0:T(8,128)(2,1)} %shard_map.107), calls=%async_computation.1 | async-start | bytes 786432 | tf_op jit(solution)/shard_map/all_to_all | solution.py:223
  44.9 5.5 %shard_map.106 = (f32[8,128,256]{2,1,0:T(8,128)S(1)}, bf16[12,64,256]{2,1,0:T(8,128)(2,1)S(1)}, bf16[12,64,256]{2,1,0:T(8,128)(2,1)S(1)}, f32[12,64,256]{2,1,0:T(8,128)S(1)}, f32[12,64,256]{2,1,0:T(8,128)S(1)}) custom-call(s32[1]{0:T(128)} %bitcast.1.place_ref, bf16[768,256]{1,0:T(8,128)(2,1)S(1)} %bitcast.9, bf16[4096,768]{1,0:T(8,128)(2,1)} %get-tuple-element.12.turned_ref), custom_call_target="tpu_custom_call" | custom-call | flops 1700000000 | bytes 9000000 | tf_op jit(solution)/shard_map/pallas_call | solution.py:229
  50.3 0.0 copy-start
  50.3 0.9 copy-done
  51.2 3.1 %collective-permute-start = (bf16[12,64,256]{2,1,0:T(8,128)(2,1)S(1)}, bf16[12,64,256]{2,1,0:T(8,128)(2,1)S(1)}, u32[]{:S(2)}, u32[]{:S(2)}) collective-permute-start(bf16[12,64,256]{2,1,0:T(8,128)(2,1)S(1)} %get-tuple-element.14), channel_id=1, source_target_pairs={{0,1},{1,2},{2,3},{3,0},{4,5},{5,6},{6,7},{7,4},{8,9},{9,10},{10,1... | collective-permute-start | bytes 1179656 | tf_op jit(solution)/shard_map/ppermute | solution.py:187
  54.3 3.4 %collective-permute-start.1 = (bf16[12,64,256]{2,1,0:T(8,128)(2,1)S(1)}, bf16[12,64,256]{2,1,0:T(8,128)(2,1)S(1)}, u32[]{:S(2)}, u32[]{:S(2)}) collective-permute-start(bf16[12,64,256]{2,1,0:T(8,128)(2,1)S(1)} %get-tuple-element.15), channel_id=1, source_target_pairs={{0,3},{1,0},{2,1},{3,2},{4,7},{5,4},{6,5},{7,6},{8,11},{9,8},{10,9... | collective-permute-start | bytes 1179656 | tf_op jit(solution)/shard_map/ppermute | solution.py:187
  57.7 7.0 %collective-permute-done.up_ref = bf16[12,64,256]{2,1,0:T(8,128)(2,1)S(1)} collective-permute-done((bf16[12,64,256]{2,1,0:T(8,128)(2,1)S(1)}, bf16[12,64,256]{2,1,0:T(8,128)(2,1)S(1)}, u32[]{:S(2)}, u32[]{:S(2)}) %collective-permute-start) | collective-permute-done | bytes 393248 | tf_op jit(solution)/shard_map/ppermute | solution.py:187
  64.7 1.6 %collective-permute-done.1.down_ref = bf16[12,64,256]{2,1,0:T(8,128)(2,1)S(1)} collective-permute-done((bf16[12,64,256]{2,1,0:T(8,128)(2,1)S(1)}, bf16[12,64,256]{2,1,0:T(8,128)(2,1)S(1)}, u32[]{:S(2)}, u32[]{:S(2)}) %collective-permute-start.1) | collective-permute-done | bytes 393248 | tf_op jit(solution)/shard_map/ppermute | solution.py:187
  66.3 0.0 all-to-all-done.1.terms_ref
  66.3 0.0 copy-start.1
  66.3 1.1 copy-done.1
  67.4 0.0 copy-start.2
  67.5 0.2 shard_map.108
  67.6 3.1 %collective-permute-start.2 = (bf16[12,64,256]{2,1,0:T(8,128)(2,1)S(1)}, bf16[12,64,256]{2,1,0:T(8,128)(2,1)S(1)}, u32[]{:S(2)}, u32[]{:S(2)}) collective-permute-start(bf16[12,64,256]{2,1,0:T(8,128)(2,1)S(1)} %get-tuple-element.19), channel_id=1, source_target_pairs={{0,1},{1,2},{2,3},{3,0},{4,5},{5,6},{6,7},{7,4},{8,9},{9,10},{10,1... | collective-permute-start | bytes 1179656 | tf_op jit(solution)/shard_map/ppermute | solution.py:187
  70.7 3.4 %collective-permute-start.3 = (bf16[12,64,256]{2,1,0:T(8,128)(2,1)S(1)}, bf16[12,64,256]{2,1,0:T(8,128)(2,1)S(1)}, u32[]{:S(2)}, u32[]{:S(2)}) collective-permute-start(bf16[12,64,256]{2,1,0:T(8,128)(2,1)S(1)} %get-tuple-element.20), channel_id=1, source_target_pairs={{0,3},{1,0},{2,1},{3,2},{4,7},{5,4},{6,5},{7,6},{8,11},{9,8},{10,9... | collective-permute-start | bytes 1179656 | tf_op jit(solution)/shard_map/ppermute | solution.py:187
  74.1 14.7 %all_to_all.20 = bf16[8,32,256]{2,1,0:T(8,128)(2,1)S(1)} all-to-all(bf16[8,32,256]{2,1,0:T(8,128)(2,1)S(1)} %get-tuple-element.21), channel_id=1, replica_groups={{0,4,8,12,16,20,24,28},{1,5,9,13,17,21,25,29},{2,6,10,14,18,22,26,30},{..., dimensions={0} | all-to-all | bytes 262144 | tf_op jit(solution)/shard_map/all_to_all | solution.py:249
  88.8 1.9 %collective-permute-start.6 = (f32[32,256]{1,0:T(8,128)S(1)}, f32[32,256]{1,0:T(8,128)S(1)}, u32[]{:S(2)}, u32[]{:S(2)}) collective-permute-start(f32[32,256]{1,0:T(8,128)S(1)} %convert_reduce_fusion.own_ref), channel_id=1, source_target_pairs={{0,1},{1,2},{2,3},{3,0},{4,5},{5,6},{6,7},{7,4},{8,9},{9,10},{10,1... | collective-permute-start | bytes 98312 | tf_op jit(solution)/shard_map/ppermute | solution.py:187
  90.7 4.5 %collective-permute-start.5 = (f32[32,256]{1,0:T(8,128)S(1)}, f32[32,256]{1,0:T(8,128)S(1)}, u32[]{:S(2)}, u32[]{:S(2)}) collective-permute-start(f32[32,256]{1,0:T(8,128)S(1)} %convert_reduce_fusion.own_ref), channel_id=1, source_target_pairs={{0,2},{1,3},{2,0},{3,1},{4,6},{5,7},{6,4},{7,5},{8,10},{9,11},{10,... | collective-permute-start | bytes 98312 | tf_op jit(solution)/shard_map/ppermute | solution.py:187
  95.3 2.6 %collective-permute-start.4 = (f32[32,256]{1,0:T(8,128)S(1)}, f32[32,256]{1,0:T(8,128)S(1)}, u32[]{:S(2)}, u32[]{:S(2)}) collective-permute-start(f32[32,256]{1,0:T(8,128)S(1)} %convert_reduce_fusion.own_ref), channel_id=1, source_target_pairs={{0,3},{1,0},{2,1},{3,2},{4,7},{5,4},{6,5},{7,6},{8,11},{9,8},{10,9... | collective-permute-start | bytes 98312 | tf_op jit(solution)/shard_map/ppermute | solution.py:187
  97.9 0.0 collective-permute-done.6.behind_ref
  97.9 0.0 collective-permute-done.5.far_ref
  97.9 2.4 %collective-permute-done.4.ahead_ref = f32[32,256]{1,0:T(8,128)S(1)} collective-permute-done((f32[32,256]{1,0:T(8,128)S(1)}, f32[32,256]{1,0:T(8,128)S(1)}, u32[]{:S(2)}, u32[]{:S(2)}) %collective-permute-start.4) | collective-permute-done | bytes 32800 | tf_op jit(solution)/shard_map/ppermute | solution.py:187
  100.3 0.0 collective-permute-done.2.next_ref
  100.3 0.0 collective-permute-done.3.last_ref
  100.3 1.0 shard_map.110
  101.2 3.5 %all-to-all-start.3 = ((bf16[8,128,256]{2,1,0:T(8,128)(2,1)}), bf16[8,128,256]{2,1,0:T(8,128)(2,1)S(1)}, u32[]{:S(2)}, u32[]{:S(2)}) async-start(bf16[8,128,256]{2,1,0:T(8,128)(2,1)} %shard_map.110), calls=%async_computation.3 | async-start | bytes 1048576 | tf_op jit(solution)/shard_map/all_to_all | solution.py:266
  104.7 6.6 %collective-permute-start.7 = (bf16[32,256]{1,0:T(8,128)(2,1)S(1)}, bf16[32,256]{1,0:T(8,128)(2,1)S(1)}, u32[]{:S(2)}, u32[]{:S(2)}) collective-permute-start(bf16[32,256]{1,0:T(8,128)(2,1)S(1)} %shard_map.109.after_ref), channel_id=1, source_target_pairs={{0,32},{32,0},{64,96},{96,64},{128,160},{160,128},{192,224},{224,1... | collective-permute-start | bytes 49160 | tf_op jit(solution)/shard_map/ppermute | solution.py:184
  111.4 0.8 collective-permute-done.7
  112.2 5.1 %collective-permute-start.10 = (bf16[64,256]{1,0:T(8,128)(2,1)S(1)}, bf16[64,256]{1,0:T(8,128)(2,1)S(1)}, u32[]{:S(2)}, u32[]{:S(2)}) collective-permute-start(bf16[64,256]{1,0:T(8,128)(2,1)S(1)} %pad_maximum_fusion.pair_ref), channel_id=1, source_target_pairs={{0,192},{32,224},{64,128},{96,160},{128,64},{160,96},{192,0},{224,... | collective-permute-start | bytes 98312 | tf_op jit(solution)/shard_map/ppermute | solution.py:184
  117.3 1.9 %collective-permute-start.9 = (bf16[64,256]{1,0:T(8,128)(2,1)S(1)}, bf16[64,256]{1,0:T(8,128)(2,1)S(1)}, u32[]{:S(2)}, u32[]{:S(2)}) collective-permute-start(bf16[64,256]{1,0:T(8,128)(2,1)S(1)} %pad_maximum_fusion.pair_ref), channel_id=1, source_target_pairs={{0,128},{32,160},{64,192},{96,224},{128,0},{160,32},{192,64},{224,... | collective-permute-start | bytes 98312 | tf_op jit(solution)/shard_map/ppermute | solution.py:184
  119.3 2.2 %collective-permute-start.8 = (bf16[64,256]{1,0:T(8,128)(2,1)S(1)}, bf16[64,256]{1,0:T(8,128)(2,1)S(1)}, u32[]{:S(2)}, u32[]{:S(2)}) collective-permute-start(bf16[64,256]{1,0:T(8,128)(2,1)S(1)} %pad_maximum_fusion.pair_ref), channel_id=1, source_target_pairs={{0,64},{32,96},{64,0},{96,32},{128,192},{160,224},{192,128},{224,1... | collective-permute-start | bytes 98312 | tf_op jit(solution)/shard_map/ppermute | solution.py:184
  121.5 0.0 collective-permute-done.10.six_ref
  121.5 1.7 %collective-permute-done.9.four_ref = bf16[64,256]{1,0:T(8,128)(2,1)S(1)} collective-permute-done((bf16[64,256]{1,0:T(8,128)(2,1)S(1)}, bf16[64,256]{1,0:T(8,128)(2,1)S(1)}, u32[]{:S(2)}, u32[]{:S(2)}) %collective-permute-start.9) | collective-permute-done | bytes 32800 | tf_op jit(solution)/shard_map/ppermute | solution.py:184
  123.2 1.0 collective-permute-done.8.two_ref
  124.3 0.0 all-to-all-done.3.parts_ref
  124.3 0.0 copy-done.2
  124.3 0.8 shard_map.111
  (3 shorter events, 0.0 us)
Async XLA Ops:
  2.7 34.9 %all-to-all-start = ((bf16[24,32,256]{2,1,0:T(8,128)(2,1)}), bf16[24,32,256]{2,1,0:T(8,128)(2,1)S(1)}, u32[]{:S(2)}, u32[]{:S(2)}) async-start(bf16[24,32,256]{2,1,0:T(8,128)(2,1)} %bitcast.12), calls=%async_computation | async-start | bytes 786432 | tf_op jit(solution)/shard_map/all_to_all | solution.py:196
  20.0 1.9 %copy-start.3 = (bf16[1,96,128,128]{3,2,1,0:T(8,128)(2,1)S(1)}, bf16[1,96,128,128]{3,2,1,0:T(8,128)(2,1)}, u32[]{:S(2)}) copy-start(bf16[1,96,128,128]{3,2,1,0:T(8,128)(2,1)} %param.17) | copy-start | bytes 9437188
  21.9 1.6 %copy-start.4 = (bf16[4096,256]{1,0:T(8,128)(2,1)S(1)}, bf16[4096,256]{1,0:T(8,128)(2,1)}, u32[]{:S(2)}) copy-start(bf16[4096,256]{1,0:T(8,128)(2,1)} %features_ref.1) | copy-start | bytes 6291460
  23.5 0.7 copy-start.5
  38.6 27.7 %all-to-all-start.1 = ((bf16[24,32,256]{2,1,0:T(8,128)(2,1)}), bf16[24,32,256]{2,1,0:T(8,128)(2,1)S(1)}, u32[]{:S(2)}, u32[]{:S(2)}) async-start(bf16[24,32,256]{2,1,0:T(8,128)(2,1)} %shard_map.107), calls=%async_computation.1 | async-start | bytes 786432 | tf_op jit(solution)/shard_map/all_to_all | solution.py:223
  50.3 0.9 copy-start
  51.2 13.5 %collective-permute-start = (bf16[12,64,256]{2,1,0:T(8,128)(2,1)S(1)}, bf16[12,64,256]{2,1,0:T(8,128)(2,1)S(1)}, u32[]{:S(2)}, u32[]{:S(2)}) collective-permute-start(bf16[12,64,256]{2,1,0:T(8,128)(2,1)S(1)} %get-tuple-element.14), channel_id=1, source_target_pairs={{0,1},{1,2},{2,3},{3,0},{4,5},{5,6},{6,7},{7,4},{8,9},{9,10},{10,1... | collective-permute-start | bytes 1179656 | tf_op jit(solution)/shard_map/ppermute | solution.py:187
  54.3 12.0 %collective-permute-start.1 = (bf16[12,64,256]{2,1,0:T(8,128)(2,1)S(1)}, bf16[12,64,256]{2,1,0:T(8,128)(2,1)S(1)}, u32[]{:S(2)}, u32[]{:S(2)}) collective-permute-start(bf16[12,64,256]{2,1,0:T(8,128)(2,1)S(1)} %get-tuple-element.15), channel_id=1, source_target_pairs={{0,3},{1,0},{2,1},{3,2},{4,7},{5,4},{6,5},{7,6},{8,11},{9,8},{10,9... | collective-permute-start | bytes 1179656 | tf_op jit(solution)/shard_map/ppermute | solution.py:187
  66.3 1.1 copy-start.1
  67.4 56.8 %copy-start.2 = (bf16[256,256]{1,0:T(8,128)(2,1)S(1)}, bf16[256,256]{1,0:T(8,128)(2,1)}, u32[]{:S(2)}) copy-start(bf16[256,256]{1,0:T(8,128)(2,1)} %weight_ref.1) | copy-start | bytes 393220
  67.6 32.6 %collective-permute-start.2 = (bf16[12,64,256]{2,1,0:T(8,128)(2,1)S(1)}, bf16[12,64,256]{2,1,0:T(8,128)(2,1)S(1)}, u32[]{:S(2)}, u32[]{:S(2)}) collective-permute-start(bf16[12,64,256]{2,1,0:T(8,128)(2,1)S(1)} %get-tuple-element.19), channel_id=1, source_target_pairs={{0,1},{1,2},{2,3},{3,0},{4,5},{5,6},{6,7},{7,4},{8,9},{9,10},{10,1... | collective-permute-start | bytes 1179656 | tf_op jit(solution)/shard_map/ppermute | solution.py:187
  70.7 29.5 %collective-permute-start.3 = (bf16[12,64,256]{2,1,0:T(8,128)(2,1)S(1)}, bf16[12,64,256]{2,1,0:T(8,128)(2,1)S(1)}, u32[]{:S(2)}, u32[]{:S(2)}) collective-permute-start(bf16[12,64,256]{2,1,0:T(8,128)(2,1)S(1)} %get-tuple-element.20), channel_id=1, source_target_pairs={{0,3},{1,0},{2,1},{3,2},{4,7},{5,4},{6,5},{7,6},{8,11},{9,8},{10,9... | collective-permute-start | bytes 1179656 | tf_op jit(solution)/shard_map/ppermute | solution.py:187
  88.8 9.0 %collective-permute-start.6 = (f32[32,256]{1,0:T(8,128)S(1)}, f32[32,256]{1,0:T(8,128)S(1)}, u32[]{:S(2)}, u32[]{:S(2)}) collective-permute-start(f32[32,256]{1,0:T(8,128)S(1)} %convert_reduce_fusion.own_ref), channel_id=1, source_target_pairs={{0,1},{1,2},{2,3},{3,0},{4,5},{5,6},{6,7},{7,4},{8,9},{9,10},{10,1... | collective-permute-start | bytes 98312 | tf_op jit(solution)/shard_map/ppermute | solution.py:187
  90.7 7.1 %collective-permute-start.5 = (f32[32,256]{1,0:T(8,128)S(1)}, f32[32,256]{1,0:T(8,128)S(1)}, u32[]{:S(2)}, u32[]{:S(2)}) collective-permute-start(f32[32,256]{1,0:T(8,128)S(1)} %convert_reduce_fusion.own_ref), channel_id=1, source_target_pairs={{0,2},{1,3},{2,0},{3,1},{4,6},{5,7},{6,4},{7,5},{8,10},{9,11},{10,... | collective-permute-start | bytes 98312 | tf_op jit(solution)/shard_map/ppermute | solution.py:187
  95.3 5.0 %collective-permute-start.4 = (f32[32,256]{1,0:T(8,128)S(1)}, f32[32,256]{1,0:T(8,128)S(1)}, u32[]{:S(2)}, u32[]{:S(2)}) collective-permute-start(f32[32,256]{1,0:T(8,128)S(1)} %convert_reduce_fusion.own_ref), channel_id=1, source_target_pairs={{0,3},{1,0},{2,1},{3,2},{4,7},{5,4},{6,5},{7,6},{8,11},{9,8},{10,9... | collective-permute-start | bytes 98312 | tf_op jit(solution)/shard_map/ppermute | solution.py:187
  101.2 23.0 %all-to-all-start.3 = ((bf16[8,128,256]{2,1,0:T(8,128)(2,1)}), bf16[8,128,256]{2,1,0:T(8,128)(2,1)S(1)}, u32[]{:S(2)}, u32[]{:S(2)}) async-start(bf16[8,128,256]{2,1,0:T(8,128)(2,1)} %shard_map.110), calls=%async_computation.3 | async-start | bytes 1048576 | tf_op jit(solution)/shard_map/all_to_all | solution.py:266
  104.7 7.5 %collective-permute-start.7 = (bf16[32,256]{1,0:T(8,128)(2,1)S(1)}, bf16[32,256]{1,0:T(8,128)(2,1)S(1)}, u32[]{:S(2)}, u32[]{:S(2)}) collective-permute-start(bf16[32,256]{1,0:T(8,128)(2,1)S(1)} %shard_map.109.after_ref), channel_id=1, source_target_pairs={{0,32},{32,0},{64,96},{96,64},{128,160},{160,128},{192,224},{224,1... | collective-permute-start | bytes 49160 | tf_op jit(solution)/shard_map/ppermute | solution.py:184
  112.2 9.3 %collective-permute-start.10 = (bf16[64,256]{1,0:T(8,128)(2,1)S(1)}, bf16[64,256]{1,0:T(8,128)(2,1)S(1)}, u32[]{:S(2)}, u32[]{:S(2)}) collective-permute-start(bf16[64,256]{1,0:T(8,128)(2,1)S(1)} %pad_maximum_fusion.pair_ref), channel_id=1, source_target_pairs={{0,192},{32,224},{64,128},{96,160},{128,64},{160,96},{192,0},{224,... | collective-permute-start | bytes 98312 | tf_op jit(solution)/shard_map/ppermute | solution.py:184
  117.3 5.9 %collective-permute-start.9 = (bf16[64,256]{1,0:T(8,128)(2,1)S(1)}, bf16[64,256]{1,0:T(8,128)(2,1)S(1)}, u32[]{:S(2)}, u32[]{:S(2)}) collective-permute-start(bf16[64,256]{1,0:T(8,128)(2,1)S(1)} %pad_maximum_fusion.pair_ref), channel_id=1, source_target_pairs={{0,128},{32,160},{64,192},{96,224},{128,0},{160,32},{192,64},{224,... | collective-permute-start | bytes 98312 | tf_op jit(solution)/shard_map/ppermute | solution.py:184
  119.3 5.0 %collective-permute-start.8 = (bf16[64,256]{1,0:T(8,128)(2,1)S(1)}, bf16[64,256]{1,0:T(8,128)(2,1)S(1)}, u32[]{:S(2)}, u32[]{:S(2)}) collective-permute-start(bf16[64,256]{1,0:T(8,128)(2,1)S(1)} %pad_maximum_fusion.pair_ref), channel_id=1, source_target_pairs={{0,64},{32,96},{64,0},{96,32},{128,192},{160,224},{192,128},{224,1... | collective-permute-start | bytes 98312 | tf_op jit(solution)/shard_map/ppermute | solution.py:184

commit v11 on v9

--- a/solution.py
+++ b/solution.py
@@ -87,9 +87,7 @@
         out_ref[y] = total
 
 
-def products(
-    place_ref, rows_ref, turned_ref, keep_ref, up_ref, down_ref, up_rest_ref, down_rest_ref, next_ref, last_ref, turned, sems
-):
+def products(place_ref, rows_ref, turned_ref, keep_ref, up_ref, down_ref, next_ref, last_ref, turned, sems):
     groups, size, _ = keep_ref.shape
     half = size // 2
     place = place_ref[0]
@@ -114,12 +112,8 @@
             down_ref[g] = two[half:].astype(down_ref.dtype)
             next_ref[g] = one[:half]
             last_ref[g] = three[half:]
-            if g < groups // 2:
-                up_ref[groups + g] = one[half:].astype(up_ref.dtype)
-                down_ref[groups + g] = three[:half].astype(down_ref.dtype)
-            else:
-                up_rest_ref[g - groups // 2] = one[half:].astype(up_ref.dtype)
-                down_rest_ref[g - groups // 2] = three[:half].astype(down_ref.dtype)
+            up_ref[groups + g] = one[half:].astype(up_ref.dtype)
+            down_ref[groups + g] = three[:half].astype(down_ref.dtype)
 
 
 def relay(terms_ref, next_ref, last_ref, up_ref, down_ref, next_out_ref, last_out_ref, share_ref):
@@ -137,17 +131,13 @@
     last_out_ref[groups * half :] = total
 
 
-def add_ring(keep_ref, up_ref, down_ref, up_rest_ref, down_rest_ref, next_ref, last_ref, out_ref):
+def add_ring(keep_ref, up_ref, down_ref, next_ref, last_ref, out_ref):
     groups, size, _ = keep_ref.shape
     half = size // 2
     for g in range(groups):
-        if g < groups // 2:
-            from_last, from_next = up_ref[groups + g], down_ref[groups + g]
-        else:
-            from_last, from_next = up_rest_ref[g - groups // 2], down_rest_ref[g - groups // 2]
         rows = slice(g * half, (g + 1) * half)
-        low = keep_ref[g, :half] + from_next.astype(jnp.float32) + next_ref[rows].astype(jnp.float32)
-        high = keep_ref[g, half:] + from_last.astype(jnp.float32) + last_ref[rows].astype(jnp.float32)
+        low = keep_ref[g, :half] + down_ref[groups + g].astype(jnp.float32) + next_ref[rows].astype(jnp.float32)
+        high = keep_ref[g, half:] + up_ref[groups + g].astype(jnp.float32) + last_ref[rows].astype(jnp.float32)
         out_ref[g, :half] = low.astype(out_ref.dtype)
         out_ref[g, half:] = high.astype(out_ref.dtype)
 
@@ -229,15 +219,14 @@
     place = (lax.axis_index("rep") % RING).astype(jnp.int32)[None]
     full = jax.ShapeDtypeStruct((columns, size, width), jnp.float32)
     waiting = jax.ShapeDtypeStruct((columns, size // 2, width), jnp.float32)
-    sent = jax.ShapeDtypeStruct((3 * columns // 2, size // 2, width), jnp.bfloat16)
-    rest = jax.ShapeDtypeStruct((columns // 2, size // 2, width), jnp.bfloat16)
+    sent = jax.ShapeDtypeStruct((2 * columns, size // 2, width), jnp.bfloat16)
     passed_on = jax.ShapeDtypeStruct((columns * size // 2 + depth, width), jnp.bfloat16)
     share = jax.ShapeDtypeStruct((depth, width), jnp.bfloat16)
-    keep, up, down, up_rest, down_rest, ahead, behind = pl.pallas_call(
+    keep, up, down, ahead, behind = pl.pallas_call(
         products,
-        out_shape=(full, sent, sent, rest, rest, waiting, waiting),
+        out_shape=(full, sent, sent, waiting, pltpu.HBM(waiting.shape, waiting.dtype)),
         in_specs=[SMEM, VMEM, HBM],
-        out_specs=(VMEM,) * 7,
+        out_specs=(VMEM,) * 5,
         scratch_shapes=[
             pltpu.VMEM((col_blocks * size, total_rows), jnp.bfloat16),
             pltpu.SemaphoreType.DMA((columns,)),
@@ -266,14 +255,13 @@
         compiler_params=params,
     )(place, own, ahead, behind, far)
     own = jnp.sum(exchange(shares, "rep", axis_index_groups=groups).astype(jnp.float32), axis=0)
-    up_rest, down_rest = passed(up_rest, 1), passed(down_rest, -1)
     parts = pl.pallas_call(
         add_ring,
         out_shape=jax.ShapeDtypeStruct((columns, size, width), jnp.bfloat16),
-        in_specs=[VMEM] * 7,
+        in_specs=[VMEM] * 5,
         out_specs=VMEM,
         compiler_params=params,
-    )(keep, up, down, up_rest, down_rest, ahead, behind)
+    )(keep, up, down, ahead, behind)
     parts = exchange(parts, "rep", axis_index_groups=groups)
 
     own = own.astype(jnp.bfloat16)

time: 126 us -> 123 us (0.976); the launches traced: 124 us -> 122 us
  starting transfers between devices: 75.2 us -> 64.9 us
  waiting for transfers between devices: 22.5 us -> 30 us
    all_to_all x1, waiting for transfers between devices: 0.01 us -> 7.07 us  [per_device(): exchange(shares, 'rep', axis_index_groups=groups).astype(jnp.float32)]
    ppermute x7 -> x5, starting transfers between devices: 22.7 us -> 16.3 us  [passed(): lax.ppermute(value, 'rep', [(i, i - i % RING + (i + step) % RING) for i i...]
    all_to_all x1, starting transfers between devices: 6.44 us -> 3.49 us  [per_device(): parts = exchange(parts, 'rep', axis_index_groups=groups)]
    unnamed x12 -> x10, local copies, waits for them, and re-layouts: 4.79 us -> 5.18 us
    ppermute x7 -> x5, waiting for transfers between devices: 14.1 us -> 14.5 us  [passed(): lax.ppermute(value, 'rep', [(i, i - i % RING + (i + step) % RING) for i i...]
  transfers between devices with their start and end apart: 15 -> 13, of which waited for: 9 -> 8; matrix products, arithmetic and copies ran while one was open for 0% -> 0% of each run, Pallas kernels for 12% -> 13%
where the time goes in v11:
time: 123 us; the launch traced here: 122 us
  starting transfers between devices  64.9 us (53%)
  waiting for transfers between devices  30 us (24%)
  Pallas kernels  20.5 us (17%)
  local copies, waits for them, and re-layouts  5.18 us (4%)
  between operations  1.46 us (1%)
    all_to_all x1, starting transfers between devices, per_device(): exchange(outgoing.reshape(n_rows, per_peer, width), 'rows')  16.7 us
    ppermute x5, starting transfers between devices, passed(): lax.ppermute(value, 'rep', [(i, i - i % RING + (i + step) % RING) for i i...  16.3 us
    ppermute x4, starting transfers between devices, swapped(): lax.ppermute(value, axis, [(i, i ^ mask) for i in range(lax.axis_size(axi...  15.4 us
    ppermute x5, waiting for transfers between devices, passed(): lax.ppermute(value, 'rep', [(i, i - i % RING + (i + step) % RING) for i i...  14.5 us
    pallas_call x1, Pallas kernels, per_device(): pl.pallas_call(place_tiles, out_shape=(pltpu.HBM((col_blocks * size, tota...  8.59 us
    all_to_all x1, waiting for transfers between devices, per_device(): exchange(shares, 'rep', axis_index_groups=groups).astype(jnp.float32)  7.07 us
    all_to_all x1, starting transfers between devices, per_device(): exchange(shares, 'rep', axis_index_groups=groups).astype(jnp.float32)  6.82 us
    pallas_call x1, Pallas kernels, per_device(): pl.pallas_call(products, out_shape=(full, sent, sent, waiting, pltpu.HBM(...  6.25 us
  transfers between devices with their start and end apart: 13, of which 8 were waited for; matrix products, arithmetic and copies ran while one was open for 0% of the time, Pallas kernels for 13%

profile of v11, /device:TPU:1, one launch (start us, length us, event | category | flops | bytes accessed | tf_op | source)
XLA Modules:
  0.0 122.1 jit_solution(6643767923232810185)
XLA Ops:
  0.6 2.0 %shard_map.104 = bf16[768,256]{1,0:T(8,128)(2,1)} custom-call(s32[24]{0:T(128)} %bitcast.14, bf16[128,256]{1,0:T(8,128)(2,1)} %out_grad_ref.1, bf16[128,256]{1,0:T(8,128)(2,1)} %pre_relu_ref.1, s32[24,32]{1,0:T(8,128)} %bitcast.13), custom_call_target="tpu_custom_call" | custom-call | tf_op jit(solution)/shard_map/pallas_call | solution.py:183
  2.7 16.7 %all-to-all-start = ((bf16[24,32,256]{2,1,0:T(8,128)(2,1)}), bf16[24,32,256]{2,1,0:T(8,128)(2,1)S(1)}, u32[]{:S(2)}, u32[]{:S(2)}) async-start(bf16[24,32,256]{2,1,0:T(8,128)(2,1)} %bitcast.12), calls=%async_computation | async-start | bytes 786432 | tf_op jit(solution)/shard_map/all_to_all | solution.py:190
  20.0 0.0 copy-start.2
  20.0 1.9 %copy-done.2 = bf16[1,96,128,128]{3,2,1,0:T(8,128)(2,1)S(1)} copy-done((bf16[1,96,128,128]{3,2,1,0:T(8,128)(2,1)S(1)}, bf16[1,96,128,128]{3,2,1,0:T(8,128)(2,1)}, u32[]{:S(2)}) %copy-start.2) | copy-done | bytes 3145752
  21.9 0.0 copy-start.3
  21.9 1.6 %copy-done.3 = bf16[4096,256]{1,0:T(8,128)(2,1)S(1)} copy-done((bf16[4096,256]{1,0:T(8,128)(2,1)S(1)}, bf16[4096,256]{1,0:T(8,128)(2,1)}, u32[]{:S(2)}) %copy-start.3) | copy-done | bytes 2097176
  23.5 0.0 copy-start.4
  23.5 0.7 copy-done.4
  24.1 8.6 %shard_map.105 = (bf16[4096,768]{1,0:T(8,128)(2,1)}, bf16[256,768]{1,0:T(8,128)(2,1)S(1)}) custom-call(s32[96]{0:T(128)S(1)} %bitcast.11, s32[1]{0:T(128)S(6)} %copy.11.count_ref, bf16[96,128,128]{2,1,0:T(8,128)(2,1)S(1)} %bitcast.10, bf16[4096,256]{1,0:T(8,128)(2,1)S(1)} %copy-done.3), custom_call_target="tpu_custom_call" | custom-call | flops 1600000000 | bytes 24000000 | tf_op jit(solution)/shard_map/pallas_call | solution.py:192
  32.7 4.8 %all-to-all-done = bf16[24,32,256]{2,1,0:T(8,128)(2,1)S(1)} async-done(((bf16[24,32,256]{2,1,0:T(8,128)(2,1)}), bf16[24,32,256]{2,1,0:T(8,128)(2,1)S(1)}, u32[]{:S(2)}, u32[]{:S(2)}) %all-to-all-start) | async-done | bytes 393248 | tf_op jit(solution)/shard_map/all_to_all | solution.py:190
  37.6 1.0 shard_map.107
  38.6 6.2 %all-to-all-start.1 = ((bf16[24,32,256]{2,1,0:T(8,128)(2,1)}), bf16[24,32,256]{2,1,0:T(8,128)(2,1)S(1)}, u32[]{:S(2)}, u32[]{:S(2)}) async-start(bf16[24,32,256]{2,1,0:T(8,128)(2,1)} %shard_map.107), calls=%async_computation.1 | async-start | bytes 786432 | tf_op jit(solution)/shard_map/all_to_all | solution.py:217
  44.8 6.2 %shard_map.106 = (f32[8,128,256]{2,1,0:T(8,128)S(1)}, bf16[16,64,256]{2,1,0:T(8,128)(2,1)S(1)}, bf16[16,64,256]{2,1,0:T(8,128)(2,1)S(1)}, f32[8,64,256]{2,1,0:T(8,128)S(1)}, f32[8,64,256]{2,1,0:T(8,128)}) custom-call(s32[1]{0:T(128)} %bitcast.1.place_ref, bf16[768,256]{1,0:T(8,128)(2,1)S(1)} %bitcast.9, bf16[4096,768]{1,0:T(8,128)(2,1)} %get-tuple-element.12.turned_ref), custom_call_target="tpu_custom_call" | custom-call | flops 1700000000 | bytes 9000000 | tf_op jit(solution)/shard_map/pallas_call | solution.py:225
  51.1 3.1 %collective-permute-start = (bf16[16,64,256]{2,1,0:T(8,128)(2,1)S(1)}, bf16[16,64,256]{2,1,0:T(8,128)(2,1)S(1)}, u32[]{:S(2)}, u32[]{:S(2)}) collective-permute-start(bf16[16,64,256]{2,1,0:T(8,128)(2,1)S(1)} %get-tuple-element.14), channel_id=1, source_target_pairs={{0,1},{1,2},{2,3},{3,0},{4,5},{5,6},{6,7},{7,4},{8,9},{9,10},{10,1... | collective-permute-start | bytes 1572872 | tf_op jit(solution)/shard_map/ppermute | solution.py:181
  54.2 3.4 %collective-permute-start.1 = (bf16[16,64,256]{2,1,0:T(8,128)(2,1)S(1)}, bf16[16,64,256]{2,1,0:T(8,128)(2,1)S(1)}, u32[]{:S(2)}, u32[]{:S(2)}) collective-permute-start(bf16[16,64,256]{2,1,0:T(8,128)(2,1)S(1)} %get-tuple-element.15), channel_id=1, source_target_pairs={{0,3},{1,0},{2,1},{3,2},{4,7},{5,4},{6,5},{7,6},{8,11},{9,8},{10,9... | collective-permute-start | bytes 1572872 | tf_op jit(solution)/shard_map/ppermute | solution.py:181
  57.6 9.8 %collective-permute-done.up_ref = bf16[16,64,256]{2,1,0:T(8,128)(2,1)S(1)} collective-permute-done((bf16[16,64,256]{2,1,0:T(8,128)(2,1)S(1)}, bf16[16,64,256]{2,1,0:T(8,128)(2,1)S(1)}, u32[]{:S(2)}, u32[]{:S(2)}) %collective-permute-start) | collective-permute-done | bytes 524320 | tf_op jit(solution)/shard_map/ppermute | solution.py:181
  67.4 1.6 %collective-permute-done.1.down_ref = bf16[16,64,256]{2,1,0:T(8,128)(2,1)S(1)} collective-permute-done((bf16[16,64,256]{2,1,0:T(8,128)(2,1)S(1)}, bf16[16,64,256]{2,1,0:T(8,128)(2,1)S(1)}, u32[]{:S(2)}, u32[]{:S(2)}) %collective-permute-start.1) | collective-permute-done | bytes 524320 | tf_op jit(solution)/shard_map/ppermute | solution.py:181
  69.0 0.0 all-to-all-done.1.terms_ref
  69.0 0.0 copy-start
  69.0 1.0 copy-done
  70.1 0.1 shard_map.108
  70.2 0.0 copy-start.1
  70.2 3.3 %collective-permute-start.2 = (bf16[544,256]{1,0:T(8,128)(2,1)S(1)}, bf16[544,256]{1,0:T(8,128)(2,1)S(1)}, u32[]{:S(2)}, u32[]{:S(2)}) collective-permute-start(bf16[544,256]{1,0:T(8,128)(2,1)S(1)} %get-tuple-element.19), channel_id=1, source_target_pairs={{0,1},{1,2},{2,3},{3,0},{4,5},{5,6},{6,7},{7,4},{8,9},{9,10},{10,1... | collective-permute-start | bytes 835592 | tf_op jit(solution)/shard_map/ppermute | solution.py:181
  73.5 3.4 %collective-permute-start.3 = (bf16[544,256]{1,0:T(8,128)(2,1)S(1)}, bf16[544,256]{1,0:T(8,128)(2,1)S(1)}, u32[]{:S(2)}, u32[]{:S(2)}) collective-permute-start(bf16[544,256]{1,0:T(8,128)(2,1)S(1)} %get-tuple-element.20), channel_id=1, source_target_pairs={{0,3},{1,0},{2,1},{3,2},{4,7},{5,4},{6,5},{7,6},{8,11},{9,8},{10,9... | collective-permute-start | bytes 835592 | tf_op jit(solution)/shard_map/ppermute | solution.py:181
  76.9 3.1 %collective-permute-start.4 = (bf16[32,256]{1,0:T(8,128)(2,1)S(1)}, bf16[32,256]{1,0:T(8,128)(2,1)S(1)}, u32[]{:S(2)}, u32[]{:S(2)}) collective-permute-start(bf16[32,256]{1,0:T(8,128)(2,1)S(1)} %get-tuple-element.21.own_ref), channel_id=1, source_target_pairs={{0,2},{1,3},{2,0},{3,1},{4,6},{5,7},{6,4},{7,5},{8,10},{9,11},{10,... | collective-permute-start | bytes 49160 | tf_op jit(solution)/shard_map/ppermute | solution.py:181
  80.0 3.1 %collective-permute-done.4.far_ref = bf16[32,256]{1,0:T(8,128)(2,1)S(1)} collective-permute-done((bf16[32,256]{1,0:T(8,128)(2,1)S(1)}, bf16[32,256]{1,0:T(8,128)(2,1)S(1)}, u32[]{:S(2)}, u32[]{:S(2)}) %collective-permute-start.4) | collective-permute-done | bytes 16416 | tf_op jit(solution)/shard_map/ppermute | solution.py:181
  83.1 0.0 collective-permute-done.2.next_ref.behind_ref
  83.1 0.0 collective-permute-done.3.last_ref.ahead_ref
  83.1 0.7 shard_map.110
  83.8 6.8 %all-to-all-start.3 = ((bf16[8,32,256]{2,1,0:T(8,128)(2,1)}), bf16[8,32,256]{2,1,0:T(8,128)(2,1)S(1)}, u32[]{:S(2)}, u32[]{:S(2)}) async-start(bf16[8,32,256]{2,1,0:T(8,128)(2,1)} %shard_map.110), calls=%async_computation.3 | async-start | bytes 262144 | tf_op jit(solution)/shard_map/all_to_all | solution.py:257
  90.6 1.0 shard_map.109
  91.6 7.1 %all-to-all-done.3 = bf16[8,32,256]{2,1,0:T(8,128)(2,1)S(1)} async-done(((bf16[8,32,256]{2,1,0:T(8,128)(2,1)}), bf16[8,32,256]{2,1,0:T(8,128)(2,1)S(1)}, u32[]{:S(2)}, u32[]{:S(2)}) %all-to-all-start.3) | async-done | bytes 131104 | tf_op jit(solution)/shard_map/all_to_all | solution.py:257
  98.7 3.5 %all-to-all-start.2 = ((bf16[8,128,256]{2,1,0:T(8,128)(2,1)}), bf16[8,128,256]{2,1,0:T(8,128)(2,1)S(1)}, u32[]{:S(2)}, u32[]{:S(2)}) async-start(bf16[8,128,256]{2,1,0:T(8,128)(2,1)} %shard_map.109), calls=%async_computation.2 | async-start | bytes 1048576 | tf_op jit(solution)/shard_map/all_to_all | solution.py:265
  102.2 6.1 %collective-permute-start.5 = (bf16[32,256]{1,0:T(8,128)(2,1)S(1)}, bf16[32,256]{1,0:T(8,128)(2,1)S(1)}, u32[]{:S(2)}, u32[]{:S(2)}) collective-permute-start(bf16[32,256]{1,0:T(8,128)(2,1)S(1)} %reduce_sum.12), channel_id=1, source_target_pairs={{0,32},{32,0},{64,96},{96,64},{128,160},{160,128},{192,224},{224,1... | collective-permute-start | bytes 49160 | tf_op jit(solution)/shard_map/ppermute | solution.py:178
  108.3 0.8 collective-permute-done.5
  109.2 5.1 %collective-permute-start.8 = (bf16[64,256]{1,0:T(8,128)(2,1)S(1)}, bf16[64,256]{1,0:T(8,128)(2,1)S(1)}, u32[]{:S(2)}, u32[]{:S(2)}) collective-permute-start(bf16[64,256]{1,0:T(8,128)(2,1)S(1)} %pad_maximum_fusion.pair_ref), channel_id=1, source_target_pairs={{0,192},{32,224},{64,128},{96,160},{128,64},{160,96},{192,0},{224,... | collective-permute-start | bytes 98312 | tf_op jit(solution)/shard_map/ppermute | solution.py:178
  114.3 1.9 %collective-permute-start.7 = (bf16[64,256]{1,0:T(8,128)(2,1)S(1)}, bf16[64,256]{1,0:T(8,128)(2,1)S(1)}, u32[]{:S(2)}, u32[]{:S(2)}) collective-permute-start(bf16[64,256]{1,0:T(8,128)(2,1)S(1)} %pad_maximum_fusion.pair_ref), channel_id=1, source_target_pairs={{0,128},{32,160},{64,192},{96,224},{128,0},{160,32},{192,64},{224,... | collective-permute-start | bytes 98312 | tf_op jit(solution)/shard_map/ppermute | solution.py:178
  116.2 2.2 %collective-permute-start.6 = (bf16[64,256]{1,0:T(8,128)(2,1)S(1)}, bf16[64,256]{1,0:T(8,128)(2,1)S(1)}, u32[]{:S(2)}, u32[]{:S(2)}) collective-permute-start(bf16[64,256]{1,0:T(8,128)(2,1)S(1)} %pad_maximum_fusion.pair_ref), channel_id=1, source_target_pairs={{0,64},{32,96},{64,0},{96,32},{128,192},{160,224},{192,128},{224,1... | collective-permute-start | bytes 98312 | tf_op jit(solution)/shard_map/ppermute | solution.py:178
  118.5 0.0 collective-permute-done.8.six_ref
  118.5 1.7 %collective-permute-done.7.four_ref = bf16[64,256]{1,0:T(8,128)(2,1)S(1)} collective-permute-done((bf16[64,256]{1,0:T(8,128)(2,1)S(1)}, bf16[64,256]{1,0:T(8,128)(2,1)S(1)}, u32[]{:S(2)}, u32[]{:S(2)}) %collective-permute-start.7) | collective-permute-done | bytes 32800 | tf_op jit(solution)/shard_map/ppermute | solution.py:178
  120.2 1.0 collective-permute-done.6.two_ref
  121.2 0.0 all-to-all-done.2.parts_ref
  121.2 0.0 copy-done.1
  121.2 0.8 shard_map.111
  (2 shorter events, 0.0 us)
Async XLA Ops:
  2.7 34.9 %all-to-all-start = ((bf16[24,32,256]{2,1,0:T(8,128)(2,1)}), bf16[24,32,256]{2,1,0:T(8,128)(2,1)S(1)}, u32[]{:S(2)}, u32[]{:S(2)}) async-start(bf16[24,32,256]{2,1,0:T(8,128)(2,1)} %bitcast.12), calls=%async_computation | async-start | bytes 786432 | tf_op jit(solution)/shard_map/all_to_all | solution.py:190
  20.0 1.9 %copy-start.2 = (bf16[1,96,128,128]{3,2,1,0:T(8,128)(2,1)S(1)}, bf16[1,96,128,128]{3,2,1,0:T(8,128)(2,1)}, u32[]{:S(2)}) copy-start(bf16[1,96,128,128]{3,2,1,0:T(8,128)(2,1)} %param.17) | copy-start | bytes 9437188
  21.9 1.6 %copy-start.3 = (bf16[4096,256]{1,0:T(8,128)(2,1)S(1)}, bf16[4096,256]{1,0:T(8,128)(2,1)}, u32[]{:S(2)}) copy-start(bf16[4096,256]{1,0:T(8,128)(2,1)} %features_ref.1) | copy-start | bytes 6291460
  23.5 0.7 copy-start.4
  38.6 30.4 %all-to-all-start.1 = ((bf16[24,32,256]{2,1,0:T(8,128)(2,1)}), bf16[24,32,256]{2,1,0:T(8,128)(2,1)S(1)}, u32[]{:S(2)}, u32[]{:S(2)}) async-start(bf16[24,32,256]{2,1,0:T(8,128)(2,1)} %shard_map.107), calls=%async_computation.1 | async-start | bytes 786432 | tf_op jit(solution)/shard_map/all_to_all | solution.py:217
  51.1 16.3 %collective-permute-start = (bf16[16,64,256]{2,1,0:T(8,128)(2,1)S(1)}, bf16[16,64,256]{2,1,0:T(8,128)(2,1)S(1)}, u32[]{:S(2)}, u32[]{:S(2)}) collective-permute-start(bf16[16,64,256]{2,1,0:T(8,128)(2,1)S(1)} %get-tuple-element.14), channel_id=1, source_target_pairs={{0,1},{1,2},{2,3},{3,0},{4,5},{5,6},{6,7},{7,4},{8,9},{9,10},{10,1... | collective-permute-start | bytes 1572872 | tf_op jit(solution)/shard_map/ppermute | solution.py:181
  54.2 14.8 %collective-permute-start.1 = (bf16[16,64,256]{2,1,0:T(8,128)(2,1)S(1)}, bf16[16,64,256]{2,1,0:T(8,128)(2,1)S(1)}, u32[]{:S(2)}, u32[]{:S(2)}) collective-permute-start(bf16[16,64,256]{2,1,0:T(8,128)(2,1)S(1)} %get-tuple-element.15), channel_id=1, source_target_pairs={{0,3},{1,0},{2,1},{3,2},{4,7},{5,4},{6,5},{7,6},{8,11},{9,8},{10,9... | collective-permute-start | bytes 1572872 | tf_op jit(solution)/shard_map/ppermute | solution.py:181
  69.0 1.0 copy-start
  70.2 51.0 %copy-start.1 = (bf16[256,256]{1,0:T(8,128)(2,1)S(1)}, bf16[256,256]{1,0:T(8,128)(2,1)}, u32[]{:S(2)}) copy-start(bf16[256,256]{1,0:T(8,128)(2,1)} %weight_ref.1) | copy-start | bytes 393220
  70.2 12.9 %collective-permute-start.2 = (bf16[544,256]{1,0:T(8,128)(2,1)S(1)}, bf16[544,256]{1,0:T(8,128)(2,1)S(1)}, u32[]{:S(2)}, u32[]{:S(2)}) collective-permute-start(bf16[544,256]{1,0:T(8,128)(2,1)S(1)} %get-tuple-element.19), channel_id=1, source_target_pairs={{0,1},{1,2},{2,3},{3,0},{4,5},{5,6},{6,7},{7,4},{8,9},{9,10},{10,1... | collective-permute-start | bytes 835592 | tf_op jit(solution)/shard_map/ppermute | solution.py:181
  73.5 9.6 %collective-permute-start.3 = (bf16[544,256]{1,0:T(8,128)(2,1)S(1)}, bf16[544,256]{1,0:T(8,128)(2,1)S(1)}, u32[]{:S(2)}, u32[]{:S(2)}) collective-permute-start(bf16[544,256]{1,0:T(8,128)(2,1)S(1)} %get-tuple-element.20), channel_id=1, source_target_pairs={{0,3},{1,0},{2,1},{3,2},{4,7},{5,4},{6,5},{7,6},{8,11},{9,8},{10,9... | collective-permute-start | bytes 835592 | tf_op jit(solution)/shard_map/ppermute | solution.py:181
  76.9 6.2 %collective-permute-start.4 = (bf16[32,256]{1,0:T(8,128)(2,1)S(1)}, bf16[32,256]{1,0:T(8,128)(2,1)S(1)}, u32[]{:S(2)}, u32[]{:S(2)}) collective-permute-start(bf16[32,256]{1,0:T(8,128)(2,1)S(1)} %get-tuple-element.21.own_ref), channel_id=1, source_target_pairs={{0,2},{1,3},{2,0},{3,1},{4,6},{5,7},{6,4},{7,5},{8,10},{9,11},{10,... | collective-permute-start | bytes 49160 | tf_op jit(solution)/shard_map/ppermute | solution.py:181
  83.8 14.9 %all-to-all-start.3 = ((bf16[8,32,256]{2,1,0:T(8,128)(2,1)}), bf16[8,32,256]{2,1,0:T(8,128)(2,1)S(1)}, u32[]{:S(2)}, u32[]{:S(2)}) async-start(bf16[8,32,256]{2,1,0:T(8,128)(2,1)} %shard_map.110), calls=%async_computation.3 | async-start | bytes 262144 | tf_op jit(solution)/shard_map/all_to_all | solution.py:257
  98.7 22.5 %all-to-all-start.2 = ((bf16[8,128,256]{2,1,0:T(8,128)(2,1)}), bf16[8,128,256]{2,1,0:T(8,128)(2,1)S(1)}, u32[]{:S(2)}, u32[]{:S(2)}) async-start(bf16[8,128,256]{2,1,0:T(8,128)(2,1)} %shard_map.109), calls=%async_computation.2 | async-start | bytes 1048576 | tf_op jit(solution)/shard_map/all_to_all | solution.py:265
  102.2 7.0 %collective-permute-start.5 = (bf16[32,256]{1,0:T(8,128)(2,1)S(1)}, bf16[32,256]{1,0:T(8,128)(2,1)S(1)}, u32[]{:S(2)}, u32[]{:S(2)}) collective-permute-start(bf16[32,256]{1,0:T(8,128)(2,1)S(1)} %reduce_sum.12), channel_id=1, source_target_pairs={{0,32},{32,0},{64,96},{96,64},{128,160},{160,128},{192,224},{224,1... | collective-permute-start | bytes 49160 | tf_op jit(solution)/shard_map/ppermute | solution.py:178
  109.2 9.3 %collective-permute-start.8 = (bf16[64,256]{1,0:T(8,128)(2,1)S(1)}, bf16[64,256]{1,0:T(8,128)(2,1)S(1)}, u32[]{:S(2)}, u32[]{:S(2)}) collective-permute-start(bf16[64,256]{1,0:T(8,128)(2,1)S(1)} %pad_maximum_fusion.pair_ref), channel_id=1, source_target_pairs={{0,192},{32,224},{64,128},{96,160},{128,64},{160,96},{192,0},{224,... | collective-permute-start | bytes 98312 | tf_op jit(solution)/shard_map/ppermute | solution.py:178
  114.3 5.9 %collective-permute-start.7 = (bf16[64,256]{1,0:T(8,128)(2,1)S(1)}, bf16[64,256]{1,0:T(8,128)(2,1)S(1)}, u32[]{:S(2)}, u32[]{:S(2)}) collective-permute-start(bf16[64,256]{1,0:T(8,128)(2,1)S(1)} %pad_maximum_fusion.pair_ref), channel_id=1, source_target_pairs={{0,128},{32,160},{64,192},{96,224},{128,0},{160,32},{192,64},{224,... | collective-permute-start | bytes 98312 | tf_op jit(solution)/shard_map/ppermute | solution.py:178
  116.2 5.0 %collective-permute-start.6 = (bf16[64,256]{1,0:T(8,128)(2,1)S(1)}, bf16[64,256]{1,0:T(8,128)(2,1)S(1)}, u32[]{:S(2)}, u32[]{:S(2)}) collective-permute-start(bf16[64,256]{1,0:T(8,128)(2,1)S(1)} %pad_maximum_fusion.pair_ref), channel_id=1, source_target_pairs={{0,64},{32,96},{64,0},{96,32},{128,192},{160,224},{192,128},{224,1... | collective-permute-start | bytes 98312 | tf_op jit(solution)/shard_map/ppermute | solution.py:178
